TPU v7x, 32 devices: a whole 2x2x4 slice. The times are simulated.
32 devices in a mesh: tm: 16 (over z, x, core), fsdp: 2 (over y).
Axes of the slice: x: 2, y: 2, z: 4, core: 2. Of those that a mesh axis runs over, the one named last changes fastest.
Arguments:
- frames: bfloat16 [2, 2, 24576, 512], P(None, 'fsdp', 'tm'), may hold values from -6 to 6
- conditioning: bfloat16 [2, 2, 24576, 512], P(None, 'fsdp', 'tm'), may hold values from -6 to 6
- lengths: int32 [2, 2, 30], P(None, 'fsdp'), may hold values from 1 to 1600, 24576 in all within a row
- steps: int32 [2, 2, 30], P(None, 'fsdp'), may hold values from 0 to 999
- prompt: bfloat16 [2, 2, 256, 512], P(None, 'fsdp', 'tm'), may hold values from -6 to 6
- queries: float32 [32, 512], P('fsdp'), may hold values from -6 to 6
- w_step: float32 [512, 1024], P('fsdp'), may hold values from -0.25 to 0.25
- w_cond: float32 [512, 1024], P('fsdp'), may hold values from -0.25 to 0.25
- w_conv: float32 [3, 512, 1024], P(None, 'fsdp'), may hold values from -0.15625 to 0.15625
- w_query: float32 [512, 512], P('fsdp'), may hold values from -0.25 to 0.25
- w_key: float32 [512, 512], P('fsdp'), may hold values from -0.25 to 0.25
- w_value: float32 [512, 512], P('fsdp'), may hold values from -0.25 to 0.25
- w_out: float32 [512, 512], P('fsdp'), may hold values from -2 to 2
- w_film: float32 [512, 1024], P('fsdp'), may hold values from -2 to 2
- w_proj: float32 [512, 1024], P('fsdp'), may hold values from -0.25 to 0.25
- grad_res: bfloat16 [2, 2, 24576, 512], P(None, 'fsdp', 'tm'), may hold values from -6 to 6
- grad_skip: bfloat16 [2, 2, 24576, 512], P(None, 'fsdp', 'tm'), may hold values from -6 to 6
Outputs:
- res_out: bfloat16 [2, 2, 24576, 512], P(None, 'fsdp', 'tm')
- skip_out: bfloat16 [2, 2, 24576, 512], P(None, 'fsdp', 'tm')
- grad_frames: float32 [2, 2, 24576, 512], P(None, 'fsdp', 'tm')
- grad_prompt: float32 [2, 2, 256, 512], P(None, 'fsdp', 'tm')
- grad_queries: float32 [32, 512], P('fsdp')
- grad_step: float32 [512, 1024], P('fsdp')
- grad_cond: float32 [512, 1024], P('fsdp')
- grad_conv: float32 [3, 512, 1024], P(None, 'fsdp')
- grad_query: float32 [512, 512], P('fsdp')
- grad_key: float32 [512, 512], P('fsdp')
- grad_value: float32 [512, 512], P('fsdp')
- grad_out: float32 [512, 512], P('fsdp')
- grad_film: float32 [512, 1024], P('fsdp')
- grad_proj: float32 [512, 1024], P('fsdp')
Inputs may be any that keep to these rules, and one draw needn't show every extreme that they name: Each pack's 30 lengths sum to its 24576 frames; the last entry is the padding at the pack's end; the longest entry is exactly 1600.
All inputs are finite; a program needn't handle non-finite values.
Results may differ from a plain program's by a relative error of at most 0.0085.
The roundings to bfloat16 on the way count: a program that leaves them out, or rounds other values in their place, can miss the bound.
Values may be sent and summed in bfloat16 or wider, within the bound.
No kernel may reach another device: no remote copies, remote signals or barrier semaphores. Data moves between devices by JAX's collectives and lax.ppermute only.
A program may use at most 104 MiB of HBM per device.

v0:
```python
import math

import jax
import jax.numpy as jnp
from jax import lax
from jax.sharding import PartitionSpec as P

HEADS = 8
QUERIES = 32
DILATION = 16
MICRO = 2


PRECISE = lax.Precision.HIGHEST
SQRT_HALF = 0.7071067811865476


def padded(block, sides, width):
    for axis, dim in sides:
        count = lax.axis_size(axis)
        forward = [(i, i + 1) for i in range(count - 1)]
        backward = [(target, source) for source, target in forward]
        low = lax.ppermute(
            lax.slice_in_dim(block, block.shape[dim] - width, None, axis=dim), axis, forward
        )
        high = lax.ppermute(lax.slice_in_dim(block, 0, width, axis=dim), axis, backward)
        block = jnp.concatenate([low, block, high], axis=dim)
    return block


def joined_2(part, axis, combine):
    gathered = jax.tree.map(lambda a: lax.all_gather(a, axis), part)

    def take(source):
        return jax.tree.map(lambda a: lax.dynamic_index_in_dim(a, source, 0, False), gathered)

    return lax.fori_loop(
        1, lax.axis_size(axis), lambda source, state: combine(state, take(source)), take(0)
    )


def contract_rows(left, right, precision=None):
    return lax.dot_general(
        left,
        right,
        (((0,), (0,)), ((), ())),
        precision=precision,
        preferred_element_type=jnp.float32,
    )


def contract_cols(left, right, precision=None):
    return lax.dot_general(
        left,
        right,
        (((1,), (1,)), ((), ())),
        precision=precision,
        preferred_element_type=jnp.float32,
    )


def softmax_join(earlier, later):
    joined = jnp.maximum(earlier[0], later[0])
    return (
        joined,
        earlier[1] * jnp.exp(earlier[0] - joined) + later[1] * jnp.exp(later[0] - joined),
    )


def step_embedding(pack_steps, width):
    half_width = width // 2
    freqs = jnp.exp(jnp.arange(half_width).astype(jnp.float32) * (-math.log(10000.0) / half_width))
    angles = pack_steps.astype(jnp.float32)[:, None] * freqs[None, :]
    return jnp.concatenate([jnp.sin(angles), jnp.cos(angles)], axis=1)


def per_device(
    frames,
    conditioning,
    lengths,
    steps,
    prompt,
    queries,
    w_step,
    w_cond,
    w_conv,
    w_query,
    w_key,
    w_value,
    w_out,
    w_film,
    w_proj,
    grad_res,
    grad_skip,
):
    frames_dev = frames.shape[2]
    width = frames.shape[3]
    prompt_rows_dev = prompt.shape[2]
    head_size = width // HEADS
    score_scale = 1.0 / math.sqrt(head_size)
    bf16 = jnp.bfloat16
    f32 = jnp.float32
    shard_q = queries.astype(bf16)
    shard_step = w_step.astype(bf16)
    shard_cond = w_cond.astype(bf16)
    shard_conv = w_conv.astype(bf16)
    shard_query = w_query.astype(bf16)
    shard_key = w_key.astype(bf16)
    shard_value = w_value.astype(bf16)
    shard_out = w_out.astype(bf16)
    shard_film = w_film.astype(bf16)
    shard_proj = w_proj.astype(bf16)
    tm_index = lax.axis_index("tm")
    first_rank = (tm_index == 0).astype(f32)
    acc_q = jnp.zeros((QUERIES, width), f32)
    acc_step = jnp.zeros((width, 2 * width), f32)
    acc_cond = jnp.zeros((width, 2 * width), f32)
    acc_conv = jnp.zeros((3 * width, 2 * width), f32)
    acc_query = jnp.zeros((width, width), f32)
    acc_key = jnp.zeros((width, width), f32)
    acc_value = jnp.zeros((width, width), f32)
    acc_out = jnp.zeros((width, width), f32)
    acc_film = jnp.zeros((width, 2 * width), f32)
    acc_proj = jnp.zeros((width, 2 * width), f32)
    res_list, skip_list, frame_list, prompt_list = ([], [], [], [])
    for micro_index in range(MICRO):
        gathered = (
            lax.all_gather(shard_q, "fsdp", axis=0, tiled=True),
            lax.all_gather(shard_step, "fsdp", axis=0, tiled=True),
            lax.all_gather(shard_cond, "fsdp", axis=0, tiled=True),
            lax.all_gather(shard_conv, "fsdp", axis=1, tiled=True),
            lax.all_gather(shard_query, "fsdp", axis=0, tiled=True),
            lax.all_gather(shard_key, "fsdp", axis=0, tiled=True),
            lax.all_gather(shard_value, "fsdp", axis=0, tiled=True),
            lax.all_gather(shard_out, "fsdp", axis=0, tiled=True),
            lax.all_gather(shard_film, "fsdp", axis=0, tiled=True),
            lax.all_gather(shard_proj, "fsdp", axis=0, tiled=True),
        )
        (
            full_q,
            full_step,
            full_cond,
            full_conv,
            full_query,
            full_key,
            full_value,
            full_out,
            full_film,
            full_proj,
        ) = gathered
        conv_flat = full_conv.reshape(3 * width, 2 * width)
        frame_rows = frames[micro_index, 0].astype(f32)
        cond_rows = conditioning[micro_index, 0]
        pack_lengths = lengths[micro_index, 0]
        utter_count = pack_lengths.shape[0]
        utter_ends = jnp.cumsum(pack_lengths)
        positions = tm_index * frames_dev - DILATION + jnp.arange(frames_dev + 2 * DILATION)
        seg_ext = jnp.sum((positions[:, None] >= utter_ends[None, :]).astype(jnp.int32), axis=1)
        segment = seg_ext[DILATION : DILATION + frames_dev]
        live_mask = (segment < utter_count - 1).astype(f32)
        same_taps = [
            seg_ext[tap * DILATION : tap * DILATION + frames_dev] == segment for tap in range(3)
        ]
        one_hot = (segment[:, None] == jnp.arange(utter_count)[None, :]).astype(f32)
        step_low = step_embedding(steps[micro_index, 0], width).astype(bf16)
        step_film = jnp.dot(step_low, full_step, preferred_element_type=f32)
        film_first = jnp.dot(one_hot, step_film, precision=PRECISE) + jnp.dot(
            cond_rows, full_cond, preferred_element_type=f32
        )
        gain_first = film_first[:, :width]
        hidden_low = (frame_rows * (1.0 + gain_first) + film_first[:, width:]).astype(bf16)
        extended = padded(hidden_low, (("tm", 0),), DILATION)
        stacked = jnp.concatenate(
            [
                extended[tap * DILATION : tap * DILATION + frames_dev]
                * same_taps[tap][:, None].astype(bf16)
                for tap in range(3)
            ],
            axis=1,
        )
        conv_out = jnp.dot(stacked, conv_flat, preferred_element_type=f32)
        tanh_part = jnp.tanh(conv_out[:, :width])
        sigm_part = jax.nn.sigmoid(conv_out[:, width:])
        activated = tanh_part * sigm_part
        prompt_rows = prompt[micro_index, 0]
        query_low = jnp.dot(full_q, full_query, preferred_element_type=f32).astype(bf16)
        key_low = jnp.dot(prompt_rows, full_key, preferred_element_type=f32).astype(bf16)
        value_low = jnp.dot(prompt_rows, full_value, preferred_element_type=f32).astype(bf16)
        query_heads = query_low.reshape(QUERIES, HEADS, head_size)
        key_heads = key_low.reshape(prompt_rows_dev, HEADS, head_size)
        value_heads = value_low.reshape(prompt_rows_dev, HEADS, head_size)
        scores = (
            jnp.einsum("qhd,khd->hqk", query_heads, key_heads, preferred_element_type=f32)
            * score_scale
        )
        local_top = jnp.max(scores, axis=-1)
        local_total = jnp.sum(jnp.exp(scores - local_top[..., None]), axis=-1)
        score_top, score_total = joined_2((local_top, local_total), "tm", softmax_join)
        probs = jnp.exp(scores - score_top[..., None]) / score_total[..., None]
        probs_low = probs.astype(bf16)
        context_part = jnp.einsum(
            "hqk,khd->qhd", probs_low, value_heads, preferred_element_type=f32
        ).reshape(QUERIES, width)
        context = lax.psum(context_part, "tm")
        context_low = context.astype(bf16)
        projected = jnp.dot(context_low, full_out, preferred_element_type=f32)
        summary_low = jnp.mean(projected, axis=0).astype(bf16)
        film_second = jnp.dot(summary_low[None, :], full_film, preferred_element_type=f32)[0]
        gain_second = film_second[:width]
        gated_low = (activated * (1.0 + gain_second) + film_second[width:]).astype(bf16)
        branch_out = jnp.dot(gated_low, full_proj, preferred_element_type=f32)
        res_list.append(
            ((frame_rows + branch_out[:, :width]) * SQRT_HALF * live_mask[:, None]).astype(bf16)
        )
        skip_list.append((branch_out[:, width:] * live_mask[:, None]).astype(bf16))
        res_cot = grad_res[micro_index, 0].astype(f32) * SQRT_HALF * live_mask[:, None]
        skip_cot = grad_skip[micro_index, 0].astype(f32) * live_mask[:, None]
        branch_cot = jnp.concatenate([res_cot, skip_cot], axis=1).astype(bf16)
        acc_proj = acc_proj + contract_rows(gated_low, branch_cot)
        gated_cot = contract_cols(branch_cot, full_proj)
        film_local = jnp.concatenate(
            [jnp.sum(gated_cot * activated, axis=0), jnp.sum(gated_cot, axis=0)]
        )
        film_cot = lax.psum(film_local, "tm")
        summary_f32 = summary_low.astype(f32)
        acc_film = acc_film + first_rank * (summary_f32[:, None] * film_cot[None, :])
        summary_cot = jnp.dot(full_film.astype(f32), film_cot, precision=PRECISE) / QUERIES
        context_total = jnp.sum(context_low.astype(f32), axis=0)
        acc_out = acc_out + first_rank * (context_total[:, None] * summary_cot[None, :])
        context_cot_row = jnp.dot(full_out.astype(f32), summary_cot, precision=PRECISE)
        context_cot = jnp.broadcast_to(context_cot_row[None, :], (QUERIES, width)).astype(bf16)
        context_cot_heads = context_cot.reshape(QUERIES, HEADS, head_size)
        prob_cot = jnp.einsum(
            "qhd,khd->hqk", context_cot_heads, value_heads, preferred_element_type=f32
        )
        row_part = jnp.sum(probs * prob_cot, axis=-1)
        row_total = lax.psum(row_part, "tm")
        score_cot = (probs * (prob_cot - row_total[..., None])).astype(bf16)
        query_cot = (
            jnp.einsum("hqk,khd->qhd", score_cot, key_heads, preferred_element_type=f32)
            * score_scale
        ).reshape(QUERIES, width)
        key_cot = (
            (
                jnp.einsum("hqk,qhd->khd", score_cot, query_heads, preferred_element_type=f32)
                * score_scale
            )
            .astype(bf16)
            .reshape(prompt_rows_dev, width)
        )
        value_cot = (
            jnp.einsum("hqk,qhd->khd", probs_low, context_cot_heads, preferred_element_type=f32)
            .astype(bf16)
            .reshape(prompt_rows_dev, width)
        )
        prompt_list.append(contract_cols(key_cot, full_key) + contract_cols(value_cot, full_value))
        acc_key = acc_key + contract_rows(prompt_rows, key_cot)
        acc_value = acc_value + contract_rows(prompt_rows, value_cot)
        acc_query = acc_query + contract_rows(full_q.astype(f32), query_cot, PRECISE)
        acc_q = acc_q + contract_cols(query_cot, full_query.astype(f32), PRECISE)
        act_cot = gated_cot * (1.0 + gain_second)
        conv_cot = jnp.concatenate(
            [
                act_cot * sigm_part * (1.0 - tanh_part * tanh_part),
                act_cot * tanh_part * sigm_part * (1.0 - sigm_part),
            ],
            axis=1,
        ).astype(bf16)
        acc_conv = acc_conv + contract_rows(stacked, conv_cot)
        cot_extended = padded(conv_cot, (("tm", 0),), DILATION)
        back_taps = jnp.stack(
            [
                cot_extended[(2 - tap) * DILATION : (2 - tap) * DILATION + frames_dev]
                * same_taps[2 - tap][:, None].astype(bf16)
                for tap in range(3)
            ],
            axis=1,
        )
        hidden_cot = lax.dot_general(
            back_taps, full_conv, (((1, 2), (0, 2)), ((), ())), preferred_element_type=f32
        )
        film_first_cot = jnp.concatenate([hidden_cot * frame_rows, hidden_cot], axis=1).astype(bf16)
        acc_cond = acc_cond + contract_rows(cond_rows, film_first_cot)
        step_film_cot = contract_rows(one_hot, film_first_cot.astype(f32), PRECISE)
        acc_step = acc_step + contract_rows(step_low.astype(f32), step_film_cot, PRECISE)
        frame_list.append(res_cot + hidden_cot * (1.0 + gain_first))
    acc_conv_taps = acc_conv.reshape(3, width, 2 * width)
    shares = (
        lax.psum_scatter(acc_q, "fsdp", scatter_dimension=0, tiled=True),
        lax.psum_scatter(acc_step, "fsdp", scatter_dimension=0, tiled=True),
        lax.psum_scatter(acc_cond, "fsdp", scatter_dimension=0, tiled=True),
        lax.psum_scatter(acc_conv_taps, "fsdp", scatter_dimension=1, tiled=True),
        lax.psum_scatter(acc_query, "fsdp", scatter_dimension=0, tiled=True),
        lax.psum_scatter(acc_key, "fsdp", scatter_dimension=0, tiled=True),
        lax.psum_scatter(acc_value, "fsdp", scatter_dimension=0, tiled=True),
        lax.psum_scatter(acc_out, "fsdp", scatter_dimension=0, tiled=True),
        lax.psum_scatter(acc_film, "fsdp", scatter_dimension=0, tiled=True),
        lax.psum_scatter(acc_proj, "fsdp", scatter_dimension=0, tiled=True),
    )
    summed = lax.psum(
        (
            shares[0],
            shares[1],
            shares[2],
            shares[3],
            shares[4],
            shares[5],
            shares[6],
            shares[7],
            shares[8],
            shares[9],
        ),
        "tm",
    )
    res_out = jnp.stack(res_list)[:, None]
    skip_out = jnp.stack(skip_list)[:, None]
    grad_frames = jnp.stack(frame_list)[:, None]
    grad_prompt = jnp.stack(prompt_list)[:, None]
    return (
        res_out,
        skip_out,
        grad_frames,
        grad_prompt,
        summed[0],
        summed[1],
        summed[2],
        summed[3],
        summed[4],
        summed[5],
        summed[6],
        summed[7],
        summed[8],
        summed[9],
    )


def solution(mesh):
    in_specs = (
        P(None, "fsdp", "tm", None),
        P(None, "fsdp", "tm", None),
        P(None, "fsdp", None),
        P(None, "fsdp", None),
        P(None, "fsdp", "tm", None),
        P("fsdp", None),
        P("fsdp", None),
        P("fsdp", None),
        P(None, "fsdp", None),
        P("fsdp", None),
        P("fsdp", None),
        P("fsdp", None),
        P("fsdp", None),
        P("fsdp", None),
        P("fsdp", None),
        P(None, "fsdp", "tm", None),
        P(None, "fsdp", "tm", None),
    )
    out_specs = (
        P(None, "fsdp", "tm", None),
        P(None, "fsdp", "tm", None),
        P(None, "fsdp", "tm", None),
        P(None, "fsdp", "tm", None),
        P("fsdp", None),
        P("fsdp", None),
        P("fsdp", None),
        P(None, "fsdp", None),
        P("fsdp", None),
        P("fsdp", None),
        P("fsdp", None),
        P("fsdp", None),
        P("fsdp", None),
        P("fsdp", None),
    )
    return jax.shard_map(
        per_device, mesh=mesh, in_specs=in_specs, out_specs=out_specs, check_vma=False
    )
```

profile of v0, /device:TPU:0, one launch (start us, length us, event | category | flops | bytes accessed | tf_op | source)
XLA Modules:
  0.0 827.3 jit_solution(15819924831970833689)
XLA Ops:
  17.6 15.5 %all_gather.70 = bf16[512,512]{1,0:T(8,128)(2,1)S(1)} all-gather(bf16[256,512]{1,0:T(8,128)(2,1)S(1)} %convert_element_type.320), channel_id=1, replica_groups=mesh['tm'=16,'fsdp'=2] {'fsdp'}, dimensions={0}, use_global_device_ids=true | all-gather | bytes 786432 | tf_op jit(solution)/shard_map/all_gather | solution.py:133
  34.2 10.2 %all_gather.67 = bf16[512,512]{1,0:T(8,128)(2,1)S(1)} all-gather(bf16[256,512]{1,0:T(8,128)(2,1)S(1)} %convert_element_type.315), channel_id=1, replica_groups=mesh['tm'=16,'fsdp'=2] {'fsdp'}, dimensions={0}, use_global_device_ids=true | all-gather | bytes 786432 | tf_op jit(solution)/shard_map/all_gather | solution.py:134
  45.5 4.4 all_gather.68
  49.9 13.5 %all_gather.69 = bf16[512,512]{1,0:T(8,128)(2,1)S(1)} all-gather(bf16[256,512]{1,0:T(8,128)(2,1)S(1)} %convert_element_type.318), channel_id=1, replica_groups=mesh['tm'=16,'fsdp'=2] {'fsdp'}, dimensions={0}, use_global_device_ids=true | all-gather | bytes 786432 | tf_op jit(solution)/shard_map/all_gather | solution.py:132
  64.1 22.6 %all-gather = f32[128,32]{1,0:T(8,128)S(1)} all-gather(f32[8,32]{1,0:T(8,128)S(1)} %get-tuple-element.438), channel_id=2, replica_groups=mesh['tm'=16,'fsdp'=2] {'tm'}, dimensions={0}, use_global_device_ids=true | all-gather | bytes 17408 | tf_op jit(solution)/shard_map/all_gather | solution.py:32
  86.7 17.6 %all-gather.1 = f32[128,32]{1,0:T(8,128)S(1)} all-gather(f32[8,32]{1,0:T(8,128)S(1)} %exponential_reduce_fusion.1), channel_id=3, replica_groups=mesh['tm'=16,'fsdp'=2] {'tm'}, dimensions={0}, use_global_device_ids=true | all-gather | bytes 17408 | tf_op jit(solution)/shard_map/all_gather | solution.py:32
  105.0 18.9 %all-gather.2 = f32[128,32]{1,0:T(8,128)S(1)} all-gather(f32[8,32]{1,0:T(8,128)S(1)} %get-tuple-element.436), channel_id=4, replica_groups=mesh['tm'=16,'fsdp'=2] {'tm'}, dimensions={0}, use_global_device_ids=true | all-gather | bytes 17408 | tf_op jit(solution)/shard_map/all_gather | solution.py:32
  124.0 17.6 %all-gather.3 = f32[128,32]{1,0:T(8,128)S(1)} all-gather(f32[8,32]{1,0:T(8,128)S(1)} %exponential_reduce_fusion), channel_id=5, replica_groups=mesh['tm'=16,'fsdp'=2] {'tm'}, dimensions={0}, use_global_device_ids=true | all-gather | bytes 17408 | tf_op jit(solution)/shard_map/all_gather | solution.py:32
  142.5 10.2 %all_gather.75 = bf16[512,512]{1,0:T(8,128)(2,1)S(1)} all-gather(bf16[256,512]{1,0:T(8,128)(2,1)S(1)} %convert_element_type.324), channel_id=1, replica_groups=mesh['tm'=16,'fsdp'=2] {'fsdp'}, dimensions={0}, use_global_device_ids=true | all-gather | bytes 786432 | tf_op jit(solution)/shard_map/all_gather | solution.py:135
  158.8 6.2 fusion.88
  166.5 5.3 convolution_add_fusion
  182.6 5.2 collective-permute-start
  196.5 9.2 %fusion.78 = f32[1536,1024]{1,0:T(8,128)} fusion(bf16[1536,1024]{1,0:T(8,128)(2,1)} %bitcast.275, bf16[1536,512]{1,0:T(8,128)(2,1)} %get-tuple-element.411, bf16[1536,512]{1,0:T(8,128)(2,1)S(1)} %get-tuple-element.404, bf16[1536,512]{1,0:T(8,128)(2,1)} %get-tuple-element.410), kind=kOutput, calls=%fused_computation.128 | convolution fusion | flops 4845993984 | bytes 14155776 | tf_op jit(solution)/shard_map/dot_general | solution.py:181
  205.8 8.5 %multiply_reduce_fusion.1 = (f32[512]{0:T(512)S(1)}, f32[512]{0:T(512)S(1)}, f32[1536,512]{1,0:T(8,128)}) fusion(f32[1536,1024]{1,0:T(8,128)} %fusion.78, bf16[512,1024]{1,0:T(8,128)(2,1)} %all-gather.18.cloned.1.call-done, bf16[1536,512]{1,0:T(8,128)(2,1)} %get-tuple-element.408, bf16[1536,512]{1,0:T(8,128)(2,1)} %get-tuple-element.406), kind=kOutput, calls=%fused_computation.108 | convolution fusion | flops 1622408192 | bytes 13635584 | tf_op jit(solution)/shard_map/dot_general | solution.py:53
  214.3 5.1 fusion.77
  219.5 3.9 multiply_reduce_fusion
  223.4 32.8 %all-reduce.2 = (f32[1024]{0:T(1024)S(1)}, f32[1024]{0:T(1024)S(1)}) all-reduce(f32[1024]{0:T(1024)S(1)} %pad_maximum_fusion.45, f32[1024]{0:T(1024)S(1)} %pad_maximum_fusion.44), channel_id=1, replica_groups=mesh['tm'=16,'fsdp'=2] {'tm'}, use_global_device_ids=true, to_apply=%region_23.24 | all-reduce | flops 2048 | bytes 16384 | tf_op jit(solution)/shard_map/psum | solution.py:224
  262.1 30.0 %all-reduce.1 = (f32[8,32]{1,0:T(8,128)S(1)}, f32[8,32]{1,0:T(8,128)S(1)}) all-reduce(f32[8,32]{1,0:T(8,128)S(1)} %get-tuple-element.442, f32[8,32]{1,0:T(8,128)S(1)} %get-tuple-element.444), channel_id=1, replica_groups=mesh['tm'=16,'fsdp'=2] {'tm'}, use_global_device_ids=true, to_apply=%region_25.26 | all-reduce | flops 512 | bytes 4096 | tf_op jit(solution)/shard_map/psum | solution.py:237
  302.4 61.7 %all-reduce.8 = (bf16[32,512]{1,0:T(8,128)(2,1)S(1)}, bf16[32,512]{1,0:T(8,128)(2,1)S(1)}, f32[16,512]{1,0:T(8,128)}) all-reduce(f32[32,512]{1,0:T(8,128)S(1)} %reshape.308, f32[32,512]{1,0:T(8,128)S(1)} %reshape.303, f32[16,512]{1,0:T(8,128)} %reduce-scatter.11.cloned.1.call-done), channel_id=1, replica_groups=mesh['tm'=16,'fsdp'=2] {'tm'}, use_global_device_ids=true, to_apply=%region_14.15 | all-reduce | flops 40960 | bytes 262144 | tf_op jit(solution)/shard_map/psum | solution.py:204
  367.3 5.8 multiply_convert_fusion.1
  397.2 6.3 fusion.199
  403.5 10.7 %fusion.39 = (bf16[1536,1,1024]{2,0,1:T(8,128)(2,1)}, bf16[1536,1,1024]{2,0,1:T(8,128)(2,1)}) fusion(bf16[16,1024]{1,0:T(8,128)(2,1)S(1)} %collective-permute-done.6, bf16[1536,512]{1,0:T(8,128)(2,1)S(1)} %copy-done.3, bf16[1536,512]{1,0:T(8,128)(2,1)S(1)} %get-tuple-element.382, bf16[1536]{0:T(1024)(128)(2,1)S(1)} %get-tuple-element.421, ...), kind=kLoop, calls=%fused_computation.56 | loop fusion | flops 25165824 | bytes 9508864 | tf_op jit(solution)/shard_map/stack | solution.py:271
  414.3 9.1 %fusion.43 = (bf16[1536,1,1024]{2,0,1:T(8,128)(2,1)S(1)}, bf16[1536,1,1024]{2,0,1:T(8,128)(2,1)S(1)}) fusion(bf16[16,1024]{1,0:T(8,128)(2,1)S(1)} %collective-permute-done.4, bf16[1536,512]{1,0:T(8,128)(2,1)S(1)} %copy-done.6, bf16[1536,512]{1,0:T(8,128)(2,1)S(1)} %copy-done.4, bf16[1536]{0:T(1024)(128)(2,1)S(1)} %get-tuple-element.419, ...), kind=kLoop, calls=%fused_computation.64 | loop fusion | flops 25165824 | bytes 9508864 | tf_op jit(solution)/shard_map/stack | solution.py:271
  423.4 6.5 fusion.23
  429.9 20.3 %fusion.80 = (bf16[1,1536,512]{2,1,0:T(8,128)(2,1)}, bf16[1,1536,512]{2,1,0:T(8,128)(2,1)}, bf16[1536,512]{1,0:T(8,128)(2,1)}, f32[1,1536,512]{2,1,0:T(8,128)}, ...) fusion(f32[1536,1024]{1,0:T(8,128)} %fusion.199, ...), kind=kOutput, calls=%fused_computation.131 | convolution fusion | flops 4887674880 | bytes 50350080 | tf_op jit(solution)/shard_map/dot_general | solution.py:279
  450.2 4.8 fusion.73
  465.8 7.8 fusion.55
  473.7 8.3 %convolution_add_fusion.2 = f32[1536,1024]{1,0:T(8,128)} fusion(f32[1536,1024]{1,0:T(8,128)S(1)} %fusion.55, bf16[1536,512]{1,0:T(8,128)(2,1)S(1)} %copy-done.7, bf16[1536,512]{1,0:T(8,128)(2,1)S(1)} %copy-done.5, bf16[1536,512]{1,0:T(8,128)(2,1)S(1)} %copy-done.29, bf16[1536,512]{1,0:T(8,128)(2,1)S(1)} %copy-done.15, bf16[1536,512]{1,0:T(8,128)(2,1)S(1)} %copy-done.28), kind=kOutput, calls=%fused_computation.37 | convolution fusion | flops 4853858304 | bytes 20447232 | tf_op jit(solution)/shard_map/dot_general | solution.py:43
  482.5 14.7 %reduce-scatter.15.cloned.1.call-done = f32[256,1024]{0,1:T(8,128)} async-done(((f32[512,1024]{0,1:T(8,128)}), f32[256,1024]{0,1:T(8,128)}) %reduce-scatter.15.cloned.1.call-update) | async-done | bytes 1048592 | tf_op jit(solution)/shard_map/reduce_scatter | solution.py:291
  497.2 34.6 %reduce-scatter.13.cloned.1.call-done = f32[256,1024]{1,0:T(8,128)} async-done(((f32[512,1024]{1,0:T(8,128)}), f32[256,1024]{1,0:T(8,128)}) %reduce-scatter.13.cloned.1.call-update) | async-done | bytes 1048592 | tf_op jit(solution)/shard_map/reduce_scatter | solution.py:290
  531.8 79.8 %reduce-scatter.17.cloned.1.call-done = f32[3,256,1024]{2,1,0:T(8,128)} async-done(((f32[3,512,1024]{2,1,0:T(8,128)}), f32[3,256,1024]{2,1,0:T(8,128)}) %reduce-scatter.17.cloned.1.call-update) | async-done | bytes 3145744 | tf_op jit(solution)/shard_map/reduce_scatter | solution.py:292
  628.9 176.1 %all-reduce.7.cloned.1.call-done = (f32[256,1024]{1,0:T(8,128)}, f32[256,1024]{0,1:T(8,128)}, f32[3,256,1024]{2,1,0:T(8,128)}, f32[256,512]{0,1:T(8,128)}, f32[2...) async-done(((f32[256,1024]{1,0:T(8,128)}, f32[256,1024]{0,1:T(8,128)}, f32[3,256,1024]{2,1,0:T(8,128)}, ...) | async-done | bytes 9437200 | tf_op jit(solution)/shard_map/psum | solution.py:300
  (396 shorter events, 128.8 us)
Async XLA Ops:
  7.2 151.6 %all-gather.12.cloned.1.call-start = ((), (), s32[]{:S(2)}) async-start(), calls=%async_computation.11 | async-start | bytes 1572864 | tf_op jit(solution)/shard_map/all_gather | solution.py:130
  9.5 155.5 %all-gather.10.cloned.1.call-start = ((), (), s32[]{:S(2)}) async-start(), calls=%async_computation.10 | async-start | bytes 1572864 | tf_op jit(solution)/shard_map/all_gather | solution.py:129
  11.7 184.8 %all-gather.14.cloned.1.call-start = ((), (), s32[]{:S(2)}) async-start(), calls=%async_computation.12 | async-start | bytes 4718592 | tf_op jit(solution)/shard_map/all_gather | solution.py:131
  13.2 192.6 %all-gather.18.cloned.1.call-start = ((), (), s32[]{:S(2)}) async-start(), calls=%async_computation.14 | async-start | bytes 1572864 | tf_op jit(solution)/shard_map/all_gather | solution.py:137
  15.4 240.8 %all-gather.16.cloned.1.call-start = ((), (), s32[]{:S(2)}) async-start(), calls=%async_computation.13 | async-start | bytes 1572864 | tf_op jit(solution)/shard_map/all_gather | solution.py:136
  16.4 29.0 %copy-start.62 = (s32[2,1,30]{2,1,0:T(1,128)S(1)}, s32[2,1,30]{2,1,0:T(1,128)}, u32[]{:S(2)}) copy-start(s32[2,1,30]{2,1,0:T(1,128)} %param.24) | copy-start | bytes 724
  16.4 29.1 %copy-start.52 = (f32[16,512]{1,0:T(8,128)S(1)}, f32[16,512]{1,0:T(8,128)}, u32[]{:S(2)}) copy-start(f32[16,512]{1,0:T(8,128)} %param.26) | copy-start | bytes 98308
  16.4 33.5 %copy-start.47 = (f32[256,512]{1,0:T(8,128)S(1)}, f32[256,512]{1,0:T(8,128)}, u32[]{:S(2)}) copy-start(f32[256,512]{1,0:T(8,128)} %param.30) | copy-start | bytes 1572868
  16.4 286.0 %reduce-scatter.11.cloned.1.call-start = ((), (), s32[]{:S(2)}) async-start(), calls=%async_computation.15 | async-start | bytes 98304 | tf_op jit(solution)/shard_map/reduce_scatter | solution.py:289
  17.4 149.0 %copy-start.53 = (s32[1536]{0:T(1024)}, s32[1536]{0:T(1024)S(1)}, u32[]{:S(2)}) copy-start(s32[1536]{0:T(1024)S(1)} %slice.240) | copy-start | bytes 18436
  34.2 108.2 %copy-start.48 = (f32[256,512]{1,0:T(8,128)S(1)}, f32[256,512]{1,0:T(8,128)}, u32[]{:S(2)}) copy-start(f32[256,512]{1,0:T(8,128)} %param.33) | copy-start | bytes 1572868
  45.4 111.2 %copy-start.50 = (f32[1536]{0:T(1024)}, f32[1536]{0:T(1024)S(1)}, u32[]{:S(2)}) copy-start(f32[1536]{0:T(1024)S(1)} %convert_element_type.345) | copy-start | bytes 18436
  180.0 9.2 %collective-permute-start.2 = (bf16[16,512]{1,0:T(8,128)(2,1)S(1)}, bf16[16,512]{1,0:T(8,128)(2,1)S(1)}, u32[]{:S(2)}, u32[]{:S(2)}) collective-permute-start(bf16[16,512]{1,0:T(8,128)(2,1)S(1)} %get-tuple-element.416), channel_id=1, source_target_pairs={{0,2},{2,4},{4,6},{6,8},{8,10},{10,12},{12,14},{14,16},{16,18},{18... | collective-permute-start | bytes 49160 | tf_op jit(solution)/shard_map/ppermute | solution.py:23
  181.3 7.9 collective-permute-start.3
  182.6 10.3 %collective-permute-start = (bf16[16,512]{1,0:T(8,128)(2,1)S(1)}, bf16[16,512]{1,0:T(8,128)(2,1)S(1)}, u32[]{:S(2)}, u32[]{:S(2)}) collective-permute-start(bf16[16,512]{1,0:T(8,128)(2,1)S(1)} %get-tuple-element.412), channel_id=1, source_target_pairs={{0,2},{2,4},{4,6},{6,8},{8,10},{10,12},{12,14},{14,16},{16,18},{18... | collective-permute-start | bytes 49160 | tf_op jit(solution)/shard_map/ppermute | solution.py:23
  187.8 5.1 collective-permute-start.1
  256.2 37.5 %copy-start.57 = (f32[1024]{0:T(1024)}, f32[1024]{0:T(1024)S(1)}, u32[]{:S(2)}) copy-start(f32[1024]{0:T(1024)S(1)} %get-tuple-element.358) | copy-start | bytes 12292
  295.4 187.0 %reduce-scatter.19.cloned.1.call-start = ((), (), s32[]{:S(2)}) async-start(), calls=%async_computation.19 | async-start | bytes 1572864 | tf_op jit(solution)/shard_map/reduce_scatter | solution.py:293
  297.1 185.3 %reduce-scatter.23.cloned.1.call-start = ((), (), s32[]{:S(2)}) async-start(), calls=%async_computation.21 | async-start | bytes 1572864 | tf_op jit(solution)/shard_map/reduce_scatter | solution.py:295
  299.3 183.1 %reduce-scatter.21.cloned.1.call-start = ((), (), s32[]{:S(2)}) async-start(), calls=%async_computation.20 | async-start | bytes 1572864 | tf_op jit(solution)/shard_map/reduce_scatter | solution.py:294
  300.2 65.6 %copy-start.2 = (bf16[512,1024]{1,0:T(8,128)(2,1)S(1)}, bf16[512,1024]{1,0:T(8,128)(2,1)}, u32[]{:S(2)}) copy-start(bf16[512,1024]{1,0:T(8,128)(2,1)} %all-gather.16.cloned.1.call-done) | copy-start | bytes 3145732
  301.5 180.9 %reduce-scatter.25.cloned.1.call-start = ((), (), s32[]{:S(2)}) async-start(), calls=%async_computation.22 | async-start | bytes 1572864 | tf_op jit(solution)/shard_map/reduce_scatter | solution.py:296
  367.3 115.2 %reduce-scatter.29.cloned.1.call-start = ((), (), s32[]{:S(2)}) async-start(), calls=%async_computation.24 | async-start | bytes 3145728 | tf_op jit(solution)/shard_map/reduce_scatter | solution.py:298
  385.1 97.4 %reduce-scatter.27.cloned.1.call-start = ((), (), s32[]{:S(2)}) async-start(), calls=%async_computation.23 | async-start | bytes 3145728 | tf_op jit(solution)/shard_map/reduce_scatter | solution.py:297
  386.1 28.2 %collective-permute-start.4 = (bf16[16,1024]{1,0:T(8,128)(2,1)S(1)}, bf16[16,1024]{1,0:T(8,128)(2,1)S(1)}, u32[]{:S(2)}, u32[]{:S(2)}) collective-permute-start(bf16[16,1024]{1,0:T(8,128)(2,1)S(1)} %get-tuple-element.398), channel_id=1, source_target_pairs={{2,0},{4,2},{6,4},{8,6},{10,8},{12,10},{14,12},{16,14},{18,16},{20... | collective-permute-start | bytes 98312 | tf_op jit(solution)/shard_map/ppermute | solution.py:26
  387.3 26.9 %collective-permute-start.5 = (bf16[16,1024]{1,0:T(8,128)(2,1)S(1)}, bf16[16,1024]{1,0:T(8,128)(2,1)S(1)}, u32[]{:S(2)}, u32[]{:S(2)}) collective-permute-start(bf16[16,1024]{1,0:T(8,128)(2,1)S(1)} %get-tuple-element.399), channel_id=1, source_target_pairs={{0,2},{2,4},{4,6},{6,8},{8,10},{10,12},{12,14},{14,16},{16,18},{18... | collective-permute-start | bytes 98312 | tf_op jit(solution)/shard_map/ppermute | solution.py:23
  391.0 12.5 %collective-permute-start.6 = (bf16[16,1024]{1,0:T(8,128)(2,1)}, bf16[16,1024]{1,0:T(8,128)(2,1)S(1)}, u32[]{:S(2)}, u32[]{:S(2)}) collective-permute-start(bf16[16,1024]{1,0:T(8,128)(2,1)} %get-tuple-element.402), channel_id=1, source_target_pairs={{2,0},{4,2},{6,4},{8,6},{10,8},{12,10},{14,12},{16,14},{18,16},{20... | collective-permute-start | bytes 98312 | tf_op jit(solution)/shard_map/ppermute | solution.py:26
  392.3 11.2 %collective-permute-start.7 = (bf16[16,1024]{1,0:T(8,128)(2,1)S(1)}, bf16[16,1024]{1,0:T(8,128)(2,1)S(1)}, u32[]{:S(2)}, u32[]{:S(2)}) collective-permute-start(bf16[16,1024]{1,0:T(8,128)(2,1)S(1)} %get-tuple-element.403), channel_id=1, source_target_pairs={{0,2},{2,4},{4,6},{6,8},{8,10},{10,12},{12,14},{14,16},{16,18},{18... | collective-permute-start | bytes 98312 | tf_op jit(solution)/shard_map/ppermute | solution.py:23
  397.1 100.1 %reduce-scatter.15.cloned.1.call-start = ((), (), s32[]{:S(2)}) async-start(), calls=%async_computation.17 | async-start | bytes 3145728 | tf_op jit(solution)/shard_map/reduce_scatter | solution.py:291
  458.3 73.5 %reduce-scatter.13.cloned.1.call-start = ((), (), s32[]{:S(2)}) async-start(), calls=%async_computation.16 | async-start | bytes 3145728 | tf_op jit(solution)/shard_map/reduce_scatter | solution.py:290
  465.7 145.9 %reduce-scatter.17.cloned.1.call-start = ((), (), s32[]{:S(2)}) async-start(), calls=%async_computation.18 | async-start | bytes 9437184 | tf_op jit(solution)/shard_map/reduce_scatter | solution.py:292
  482.1 322.9 %all-reduce.7.cloned.1.call-start = ((), (), s32[]{:S(2)}) async-start(), calls=%async_computation.25 | async-start | bytes 18874368 | tf_op jit(solution)/shard_map/psum | solution.py:300
  (69 other events, 400.8 us)
Sparse Core Ops, SparseCore 0:
  10.1 30.0 all-gather.11
  42.4 26.2 all-gather.9
  70.7 45.4 all-gather.13
  118.2 21.2 all-gather.17
  141.5 21.7 all-gather.15
  295.5 6.0 reduce-scatter.10
  304.4 20.3 reduce-scatter.18
  327.7 20.3 reduce-scatter.22
  350.9 20.3 reduce-scatter.20
  374.0 20.3 reduce-scatter.24
  396.6 31.8 reduce-scatter.28
  430.6 31.8 reduce-scatter.26
  465.3 31.8 reduce-scatter.14
  499.9 31.8 reduce-scatter.12
  534.5 77.0 reduce-scatter.16
  617.0 187.9 all-reduce.6
where the time goes:
time: 832 us; the launch traced here: 827 us
  waiting for transfers between devices  306 us (37%)
  blocking collectives  255 us (31%)
  matrix products  135 us (16%)
  other arithmetic  69.2 us (8%)
  local copies, waits for them, and re-layouts  27.7 us (3%)
  starting transfers between devices  18.7 us (2%)
  between operations  15.6 us (2%)
    psum x1, waiting for transfers between devices, per_device(): lax.psum((shares[0], shares[1], shares[2], shares[3], shares[4], shares[5...  176 us
    reduce_scatter x1, waiting for transfers between devices, per_device(): lax.psum_scatter(acc_conv_taps, 'fsdp', scatter_dimension=1, tiled=True)  79.8 us
    all_gather x4, blocking collectives, joined_2(): gathered = jax.tree.map(lambda a: lax.all_gather(a, axis), part)  76.7 us
    psum x1, blocking collectives, per_device(): context = lax.psum(context_part, 'tm')  61.7 us
    dot_general x16, matrix products, contract_rows(): lax.dot_general(left, right, (((0,), (0,)), ((), ())), precision=precisio...  41.8 us
    reduce_scatter x1, waiting for transfers between devices, per_device(): lax.psum_scatter(acc_step, 'fsdp', scatter_dimension=0, tiled=True)  34.6 us
    psum x1, blocking collectives, per_device(): film_cot = lax.psum(film_local, 'tm')  32.8 us
    psum x1, blocking collectives, per_device(): row_total = lax.psum(row_part, 'tm')  30 us
  transfers between devices with their start and end apart: 24, of which 4 were waited for; matrix products, arithmetic and copies ran while one was open for 24% of the time, Pallas kernels for 0%

commit v1 on v0

v1 whole, which is shorter than its diff:
```python
import functools
import math

import jax
import jax.numpy as jnp
from jax import lax
from jax.experimental import pallas as pl
from jax.experimental.pallas import tpu as pltpu
from jax.sharding import PartitionSpec as P

HEADS = 8
QUERIES = 32
DILATION = 16
MICRO = 2
HALO = 2 * DILATION

SQRT_HALF = 0.7071067811865476
VMEM_LIMIT = 40 * 2**20
NT = ((1,), (1,))
TN = ((0,), (0,))
bf16 = jnp.bfloat16
f32 = jnp.float32


def dotf(left, right, dims=((1,), (0,))):
    return lax.dot_general(left, right, (dims, ((), ())), preferred_element_type=f32)


def lanes(block, width):
    return jnp.concatenate([block] * (width // block.shape[1]), axis=1)


VSPEC = pl.BlockSpec(memory_space=pltpu.VMEM)
SSPEC = pl.BlockSpec(memory_space=pltpu.SMEM)
ANYSPEC = pl.BlockSpec(memory_space=pl.ANY)


def fixed(array):
    return pltpu.with_memory_space_constraint(array, pltpu.VMEM), VSPEC


def whole(array):
    return pltpu.with_memory_space_constraint(array, pltpu.HBM), pl.BlockSpec(array.shape, lambda *_: (0,) * array.ndim)


def blocks(array, tile, first=0):
    return pltpu.with_memory_space_constraint(array, pltpu.HBM), pl.BlockSpec(
        (1, tile, array.shape[2]), lambda i, j: (i + first, j, 0)
    )


def hbm(array):
    return pltpu.with_memory_space_constraint(array, pltpu.HBM), pl.BlockSpec(memory_space=pltpu.HBM)


def scalars(array):
    return array, SSPEC


def call(kernel, grid, ins, outs, name, flops, scratch=(), after=(), aliases=None):
    count, waits = len(ins), len(after)

    def body(*refs):
        kernel(*refs[:count], *refs[count + waits :])

    return pl.pallas_call(
        body,
        grid=grid,
        in_specs=[spec for _, spec in ins] + [ANYSPEC] * waits,
        out_specs=[spec for _, spec in outs],
        out_shape=[out for out, _ in outs],
        scratch_shapes=scratch,
        input_output_aliases=aliases or {},
        cost_estimate=pl.CostEstimate(
            flops=int(flops), bytes_accessed=2**12, transcendentals=0
        ),
        compiler_params=pltpu.CompilerParams(vmem_limit_bytes=VMEM_LIMIT),
        name=name,
    )(*[array for array, _ in ins], *after)


def new(shape, kind=f32):
    return pltpu.HBM(shape, kind), pl.BlockSpec(shape, lambda *_: (0,) * len(shape))


def new_fixed(shape, kind=f32):
    return pltpu.VMEM(shape, kind), VSPEC


def new_hbm(shape, kind=f32):
    return pltpu.HBM(shape, kind), pl.BlockSpec(memory_space=pltpu.HBM)


def new_blocks(shape, kind, tile, first=0):
    return pltpu.HBM(shape, kind), pl.BlockSpec(
        (1, tile, shape[2]), lambda i, j: (i + first, j, 0)
    )


def split_rows(row, parts):
    terms = []
    for _ in range(parts):
        term = row.astype(bf16)
        terms.append(term)
        row = row - term.astype(f32)
    return terms


def pack_kernel(layouts, place, *refs):
    count = sum(map(len, layouts))
    weights, refs = list(refs[:count]), refs[count:]
    outs, helds, sems = refs[: len(layouts)], refs[len(layouts) : -1], refs[-1]
    copies = []
    for layout, held in zip(layouts, helds, strict=True):
        for row, column in layout:
            weight = weights.pop(0)
            views = [weight] if len(weight.shape) == 2 else [weight.at[t] for t in range(weight.shape[0])]
            rows = views[0].shape[0] // 4
            start = pl.multiple_of(place[3] * rows, rows)
            for t, view in enumerate(views):
                copies.append(
                    pltpu.make_async_copy(
                        view.at[pl.ds(start, rows)],
                        held.at[pl.ds(row + t * rows, rows), pl.ds(column, view.shape[1])],
                        sems.at[len(copies)],
                    )
                )
    for copy in copies:
        copy.start()
    for copy in copies:
        copy.wait()
    for out, held in zip(outs, helds, strict=True):
        out[...] = held[...].astype(bf16)


def edges_kernel(*refs):
    arrays, (last, first, sems) = refs[:-3], refs[-3:]
    copies = []
    for k, array in enumerate(arrays):
        rows = array.shape[1]
        copies.append(
            pltpu.make_async_copy(array.at[:, pl.ds(rows - HALO, HALO)], last.at[k], sems.at[2 * k])
        )
        copies.append(
            pltpu.make_async_copy(array.at[:, pl.ds(0, HALO)], first.at[k], sems.at[2 * k + 1])
        )
    for copy in copies:
        copy.start()
    for copy in copies:
        copy.wait()


def unpack_kernel(layout, members, place, *refs):
    count = len(layout)
    shards, (here, over, core, both) = refs[:count], refs[count : count + 4]
    fulls, copies = refs[count + 4 : 2 * count + 4], refs[2 * count + 4 :]
    member, quarter = place[2], place[3]
    sources = ((here, quarter), (over, quarter ^ 1), (core, quarter ^ 2), (both, quarter ^ 3))
    for shard, full, (row, column) in zip(shards, fulls, layout, strict=True):
        rows, width = shard.shape[-2:]
        part = rows // 4
        taps = 1 if len(shard.shape) == 2 else shard.shape[0]
        for t in range(taps):
            own = shard[...] if taps == 1 else shard[t]
            top = t * members * rows
            full[pl.ds(pl.multiple_of(top + member * rows, part), rows)] = own.astype(bf16)
            at = row + t * part
            for j in range(1, members):
                for source, q in sources:
                    start = pl.multiple_of(top + (member ^ j) * rows + q * part, part)
                    full[pl.ds(start, part)] = source[j - 1, at : at + part, column : column + width]
    for full, copy in zip(fulls, copies, strict=False):
        copy[...] = full[...]


def masks_kernel(rows, slot, total, place, lengths, masks, ends):
    micro, utters = lengths.shape
    hots = masks.shape[2] - 3 * 128
    lane = lax.broadcasted_iota(jnp.int32, (1, hots), 1)
    lane = jnp.where(lane >= micro * slot, lane - micro * slot, lane)
    row = lax.broadcasted_iota(jnp.int32, (hots, 128), 0)
    count = jnp.where(row < micro * slot, 1.0, 0.0).astype(bf16)
    first = place[1] * rows - HALO
    chunk = rows // 6
    for i in range(micro):
        opens = jnp.full((1, hots), total, jnp.int32)
        closes = jnp.zeros((1, hots), jnp.int32)
        end = jnp.int32(0)
        for u in range(utters):
            mine = lane == i * slot + u
            if u == utters - 1:
                alive_until = end
            opens = jnp.where(mine, end, opens)
            end = end + lengths[i, u]
            closes = jnp.where(mine, end, closes)

        def rows_of(start, size, i=i, opens=opens, closes=closes, alive_until=alive_until):
            position = lax.broadcasted_iota(jnp.int32, (size, hots), 0) + start

            def one_hot(offset):
                shifted = position + offset
                return jnp.where((shifted >= opens) & (shifted < closes), 1.0, 0.0).astype(bf16)

            here = one_hot(0)
            low = dotf(here * one_hot(-DILATION), count).astype(bf16)
            high = dotf(here * one_hot(DILATION), count).astype(bf16)
            alive = (position[:, :128] < alive_until) & (position[:, :128] >= 0)
            return jnp.concatenate(
                [low, high, jnp.where(alive, 1.0, 0.0).astype(bf16), here], axis=1
            )

        ends[i, 0:HALO] = rows_of(first, HALO)
        ends[i, HALO:] = rows_of(first + HALO + rows, HALO)

        @pl.loop(0, rows // chunk)
        def _(k, i=i, rows_of=rows_of):
            at = pl.multiple_of(k * chunk, chunk)
            masks[i, pl.ds(at, chunk)] = rows_of(first + HALO + at, chunk)


def film_kernel(
    tile, frames, cond, low, high, masks, ends, embed, w_step, w_cond, hidden, gain, film_rows
):
    i, j = pl.program_id(0), pl.program_id(1)
    width = frames.shape[2]
    rows = hidden.shape[1] - 2 * HALO - 2 * DILATION

    @pl.when((i == 0) & (j == 0))
    def _():
        step_film = dotf(embed[...], w_step[...])
        film_rows[...] = jnp.concatenate(split_rows(step_film, 2), axis=0)

    def film(frame_rows, cond_rows, hot):
        both = dotf(cond_rows, w_cond[...]) + dotf(hot, film_rows[...])
        gain_rows = both[:, :width]
        return (frame_rows.astype(f32) * (1.0 + gain_rows) + both[:, width:]).astype(bf16), gain_rows

    @pl.when(j == 0)
    def _():
        edge, _ = film(
            jnp.concatenate([low[0, i], high[0, i]], axis=0),
            jnp.concatenate([low[1, i], high[1, i]], axis=0),
            ends[i, :, 384:],
        )
        nothing = jnp.zeros((DILATION, width), bf16)
        hidden[i, 0:DILATION] = nothing
        hidden[i, DILATION : DILATION + HALO] = edge[:HALO]
        hidden[i, DILATION + HALO + rows : DILATION + 2 * HALO + rows] = edge[HALO:]
        hidden[i, DILATION + 2 * HALO + rows :] = nothing

    base = pl.multiple_of(j * tile, tile)
    own, gain_rows = film(frames[0], cond[0], masks[0, :, 384:])
    hidden[i, pl.ds(DILATION + HALO + base, tile)] = own
    gain[0] = gain_rows


def halves_of(core, width):
    mine = pl.multiple_of(core * width, width)
    other = pl.multiple_of((1 - core) * width, width)
    return mine, other


def conv_kernel(
    tile, place, hidden, masks, mask_ends, res, skip, low, high, w_conv, w_proj, film,
    d_conv, d_conv_copy, gated, sums, keep, send, proj_total, columns, sems,
):
    i, j = pl.program_id(0), pl.program_id(1)
    width = res.shape[2]
    rows = d_conv.shape[1] - 2 * HALO
    gain, shift = 1.0 + film[i, 0:1, :width], film[i, 0:1, width:]

    def body(before, here, after, keep_low, keep_high, alive, res_rows, skip_rows):
        taps = jnp.concatenate(
            [before * lanes(keep_low, width), here, after * lanes(keep_high, width)], axis=1
        )
        conv = dotf(taps, w_conv[...])
        th = jnp.tanh(conv[:, :width])
        sg = 0.5 + 0.5 * jnp.tanh(0.5 * conv[:, width:])
        alive = lanes(alive.astype(f32), width)
        branch = jnp.concatenate(
            [
                (res_rows.astype(f32) * (SQRT_HALF * alive)).astype(bf16),
                (skip_rows.astype(f32) * alive).astype(bf16),
            ],
            axis=1,
        )
        d_gated = dotf(branch, w_proj[...], NT)
        act = th * sg
        d_act = d_gated * gain
        left = (d_act * sg * (1.0 - th * th)).astype(bf16)
        right = (d_act * act * (1.0 - sg)).astype(bf16)
        return act, d_gated, branch, left, right

    @pl.when(j == 0)
    def _():
        def ends(ref, at):
            return jnp.concatenate(
                [ref[i, at : at + HALO], ref[i, at + HALO + rows : at + 2 * HALO + rows]], axis=0
            )

        _, _, _, left, right = body(
            ends(hidden, 0),
            ends(hidden, DILATION),
            ends(hidden, 2 * DILATION),
            mask_ends[i, :, 0:128],
            mask_ends[i, :, 128:256],
            mask_ends[i, :, 256:384],
            jnp.concatenate([low[2, i], high[2, i]], axis=0),
            jnp.concatenate([low[3, i], high[3, i]], axis=0),
        )
        d_conv[i, 0:HALO, :width] = left[:HALO]
        d_conv[i, 0:HALO, width:] = right[:HALO]
        d_conv[i, HALO + rows :, :width] = left[HALO:]
        d_conv[i, HALO + rows :, width:] = right[HALO:]
        columns[...] = jnp.zeros(columns.shape, f32)

    @pl.when((i == 0) & (j == 0))
    def _():
        sums[...] = jnp.zeros(sums.shape, f32)

    base = pl.multiple_of(j * tile, tile)

    def at(ref, offset):
        return ref[i, pl.ds(base + offset, tile)]

    act, d_gated, branch, left, right = body(
        at(hidden, HALO),
        at(hidden, HALO + DILATION),
        at(hidden, HALO + 2 * DILATION),
        masks[0, :, 0:128],
        masks[0, :, 128:256],
        masks[0, :, 256:384],
        res[0],
        skip[0],
    )
    d_conv[i, pl.ds(base + HALO, tile), :width] = left
    d_conv[i, pl.ds(base + HALO, tile), width:] = right
    gated_rows = (act * gain + shift).astype(bf16)
    gated[0] = gated_rows
    columns[:, :width] += jnp.sum((d_gated * act).reshape(tile // 8, 8, width), axis=0)
    columns[:, width:] += jnp.sum(d_gated.reshape(tile // 8, 8, width), axis=0)
    part = dotf(gated_rows, branch, TN)
    first = (i == 0) & (j == 0)

    @pl.when(first)
    def _():
        proj_total[...] = part

    @pl.when(jnp.logical_not(first))
    def _():
        proj_total[...] += part

    last = j == rows // tile - 1
    copies = [
        pltpu.make_async_copy(d_conv.at[m], d_conv_copy.at[m], sems.at[m]) for m in range(MICRO)
    ]
    for m in range(MICRO):
        pl.when(last & (i == m))(copies[m].start)

    @pl.when(last & (i == MICRO - 1))
    def _():
        for copy in copies:
            copy.wait()

    for m in range(MICRO):

        @pl.when(last & (i == m))
        def _(m=m):
            sums[m : m + 1] = jnp.sum(columns[...], axis=0, keepdims=True)

    @pl.when(last & (i == MICRO - 1))
    def _():
        mine, other = halves_of(place[0], width)
        send[0] = proj_total[:, pl.ds(other, width)].astype(bf16)
        keep[0] = proj_total[:, pl.ds(mine, width)]


def conv_grad_kernel(place, hidden, masks, d_conv, keep, send):
    t = pl.program_id(0)
    micro, width = hidden.shape[0], hidden.shape[2]
    rows = d_conv.shape[1] - 2 * HALO
    mine, other = halves_of(place[0], width)

    for tap, lane in ((0, 0), (1, None), (2, 128)):

        @pl.when(t == tap)
        def _(tap=tap, lane=lane):
            def tap_rows(i):
                part = hidden[i, HALO + DILATION * tap : HALO + DILATION * tap + rows]
                return part if lane is None else part * lanes(masks[i, :, lane : lane + 128], width)

            for columns, ref in ((other, send), (mine, keep)):
                total = dotf(tap_rows(0), d_conv[0, HALO : HALO + rows, pl.ds(columns, width)], TN)
                for i in range(1, micro):
                    total = total + dotf(
                        tap_rows(i), d_conv[i, HALO : HALO + rows, pl.ds(columns, width)], TN
                    )
                ref[tap] = total.astype(ref.dtype)


def hidden_grad_rows(tile, i, d_conv, masks, frames, gain, res, cond, w_conv, grad_frames, window, sems):
    j = pl.program_id(1)
    steps = pl.num_programs(1)
    width = frames.shape[2]

    def fetch(step):
        start = pl.multiple_of(HALO - DILATION + step * tile, DILATION)
        return pltpu.make_async_copy(
            d_conv.at[i, pl.ds(start, tile + 2 * DILATION)], window.at[step % 2], sems.at[step % 2]
        )

    @pl.when(j == 0)
    def _():
        fetch(0).start()

    @pl.when(j + 1 < steps)
    def _():
        fetch(j + 1).start()

    fetch(j).wait()
    slot = j % 2
    d_hidden = (
        dotf(window[slot, 2 * DILATION :] * lanes(masks[0, :, 128:256], 2 * width), w_conv[0], NT)
        + dotf(window[slot, DILATION : DILATION + tile], w_conv[1], NT)
        + dotf(window[slot, 0:tile] * lanes(masks[0, :, 0:128], 2 * width), w_conv[2], NT)
    )
    alive = lanes(masks[0, :, 256:384].astype(f32), width)
    grad_frames[0] = res[0].astype(f32) * (SQRT_HALF * alive) + d_hidden * (1.0 + gain[0])
    d_film = jnp.concatenate(
        [(d_hidden * frames[0].astype(f32)).astype(bf16), d_hidden.astype(bf16)], axis=1
    )
    return dotf(jnp.concatenate([cond[0], masks[0, :, 384:]], axis=1), d_film, TN)


def hidden_grad_first_kernel(
    tile, d_conv, masks, frames, gain, res, cond, w_conv, grad_frames, total, window, sems
):
    part = hidden_grad_rows(
        tile, 0, d_conv, masks, frames, gain, res, cond, w_conv, grad_frames, window, sems
    )
    j = pl.program_id(1)

    @pl.when(j == 0)
    def _():
        total[...] = part

    @pl.when(j > 0)
    def _():
        total[...] += part


def hidden_grad_last_kernel(
    tile, place, d_conv, masks, frames, gain, res, cond, w_conv, embed, earlier, _frames_0,
    grad_frames, keep, send, total, window, sems,
):
    part = hidden_grad_rows(
        tile, 1, d_conv, masks, frames, gain, res, cond, w_conv, grad_frames, window, sems
    )
    j = pl.program_id(1)
    width = frames.shape[2]

    @pl.when(j == 0)
    def _():
        total[...] = earlier[...] + part

    @pl.when(j > 0)
    def _():
        total[...] += part

    @pl.when(j == pl.num_programs(1) - 1)
    def _():
        mine, other = halves_of(place[0], width)
        count = embed.shape[0]
        for columns, ref in ((other, send), (mine, keep)):
            ref[0] = total[:width, pl.ds(columns, width)].astype(ref.dtype)
            d_step = total[width : width + count, pl.ds(columns, width)]
            step = jnp.zeros((width, width), f32)
            for term in split_rows(d_step, 3):
                step = step + dotf(embed[...], term, TN)
            ref[1] = step.astype(ref.dtype)


def out_kernel(gated, frames, masks, w_proj, res, skip):
    width = gated.shape[2]
    branch = dotf(gated[0], w_proj[...])
    alive = lanes(masks[0, :, 256:384].astype(f32), width)
    res[0] = ((frames[0].astype(f32) + branch[:, :width]) * (SQRT_HALF * alive)).astype(bf16)
    skip[0] = (branch[:, width:] * alive).astype(bf16)


def head_masks(width):
    column = lax.broadcasted_iota(jnp.int32, (1, width), 1)
    size = width // HEADS
    return [((column >= h * size) & (column < (h + 1) * size)).astype(f32) for h in range(HEADS)]


def attention_kernel(groups, place, *refs):
    pieces = refs[:groups]
    queries, w_query, w_key, w_value, w_out, w_film = refs[groups : groups + 6]
    film, prompt, probs, keys, values, spread, summaries, totals = refs[groups + 6 :]
    _, micro, shard, width = pieces[0].shape
    masks = head_masks(width)
    scale = 1.0 / math.sqrt(width // HEADS)
    for g, four in enumerate(pieces):
        for k in range(4):
            start = pl.multiple_of((place[1] ^ (4 * g + k)) * shard, shard)
            for i in range(micro):
                prompt[i, pl.ds(start, shard)] = four[k, i]
    query = dotf(queries[...], w_query[...])
    spread[...] = jnp.concatenate([(query * mask).astype(bf16) for mask in masks], axis=0)
    for i in range(micro):
        keys[i] = dotf(prompt[i], w_key[...]).astype(bf16)
        values[i] = dotf(prompt[i], w_value[...]).astype(bf16)
        scores = dotf(spread[...], keys[i], NT) * scale
        weights = jnp.exp(scores - jnp.max(scores, axis=1, keepdims=True))
        weights = weights / jnp.sum(weights, axis=1, keepdims=True)
        probs[i] = weights
        heads = dotf(weights.astype(bf16), values[i])
        context = heads[:QUERIES] * masks[0]
        for h in range(1, HEADS):
            context = context + heads[h * QUERIES : (h + 1) * QUERIES] * masks[h]
        context = context.astype(bf16)
        mixed = dotf(context, w_out[...])
        summary = jnp.mean(mixed, axis=0, keepdims=True).astype(bf16)
        summary = jnp.broadcast_to(summary.astype(f32), (8, width))
        summaries[i] = summary
        totals[i] = jnp.broadcast_to(
            jnp.sum(context.astype(f32), axis=0, keepdims=True), (8, width)
        )
        wide = jnp.concatenate([summary, summary], axis=0).astype(bf16)
        film[i] = dotf(wide, w_film[...])[:8]


def exact_dot(row, matrix):
    terms = split_rows(row, 3)
    stacked = jnp.concatenate(
        [term.astype(f32) for term in terms] + [jnp.zeros((13, row.shape[1]), f32)], axis=0
    )
    return jnp.sum(dotf(stacked.astype(bf16), matrix, NT), axis=0, keepdims=True)


SMALL_ROWS = QUERIES + 5 * 8


def attention_grad_kernel(
    place, sums, prompt, probs, keys, values, spread, summaries, totals, w_key, w_value, w_out, w_film,
    grad_prompt, keep, small, pair,
):
    micro, length, width = prompt.shape
    masks = head_masks(width)
    scale = 1.0 / math.sqrt(width // HEADS)
    mine, _ = halves_of(place[0], width)
    shard = grad_prompt.shape[1]
    own = pl.multiple_of(place[1] * shard, shard)
    d_query_total = jnp.zeros((QUERIES, width), f32)
    small[...] = jnp.zeros(small.shape, f32)
    for i in range(micro):
        d_film = sums[i : i + 1]
        d_mixed = exact_dot(d_film, w_film[...]) / QUERIES
        d_context = exact_dot(d_mixed, w_out[...]).astype(bf16).astype(f32)
        d_heads = jnp.concatenate(
            [d_context * mask for mask in masks] + [jnp.zeros((8, width), f32)], axis=0
        ).astype(bf16)
        d_probs = dotf(d_heads, values[i], NT)
        d_probs = jnp.concatenate(
            [jnp.broadcast_to(d_probs[h : h + 1], (QUERIES, length)) for h in range(HEADS)], axis=0
        )
        weights = probs[i]
        row_sums = jnp.sum(weights * d_probs, axis=1, keepdims=True)
        d_scores = (weights * (d_probs - row_sums)).astype(bf16)
        heads = dotf(d_scores, keys[i])
        d_query = heads[:QUERIES] * masks[0]
        for h in range(1, HEADS):
            d_query = d_query + heads[h * QUERIES : (h + 1) * QUERIES] * masks[h]
        d_query_total = d_query_total + d_query * scale
        pair[i, :, :width] = (dotf(d_scores, spread[...], TN) * scale).astype(bf16)
        wide = jnp.concatenate(
            [jnp.broadcast_to(d_context * mask, (QUERIES, width)) for mask in masks], axis=0
        ).astype(bf16)
        pair[i, :, width:] = dotf(weights.astype(bf16), wide, TN).astype(bf16)
        grad_prompt[i] = dotf(pair[i, pl.ds(own, shard), :width], w_key[...], NT) + dotf(
            pair[i, pl.ds(own, shard), width:], w_value[...], NT
        )
        rows = (summaries[i, 0:1], d_film[:, :width], d_film[:, width:], totals[i, 0:1], d_mixed)
        for k, row in enumerate(rows):
            at = QUERIES + 8 * k + i
            small[at : at + 1] = row
    small[0:QUERIES] = d_query_total
    grad = jnp.zeros((width, width), f32)
    for i in range(micro):
        grad = grad + dotf(prompt[i], pair[i, :, pl.ds(mine, width)], TN)
    keep[...] = grad


def exact_outer(left, right):
    one = [t.astype(f32) for t in split_rows(left, 3)]
    two = [t.astype(f32) for t in split_rows(right, 3)]
    picks = ((0, 0), (0, 1), (0, 2), (1, 0), (1, 1), (2, 0))
    stacked = [jnp.concatenate([side[p[k]] for p in picks], axis=0) for k, side in ((0, one), (1, two))]
    return dotf(stacked[0].astype(bf16), stacked[1].astype(bf16), TN)


def small_grad_kernel(place, packs, queries, w_query, g_queries, g_query, g_out, g_film, rows_of, queries_of):
    members, _, width = packs.shape
    member = place[2]
    shard = g_query.shape[0]
    start = pl.multiple_of(member * shard, shard)

    def group(k):
        at = QUERIES + 8 * k
        return jnp.concatenate([packs[m, at : at + 8] for m in range(members)], axis=0)

    rows_of[...] = exact_outer(
        group(0), jnp.concatenate([group(1), group(2)], axis=1)
    )
    g_film[...] = rows_of[pl.ds(start, shard)]
    rows_of[:, :width] = exact_outer(group(3), group(4))
    g_out[...] = rows_of[pl.ds(start, shard), :width]
    d_query = packs[0, 0:QUERIES]
    for m in range(1, members):
        d_query = d_query + packs[m, 0:QUERIES]
    rows_of[:, width:] = exact_outer(queries[...].astype(f32), d_query)
    g_query[...] = rows_of[pl.ds(start, shard), width:]
    terms = jnp.concatenate(split_rows(d_query, 3), axis=0)
    product = dotf(terms, w_query[...], NT)
    queries_of[...] = product[:QUERIES] + product[QUERIES : 2 * QUERIES] + product[2 * QUERIES :]
    count = g_queries.shape[0]
    for m in range(members):

        @pl.when(member == m)
        def _(m=m):
            g_queries[...] = queries_of[m * count : (m + 1) * count]


def swapped(array, axis, bit):
    count = lax.axis_size(axis)
    return lax.ppermute(array, axis, [(i, i ^ bit) for i in range(count)])


def bit_of(axis, bit):
    return (lax.axis_index(axis) // bit) % 2


def bits_of(axis):
    count = lax.axis_size(axis)
    assert count & (count - 1) == 0
    return [1 << b for b in range(count.bit_length() - 1)]


def rounded(array):
    return lax.reduce_precision(array, 8, 7)


def parted(total, axis, bit, dim):
    size = total.shape[dim] // 2
    mine = bit_of(axis, bit)
    away = lax.dynamic_slice_in_dim(total, (1 - mine) * size, size, dim).astype(bf16)
    return away, lax.dynamic_slice_in_dim(total, mine * size, size, dim)


def halvings(order):
    members = [("fsdp", bit, 1) for bit in reversed(bits_of("fsdp"))]
    second = [("tm", 2, 2)]
    return members + second if order == 0 else second + members


def doubled(mine, theirs, axis, bit, dim):
    clear = bit_of(axis, bit) == 0
    return jnp.concatenate(
        [jnp.where(clear, mine, theirs), jnp.where(clear, theirs, mine)], axis=dim
    )


def behind(array, *others):
    return lax.optimization_barrier((array, *others))[0]


def gathered(packed, members, *others):
    every = packed[None]
    for bit in bits_of("fsdp"):
        theirs = swapped(every, "fsdp", bit)
        every = theirs if members == 2 else jnp.concatenate([every, theirs], axis=0)
    here = every if members == 2 else every[1:]
    if others:
        here = behind(here, *others)
    over = swapped(here, "tm", 2)
    return here, over, swapped(here, "tm", 1), swapped(over, "tm", 1)


class Reduction:
    def __init__(self, halves):
        members = lax.axis_size("fsdp")
        self.steps = [halvings(k) for k in range(2)]
        self.totals = []
        for keeps, received in halves:
            total = jnp.concatenate(
                [k + r.astype(f32) for k, r in zip(keeps, received, strict=True)], axis=0
            )
            parts, rows, width = total.shape
            self.totals.append(total.reshape(parts, members, 2, rows // members // 2, width))
        self.depart()

    def depart(self):
        self.aways, self.kept = zip(
            *[parted(t, *s[0]) for t, s in zip(self.totals, self.steps, strict=True)], strict=True
        )

    def step(self):
        self.totals = [
            k + swapped(a, s[0][0], s[0][1]).astype(f32)
            for a, k, s in zip(self.aways, self.kept, self.steps, strict=True)
        ]
        self.steps = [s[1:] for s in self.steps]
        if self.steps[0]:
            self.depart()

    def finish(self):
        while self.steps[0]:
            self.step()
        total = jnp.concatenate(self.totals, axis=0)
        parts, rows, width = total.shape[0], total.shape[3], total.shape[4]
        total = total.reshape(parts, rows, width)
        away, kept = parted(total, "tm", 4, 1)
        total = kept + swapped(away, "tm", 4).astype(f32)
        for bit in bits_of("tm")[3:]:
            own = rounded(total)
            total = own + swapped(own.astype(bf16), "tm", bit).astype(f32)
        own = rounded(total).astype(bf16)
        for bit in (4, 2):
            own = doubled(own, swapped(own, "tm", bit), "tm", bit, 1)
        return own, swapped(own, "tm", 1)


def joined(pair, part):
    own, other = (a[part] for a in pair)
    return doubled(own, other, "tm", 1, own.ndim - 1).astype(f32)


def step_embedding(pack_steps, width):
    half_width = width // 2
    freqs = jnp.exp(jnp.arange(half_width).astype(f32) * (-math.log(10000.0) / half_width))
    angles = pack_steps.astype(f32)[:, None] * freqs[None, :]
    return jnp.concatenate([jnp.sin(angles), jnp.cos(angles)], axis=1)


def per_device(
    frames, conditioning, lengths, steps, prompt, queries, w_step, w_cond, w_conv, w_query, w_key,
    w_value, w_out, w_film, w_proj, grad_res, grad_skip,
):
    rows, width = frames.shape[2:]
    wide = 2 * width
    tile = rows // 3 if rows % 48 == 0 else rows
    tiles = (MICRO, rows // tile)
    tm_count, tm_index = lax.axis_size("tm"), lax.axis_index("tm")
    members, member = lax.axis_size("fsdp"), lax.axis_index("fsdp")
    shard_rows = w_cond.shape[0]
    shard_queries = queries.shape[0]
    frames, cond, res, skip = frames[:, 0], conditioning[:, 0], grad_res[:, 0], grad_skip[:, 0]
    core = tm_index % 2
    quarter = core * 2 + (tm_index // 2) % 2
    place = jnp.stack([core, tm_index, member, quarter]).astype(jnp.int32)
    product = 2 * MICRO * rows * width * wide

    part = shard_rows // 4

    def pack(weights, layouts, heights, name, after=()):
        return call(
            functools.partial(pack_kernel, layouts),
            (1,),
            [scalars(place)] + [hbm(w) for w in weights],
            [new_fixed((height, wide), bf16) for height in heights],
            name,
            10**5,
            scratch=[pltpu.VMEM((height, wide), f32) for height in heights]
            + [pltpu.SemaphoreType.DMA((10,))],
            after=after,
        )

    def unpack(weights, layout, quarters, name, *make):
        return call(
            functools.partial(unpack_kernel, layout, members),
            (1,),
            [scalars(place)] + [whole(w) for w in weights] + [whole(q) for q in quarters],
            [m((members * math.prod(w.shape[:-1]), w.shape[-1]), bf16) for m in make for w in weights],
            name,
            10**5,
        )

    first_weights = [w_cond, w_step]
    first_layout = [(0, 0), (part, 0)]
    second_weights = [w_key, w_value, w_query, w_out, w_film]
    second_layout = [(0, 0), (0, width), (part, 0), (part, width), (2 * part, 0)]
    third_weights = [w_conv, w_proj]
    third_layout = [(0, 0), (3 * part, 0)]
    (first,) = pack(first_weights, [first_layout], [2 * part], "pack_first")
    first_quarters = gathered(first, members)

    edge = (4, MICRO, HALO, width)
    last_rows, first_rows = call(
        edges_kernel,
        (1,),
        [hbm(a) for a in (frames, cond, res, skip)],
        [new_fixed(edge, bf16), new_fixed(edge, bf16)],
        "edges",
        10**5,
        scratch=[pltpu.SemaphoreType.DMA((8,))],
        after=[first],
    )
    low = lax.ppermute(last_rows, "tm", [(d, d + 1) for d in range(tm_count - 1)])
    high = lax.ppermute(first_rows, "tm", [(d + 1, d) for d in range(tm_count - 1)])

    utters = lengths.shape[2]
    slot = -(-utters // 32) * 32
    lane_count = 3 * 128 + 2 * MICRO * slot
    masks, mask_ends = call(
        functools.partial(masks_kernel, rows, slot, tm_count * rows),
        (1,),
        [scalars(place), scalars(lengths[:, 0])],
        [new((MICRO, rows, lane_count), bf16), new((MICRO, 2 * HALO, lane_count), bf16)],
        "masks",
        10**5,
        after=[last_rows],
    )
    own = prompt[:, 0]
    across = swapped(own, "tm", 2)
    near = jnp.stack([own, swapped(own, "tm", 1), across, swapped(across, "tm", 1)])
    second, third = pack(
        second_weights + third_weights,
        [second_layout, third_layout],
        [3 * part, 4 * part],
        "pack_rest",
        after=[masks, first_quarters[0], low, high, near],
    )

    pieces = [near] + [swapped(near, "tm", 4 * k) for k in range(1, tm_count // 4)]
    full_queries = queries.astype(bf16)
    for bit in bits_of("fsdp"):
        full_queries = doubled(full_queries, swapped(full_queries, "fsdp", bit), "fsdp", bit, 0)

    slots = jnp.pad(steps[:, 0], ((0, 0), (0, slot - utters))).reshape(-1)
    embed = step_embedding(slots, width).astype(bf16)

    full_cond, full_step = unpack(
        first_weights, first_layout, first_quarters, "unpack_first", new_fixed
    )
    hidden, gain = call(
        functools.partial(film_kernel, tile),
        tiles,
        [
            blocks(frames, tile),
            blocks(cond, tile),
            whole(low),
            whole(high),
            blocks(masks, tile),
            whole(mask_ends),
            whole(embed),
            fixed(full_step),
            fixed(full_cond),
        ],
        [
            new_fixed((MICRO, rows + 2 * HALO + 2 * DILATION, width), bf16),
            new_blocks((MICRO, rows, width), f32, tile),
        ],
        "film",
        10**5,
        scratch=[pltpu.VMEM((2 * MICRO * slot, wide), bf16)],
        after=[*pieces, full_queries],
    )

    full_key, full_value, full_query, full_out, full_film = unpack(
        second_weights, second_layout, gathered(second, members, hidden), "unpack_second", new
    )
    length = tm_count * prompt.shape[2]
    film, prompt_full, probs, keys, values, spread, summaries, totals = call(
        functools.partial(attention_kernel, len(pieces)),
        (1,),
        [scalars(place)]
        + [whole(a) for a in (*pieces, full_queries, full_query, full_key, full_value, full_out, full_film)],
        [
            new((MICRO, 8, wide)),
            new((MICRO, length, width), bf16),
            new((MICRO, HEADS * QUERIES, length)),
            new((MICRO, length, width), bf16),
            new((MICRO, length, width), bf16),
            new((HEADS * QUERIES, width), bf16),
            new((MICRO, 8, width)),
            new((MICRO, 8, width)),
        ],
        "attention",
        10**5,
    )

    full_conv, full_proj, conv_later, proj_later = unpack(
        third_weights, third_layout, gathered(third, members, hidden), "unpack_third", new_fixed, new
    )
    d_conv, d_conv_copy, gated, sums, proj_keep, proj_send = call(
        functools.partial(conv_kernel, tile),
        tiles,
        [
            scalars(place),
            fixed(hidden),
            blocks(masks, tile),
            whole(mask_ends),
            blocks(res, tile),
            blocks(skip, tile),
            whole(low),
            whole(high),
            fixed(full_conv),
            fixed(full_proj),
            whole(film),
        ],
        [
            new_fixed((MICRO, rows + 2 * HALO, wide), bf16),
            new_hbm((MICRO, rows + 2 * HALO, wide), bf16),
            new_blocks((MICRO, rows, width), bf16, tile),
            new((8, wide)),
            new((1, width, width)),
            new((1, width, width), bf16),
        ],
        "conv",
        5.5 * product,
        scratch=[
            pltpu.VMEM((width, wide), f32),
            pltpu.VMEM((8, wide), f32),
            pltpu.SemaphoreType.DMA((MICRO,)),
        ],
    )

    conv_keep, conv_send = call(
        conv_grad_kernel,
        (3,),
        [scalars(place), fixed(hidden), whole(masks), fixed(d_conv)],
        [new((3, width, width)), new((3, width, width), bf16)],
        "conv_grad",
        3 * product,
    )
    proj_received = swapped(proj_send, "tm", 1)
    conv_received = swapped(conv_send, "tm", 1)

    res_out, skip_out = call(
        out_kernel,
        tiles,
        [blocks(gated, tile), blocks(frames, tile), blocks(masks, tile), whole(proj_later)],
        [new_blocks((MICRO, rows, width), bf16, tile)] * 2,
        "outputs",
        product,
        after=[conv_send],
    )
    for bit in bits_of("tm"):
        sums = sums + swapped(sums, "tm", bit)

    conv_proj = Reduction(
        [
            ([conv_keep[:2]], [conv_received[:2]]),
            ([conv_keep[2:], proj_keep], [conv_received[2:], proj_received]),
        ]
    )
    stream = functools.partial(blocks, tile=tile)
    taps = conv_later.reshape(3, width, wide)
    window = [
        pltpu.VMEM((2, tile + 2 * DILATION, wide), bf16),
        pltpu.SemaphoreType.DMA((2,)),
    ]
    film_height = width + lane_count - 3 * 128
    grad_frames, total = call(
        functools.partial(hidden_grad_first_kernel, tile),
        (1, rows // tile),
        [hbm(d_conv_copy)] + [stream(a) for a in (masks, frames, gain, res, cond)] + [whole(taps)],
        [new_blocks((MICRO, rows, width), f32, tile), new((film_height, wide))],
        "hidden_grad_first",
        2.25 * product,
        scratch=window,
        after=[*conv_proj.aways, res_out],
    )
    grad_prompt, pair, small = call(
        attention_grad_kernel,
        (1,),
        [scalars(place)]
        + [
            whole(a)
            for a in (
                sums, prompt_full, probs, keys, values, spread, summaries, totals, full_key, full_value, full_out,
                full_film,
            )
        ],
        [new((MICRO, length // tm_count, width)), new((width, width)), new((SMALL_ROWS, width))],
        "attention_grad",
        product / 2,
        scratch=[pltpu.VMEM((MICRO, length, wide), bf16)],
    )
    conv_proj.step()
    grad_frames, keep, send = call(
        functools.partial(hidden_grad_last_kernel, tile),
        (1, rows // tile),
        [scalars(place), hbm(d_conv_copy)]
        + [stream(a, first=1) for a in (masks, frames, gain, res, cond)]
        + [whole(taps), whole(embed), whole(total), hbm(grad_frames)],
        [
            new_blocks((MICRO, rows, width), f32, tile, first=1),
            new((2, width, width)),
            new((2, width, width), bf16),
        ],
        "hidden_grad_last",
        2.25 * product,
        scratch=[pltpu.VMEM((film_height, wide), f32), *window],
        after=[*conv_proj.aways, small],
        aliases={10: 0},
    )
    received = swapped(send, "tm", 1)
    cond_step = Reduction([([keep[:1]], [received[:1]]), ([keep[1:]], [received[1:]])])

    for bit in reversed(bits_of("fsdp")):
        away, pair = parted(pair, "fsdp", bit, 0)
        pair = pair + swapped(away, "fsdp", bit).astype(f32)
    pair = rounded(pair).astype(bf16)
    pair_other = swapped(pair, "tm", 1)
    clear = bit_of("tm", 1) == 0
    grad_key = jnp.where(clear, pair, pair_other).astype(f32)
    grad_value = jnp.where(clear, pair_other, pair).astype(f32)

    packs = small[None]
    for bit in bits_of("fsdp"):
        packs = jnp.concatenate([packs, swapped(packs, "fsdp", bit)], axis=0)
    grad_queries, grad_query, grad_out, grad_film = call(
        small_grad_kernel,
        (1,),
        [scalars(place), whole(packs), whole(full_queries), whole(full_query)],
        [
            new((shard_queries, width)),
            new((shard_rows, width)),
            new((shard_rows, width)),
            new((shard_rows, wide)),
        ],
        "small_grads",
        product / 10,
        scratch=[pltpu.VMEM((width, wide), f32), pltpu.VMEM((QUERIES, width), f32)],
    )

    conv_proj = conv_proj.finish()
    cond_step = cond_step.finish()
    return (
        res_out[:, None],
        skip_out[:, None],
        grad_frames[:, None],
        grad_prompt[:, None],
        grad_queries,
        joined(cond_step, 1),
        joined(cond_step, 0),
        joined(conv_proj, slice(0, 3)),
        grad_query,
        grad_key,
        grad_value,
        grad_out,
        grad_film,
        joined(conv_proj, 3),
    )


def solution(mesh):
    packed = P(None, "fsdp", "tm", None)
    short = P(None, "fsdp", None)
    weight = P("fsdp", None)
    taps = P(None, "fsdp", None)
    in_specs = (packed, packed, short, short, packed) + (weight,) * 3 + (taps,) + (weight,) * 6 + (packed,) * 2
    out_specs = (packed,) * 4 + (weight,) * 3 + (taps,) + (weight,) * 6
    return jax.shard_map(
        per_device, mesh=mesh, in_specs=in_specs, out_specs=out_specs, check_vma=False
    )
```

time: 832 us -> 294 us (0.35)
  blocking collectives: 255 us -> 0 us
  waiting for transfers between devices: 306 us -> 87.4 us
  matrix products: 135 us -> 0 us
  Pallas kernels: 0 us -> 134 us
  other arithmetic: 69.2 us -> 16.4 us
  starting transfers between devices: 18.7 us -> 45.6 us
  local copies, waits for them, and re-layouts: 27.7 us -> 8.25 us
  between operations: 15.6 us -> 1.49 us
    psum x1 -> x0, waiting for transfers between devices: 176 us -> none  [per_device(): lax.psum((shares[0], shares[1], shares[2], shares[3], shares[4], shares[5...]
    dot_general x61 -> x0, matrix products: 135 us -> none  [the longest x16 41.8 us: contract_rows(): lax.dot_general(left, right, (((0,), (0,)), ((), ())), precision=precisio...]
    pallas_call x0 -> x16, Pallas kernels: none -> 134 us  [call(): pl.pallas_call(body, grid=grid, in_specs=[spec for _, spec in ins] + [ANY...]
    all_gather x9 -> x0, blocking collectives: 131 us -> none  [the longest x4 76.7 us: joined_2(): gathered = jax.tree.map(lambda a: lax.all_gather(a, axis), part)]
    reduce_scatter x10 -> x0, waiting for transfers between devices: 129 us -> none  [the longest x1 79.8 us: per_device(): lax.psum_scatter(acc_conv_taps, 'fsdp', scatter_dimension=1, tiled=True)]
    psum x3 -> x0, blocking collectives: 125 us -> none  [the longest x1 61.7 us: per_device(): context = lax.psum(context_part, 'tm')]
    ppermute x8 -> x49, waiting for transfers between devices: 0.02 us -> 87.4 us  [the longest x47 87.4 us: swapped(): return lax.ppermute(array, axis, [(i, i ^ bit) for i in range(count)])]
    another operation x12 -> x3, other arithmetic: 36.2 us -> 0.4 us  [the longest x2 19.9 us: per_device(): jnp.stack([cot_extended[(2 - tap) * DILATION:(2 - tap) * DILATION + frame...]
  transfers between devices with their start and end apart: 24 -> 49, of which waited for: 4 -> 17; matrix products, arithmetic and copies ran while one was open for 24% -> 5% of each run, Pallas kernels for 0% -> 29%
where the time goes in v1:
time: 294 us; the launch traced here: 293 us
  Pallas kernels  134 us (46%)
  waiting for transfers between devices  87.4 us (30%)
  starting transfers between devices  45.6 us (16%)
  other arithmetic  16.4 us (6%)
  local copies, waits for them, and re-layouts  8.25 us (3%)
    pallas_call x16, Pallas kernels, call(): pl.pallas_call(body, grid=grid, in_specs=[spec for _, spec in ins] + [ANY...  134 us
    ppermute x47, waiting for transfers between devices, swapped(): return lax.ppermute(array, axis, [(i, i ^ bit) for i in range(count)])  87.4 us
    ppermute x47, starting transfers between devices, swapped(): return lax.ppermute(array, axis, [(i, i ^ bit) for i in range(count)])  41.9 us
    unnamed x66, local copies, waits for them, and re-layouts  6.74 us
  transfers between devices with their start and end apart: 49, of which 17 were waited for; matrix products, arithmetic and copies ran while one was open for 5% of the time, Pallas kernels for 29%

profile of v1, /device:TPU:0, one launch (start us, length us, event | category | flops | bytes accessed | tf_op | source)
XLA Modules:
  0.0 293.1 jit_solution(6894058923833886391)
XLA Ops:
  2.5 3.0 %collective-permute-start.2 = (bf16[1,128,1024]{2,1,0:T(8,128)(2,1)S(1)}, bf16[1,128,1024]{2,1,0:T(8,128)(2,1)S(1)}, u32[]{:S(2)}, u32[]{:S(2)}) collective-permute-start(bf16[1,128,1024]{2,1,0:T(8,128)(2,1)S(1)} %bitcast.73), channel_id=1, source_target_pairs={{0,1},{1,0},{2,3},{3,2},{4,5},{5,4},{6,7},{7,6},{8,9},{9,8},{10,11... | collective-permute-start | bytes 786440 | tf_op jit(solution)/shard_map/ppermute | solution.py:637
  8.2 2.4 collective-permute-start
  11.9 2.5 collective-permute-start.3
  15.1 5.2 %masks.1 = (bf16[2,1536,512]{2,1,0:T(8,128)(2,1)}, bf16[2,64,512]{2,1,0:T(8,128)(2,1)}) custom-call(s32[4]{0:T(128)S(1)} %pad_add_fusion.refs_0_, s32[2,30]{1,0:T(2,128)S(1)} %bitcast.76, bf16[4,2,32,512]{3,2,1,0:T(8,128)(2,1)S(1)} %get-tuple-element.65.refs_2_), custom_call_target="tpu_custom_call" | custom-call | flops 100000 | bytes 4096 | tf_op jit(solution)/shard_map/masks/pallas_call | solution.py:66
  23.1 2.2 pack_rest.1
  30.0 2.4 collective-permute-start.10
  35.8 7.1 %collective-permute-done.10.refs_11_.refs_3_ = bf16[4,2,16,512]{3,2,1,0:T(8,128)(2,1)S(1)} collective-permute-done((bf16[4,2,16,512]{3,2,1,0:T(8,128)(2,1)S(1)}, bf16[4,2,16,512]{3,2,1,0:T(8,128)(2,1)S(1)}, u32[]{:S(2)}, u32[]{:S(2)}) %collective-permute-start.10) | collective-permute-done | bytes 131104 | tf_op jit(solution)/shard_map/ppermute | solution.py:637
  42.9 11.1 %film.1 = (bf16[2,1632,512]{2,1,0:T(8,128)(2,1)S(1)}, f32[2,1536,512]{2,1,0:T(8,128)}) custom-call(bf16[2,1536,512]{2,1,0:T(8,128)(2,1)} %bitcast.80, bf16[2,1536,512]{2,1,0:T(8,128)(2,1)} %bitcast.85, bf16[4,2,32,512]{3,2,1,0:T(8,128)(2,1)} %copy-done.4, bf16[4,2,32,512]{3,2,1,0:T(8,128)(2,1)} %copy-done.5, ...), custom_call_target="tpu_custom_call" | custom-call | flops 100000 | bytes 4096 | tf_op jit(solution)/shard_map/film/pallas_call | solution.py:66
  56.1 12.8 %collective-permute-done.14.refs_4_ = bf16[1,256,1024]{2,1,0:T(8,128)(2,1)S(1)} collective-permute-done((bf16[1,256,1024]{2,1,0:T(8,128)(2,1)S(1)}, bf16[1,256,1024]{2,1,0:T(8,128)(2,1)S(1)}, u32[]{:S(2)}, u32[]{:S(2)}) %collective-permute-start.14) | collective-permute-done | bytes 524320 | tf_op jit(solution)/shard_map/ppermute | solution.py:637
  69.5 4.8 %collective-permute-done.18.refs_7_ = bf16[1,192,1024]{2,1,0:T(8,128)(2,1)S(1)} collective-permute-done((bf16[1,192,1024]{2,1,0:T(8,128)(2,1)S(1)}, bf16[1,192,1024]{2,1,0:T(8,128)(2,1)S(1)}, u32[]{:S(2)}, u32[]{:S(2)}) %collective-permute-start.18) | collective-permute-done | bytes 393248 | tf_op jit(solution)/shard_map/ppermute | solution.py:637
  76.8 4.2 %unpack_second.1 = (bf16[512,512]{1,0:T(8,128)(2,1)}, bf16[512,512]{1,0:T(8,128)(2,1)}, bf16[512,512]{1,0:T(8,128)(2,1)}, bf16[512,512]{1,0:T(8,128)(2,1)}, bf16[512,1024]{1,0:T(8,128)(2,1)}) custom-call(s32[4]{0:T(128)S(1)} %pad_add_fusion.refs_0_, f32[256,512]{1,0:T(8,128)} %refs_1_.9, f32[256,512]{1,0:T(8,128)} %refs_2_.9, f32[256,512]{1,0:T(8,128)} %refs_3_.3, ...), custom_call_target="tpu_custom_call" | custom-call | flops 100000 | bytes 4096 | tf_op jit(solution)/shard_map/unpack_second/pallas_call | solution.py:66
  81.0 5.4 %attention.1 = (f32[2,8,1024]{2,1,0:T(8,128)}, bf16[2,256,512]{2,1,0:T(8,128)(2,1)}, f32[2,256,256]{2,1,0:T(8,128)}, bf16[2,256,512]{2,1,0:T(8,128)(2,1)}, bf16[...) custom-call(s32[4]{0:T(128)S(1)} %pad_add_fusion.refs_0_, ...), custom_call_target="tpu_custom_call" | custom-call | flops 100000 | bytes 4096 | tf_op jit(solution)/shard_map/attention/pallas_call | solution.py:66
  87.9 5.4 %unpack_third.1 = (bf16[1536,1024]{1,0:T(8,128)(2,1)S(1)}, bf16[512,1024]{1,0:T(8,128)(2,1)S(1)}, bf16[1536,1024]{1,0:T(8,128)(2,1)}, bf16[512,1024]{1,0:T(8,128)(2,1)}) custom-call(s32[4]{0:T(128)S(1)} %pad_add_fusion.refs_0_, f32[3,256,1024]{2,1,0:T(8,128)} %refs_1_.8, f32[256,1024]{1,0:T(8,128)} %refs_2_.8, bf16[1,256,1024]{2,1,0:T(8,128)(2,1)} %copy-done.17, ...), custom_call_target="tpu_custom_call" | custom-call | flops 100000 | bytes 4096 | tf_op jit(solution)/shard_map/unpack_third/pallas_call | solution.py:66
  93.3 28.5 %conv.1 = (bf16[2,1600,1024]{2,1,0:T(8,128)(2,1)S(1)}, bf16[2,1600,1024]{2,1,0:T(8,128)(2,1)}, bf16[2,1536,512]{2,1,0:T(8,128)(2,1)}, f32[8,1024]{1,0:T(8,128)},...) custom-call(s32[4]{0:T(128)S(1)} %pad_add_fusion.refs_0_, bf16[2,1632,512]{2,1,0:T(8,128)(2,1)S(1)} %get-tuple-element.71.refs_1_, ...), custom_call_target="tpu_custom_call" | custom-call | flops 17716740096 | bytes 4096 | tf_op jit(solution)/shard_map/conv/pallas_call | solution.py:66
  121.8 14.9 %conv_grad.1 = (f32[3,512,512]{2,1,0:T(8,128)}, bf16[3,512,512]{2,1,0:T(8,128)(2,1)}) custom-call(s32[4]{0:T(128)S(1)} %pad_add_fusion.refs_0_, bf16[2,1632,512]{2,1,0:T(8,128)(2,1)S(1)} %get-tuple-element.71.refs_1_, bf16[2,1536,512]{2,1,0:T(8,128)(2,1)} %get-tuple-element.67.refs_4_.refs_8_.refs_2_.refs_1_, ...), custom_call_target="tpu_custom_call" | custom-call | flops 9663676416 | bytes 4096 | tf_op jit(solution)/shard_map/conv_grad/pallas_call | solution.py:66
  137.4 2.6 collective-permute-done.25
  141.7 2.2 collective-permute-done.26
  143.9 3.3 %collective-permute-start.27 = (f32[8,1024]{1,0:T(8,128)S(1)}, f32[8,1024]{1,0:T(8,128)S(1)}, u32[]{:S(2)}, u32[]{:S(2)}) collective-permute-start(f32[8,1024]{1,0:T(8,128)S(1)} %add.161), channel_id=1, source_target_pairs={{0,8},{2,10},{4,12},{6,14},{8,0},{10,2},{12,4},{14,6},{16,24},{18,... | collective-permute-start | bytes 98312 | tf_op jit(solution)/shard_map/ppermute | solution.py:637
  149.0 3.1 %collective-permute-start.28 = (f32[8,1024]{1,0:T(8,128)S(1)}, f32[8,1024]{1,0:T(8,128)S(1)}, u32[]{:S(2)}, u32[]{:S(2)}) collective-permute-start(f32[8,1024]{1,0:T(8,128)S(1)} %add.162), channel_id=1, source_target_pairs={{0,16},{2,18},{4,20},{6,22},{8,24},{10,26},{12,28},{14,30},{16,0},... | collective-permute-start | bytes 98312 | tf_op jit(solution)/shard_map/ppermute | solution.py:637
  153.5 9.7 %outputs.1 = (bf16[2,1536,512]{2,1,0:T(8,128)(2,1)}, bf16[2,1536,512]{2,1,0:T(8,128)(2,1)}) custom-call(bf16[2,1536,512]{2,1,0:T(8,128)(2,1)} %get-tuple-element.84.refs_0_, bf16[2,1536,512]{2,1,0:T(8,128)(2,1)} %bitcast.81, bf16[2,1536,512]{2,1,0:T(8,128)(2,1)} %get-tuple-element.67.refs_4_.refs_8_.refs_2_.refs_1_, ...), custom_call_target="tpu_custom_call" | custom-call | flops 3221225472 | bytes 4096 | tf_op jit(solution)/shard_map/outputs/pallas_call | solution.py:66
  163.9 7.0 %attention_grad.1 = (f32[2,16,512]{2,1,0:T(8,128)}, f32[512,512]{1,0:T(8,128)}, f32[72,512]{1,0:T(8,128)}) custom-call(s32[4]{0:T(128)S(1)} %pad_add_fusion.refs_0_, f32[8,1024]{1,0:T(8,128)} %add.163.refs_1_, bf16[2,256,512]{2,1,0:T(8,128)(2,1)} %get-tuple-element.99.refs_2_, f32[2,256,256]{2,1,0:T(8,128)} %get-tuple-element.100.refs_3_, ...), custom_call_target="tpu_custom_call" | custom-call | flops 1610612736 | bytes 4096 | tf_op jit(solution)/shard_map/attention_grad/pallas_call | solution.py:66
  175.1 15.2 %hidden_grad_first.1 = (f32[2,1536,512]{2,1,0:T(8,128)}, f32[640,1024]{1,0:T(8,128)}) custom-call(bf16[2,1600,1024]{2,1,0:T(8,128)(2,1)} %get-tuple-element.90.refs_0_.refs_1_, bf16[2,1536,512]{2,1,0:T(8,128)(2,1)} %get-tuple-element.67.refs_4_.refs_8_.refs_2_.refs_1_, bf16[2,1536,512]{2,1,0:T(8,128)(2,1)} %bitcast.82, ...), custom_call_target="tpu_custom_call" | custom-call | flops 7247757312 | bytes 4096 | tf_op jit(solution)/shard_map/hidden_grad_first/pallas_call | solution.py:66
  193.1 17.2 %hidden_grad_last.1 = (f32[2,1536,512]{2,1,0:T(8,128)}, f32[2,512,512]{2,1,0:T(8,128)}, bf16[2,512,512]{2,1,0:T(8,128)(2,1)}) custom-call(s32[4]{0:T(128)S(1)} %pad_add_fusion.refs_0_, bf16[2,1600,1024]{2,1,0:T(8,128)(2,1)} %get-tuple-element.90.refs_0_.refs_1_, ...), custom_call_target="tpu_custom_call", output_to_operand_aliasing={{0}: (10, {})} | custom-call | flops 7247757312 | bytes 4096 | tf_op jit(solution)/shard_map/hidden_grad_last/pallas_call | solution.py:66
  211.3 9.0 %collective-permute-done.42 = bf16[4,64,512]{2,1,0:T(8,128)(2,1)} collective-permute-done((bf16[4,64,512]{2,1,0:T(8,128)(2,1)}, bf16[4,64,512]{2,1,0:T(8,128)(2,1)}, u32[]{:S(2)}, u32[]{:S(2)}) %collective-permute-start.42) | collective-permute-done | bytes 262176 | tf_op jit(solution)/shard_map/ppermute | solution.py:637
  225.4 11.4 %collective-permute-done.43 = bf16[4,64,512]{2,1,0:T(8,128)(2,1)} collective-permute-done((bf16[4,64,512]{2,1,0:T(8,128)(2,1)}, bf16[4,64,512]{2,1,0:T(8,128)(2,1)}, u32[]{:S(2)}, u32[]{:S(2)}) %collective-permute-start.43) | collective-permute-done | bytes 262176 | tf_op jit(solution)/shard_map/ppermute | solution.py:637
  241.6 4.6 %collective-permute-done.44 = bf16[4,64,512]{2,1,0:T(8,128)(2,1)S(1)} collective-permute-done((bf16[4,64,512]{2,1,0:T(8,128)(2,1)S(1)}, bf16[4,64,512]{2,1,0:T(8,128)(2,1)S(1)}, u32[]{:S(2)}, u32[]{:S(2)}) %collective-permute-start.44) | collective-permute-done | bytes 262176 | tf_op jit(solution)/shard_map/ppermute | solution.py:637
  250.1 3.0 %collective-permute-done.34 = bf16[1,1,1,128,512]{4,3,0,2,1:T(8,128)(2,1)S(1)} collective-permute-done((bf16[1,1,1,128,512]{4,3,0,2,1:T(8,128)(2,1)S(1)}, bf16[1,1,1,128,512]{4,3,0,2,1:T(8,128)(2,1)S(1)}, u32[]{:S(2)}, u32[]{:S(2)}) %collective-permute-start.34) | collective-permute-done | bytes 131104 | tf_op jit(solution)/shard_map/ppermute | solution.py:637
  253.2 9.0 %collective-permute-done.32 = bf16[1,1,1,128,512]{4,3,0,2,1:T(8,128)(2,1)S(1)} collective-permute-done((bf16[1,1,1,128,512]{4,3,0,2,1:T(8,128)(2,1)S(1)}, bf16[1,1,1,128,512]{4,3,0,2,1:T(8,128)(2,1)S(1)}, u32[]{:S(2)}, u32[]{:S(2)}) %collective-permute-start.32) | collective-permute-done | bytes 131104 | tf_op jit(solution)/shard_map/ppermute | solution.py:637
  264.6 3.4 %small_grads.1 = (f32[16,512]{1,0:T(8,128)}, f32[256,512]{1,0:T(8,128)}, f32[256,512]{1,0:T(8,128)}, f32[256,1024]{1,0:T(8,128)}) custom-call(s32[4]{0:T(128)S(1)} %pad_add_fusion.refs_0_, f32[2,72,512]{2,1,0:T(8,128)} %pad_maximum_fusion.4.refs_1_, bf16[32,512]{1,0:T(8,128)(2,1)} %copy-done.11, bf16[512,512]{1,0:T(8,128)(2,1)} %get-tuple-element.78.refs_6_.refs_3_), custom_call_target="tpu_custom_call" | custom-call | flops 322122560 | bytes 4096 | tf_op jit(solution)/shard_map/small_grads/pallas_call | solution.py:66
  269.1 6.8 %collective-permute-done.36 = bf16[2,64,512]{2,1,0:T(8,128)(2,1)S(1)} collective-permute-done((bf16[2,64,512]{2,1,0:T(8,128)(2,1)S(1)}, bf16[2,64,512]{2,1,0:T(8,128)(2,1)S(1)}, u32[]{:S(2)}, u32[]{:S(2)}) %collective-permute-start.36) | collective-permute-done | bytes 131104 | tf_op jit(solution)/shard_map/ppermute | solution.py:637
  276.2 4.8 %collective-permute-done.37 = bf16[2,64,512]{2,1,0:T(8,128)(2,1)S(1)} collective-permute-done((bf16[2,64,512]{2,1,0:T(8,128)(2,1)S(1)}, bf16[2,64,512]{2,1,0:T(8,128)(2,1)S(1)}, u32[]{:S(2)}, u32[]{:S(2)}) %collective-permute-start.37) | collective-permute-done | bytes 131104 | tf_op jit(solution)/shard_map/ppermute | solution.py:637
  282.8 4.6 %collective-permute-done.38 = bf16[2,128,512]{2,1,0:T(8,128)(2,1)S(1)} collective-permute-done((bf16[2,128,512]{2,1,0:T(8,128)(2,1)S(1)}, bf16[2,128,512]{2,1,0:T(8,128)(2,1)S(1)}, u32[]{:S(2)}, u32[]{:S(2)}) %collective-permute-start.38) | collective-permute-done | bytes 262176 | tf_op jit(solution)/shard_map/ppermute | solution.py:637
  (207 shorter events, 63.1 us)
Async XLA Ops:
  2.5 9.4 %collective-permute-start.2 = (bf16[1,128,1024]{2,1,0:T(8,128)(2,1)S(1)}, bf16[1,128,1024]{2,1,0:T(8,128)(2,1)S(1)}, u32[]{:S(2)}, u32[]{:S(2)}) collective-permute-start(bf16[1,128,1024]{2,1,0:T(8,128)(2,1)S(1)} %bitcast.73), channel_id=1, source_target_pairs={{0,1},{1,0},{2,3},{3,2},{4,5},{5,4},{6,7},{7,6},{8,9},{9,8},{10,11... | collective-permute-start | bytes 786440 | tf_op jit(solution)/shard_map/ppermute | solution.py:637
  5.5 8.9 %collective-permute-start.7 = (bf16[2,16,512]{2,1,0:T(8,128)(2,1)S(1)}, bf16[2,16,512]{2,1,0:T(8,128)(2,1)S(1)}, u32[]{:S(2)}, u32[]{:S(2)}) collective-permute-start(bf16[2,16,512]{2,1,0:T(8,128)(2,1)S(1)} %bitcast.105), channel_id=1, source_target_pairs={{0,4},{2,6},{4,0},{6,2},{8,12},{10,14},{12,8},{14,10},{16,20},{18,... | collective-permute-start | bytes 98312 | tf_op jit(solution)/shard_map/ppermute | solution.py:637
  7.0 13.3 %collective-permute-start.6 = (bf16[2,16,512]{2,1,0:T(8,128)(2,1)S(1)}, bf16[2,16,512]{2,1,0:T(8,128)(2,1)S(1)}, u32[]{:S(2)}, u32[]{:S(2)}) collective-permute-start(bf16[2,16,512]{2,1,0:T(8,128)(2,1)S(1)} %bitcast.106), channel_id=1, source_target_pairs={{0,2},{2,0},{4,6},{6,4},{8,10},{10,8},{12,14},{14,12},{16,18},{18,... | collective-permute-start | bytes 98312 | tf_op jit(solution)/shard_map/ppermute | solution.py:637
  8.2 12.8 %collective-permute-start = (bf16[4,2,32,512]{3,2,1,0:T(8,128)(2,1)S(1)}, bf16[4,2,32,512]{3,2,1,0:T(8,128)(2,1)S(1)}, u32[]{:S(2)}, u32[]{:S(2)}) collective-permute-start(bf16[4,2,32,512]{3,2,1,0:T(8,128)(2,1)S(1)} %get-tuple-element.65.refs_2_), channel_id=1, source_target_pairs={{0,2},{2,4},{4,6},{6,8},{8,10},{10,12},{12,14},{14,16},{16,18},{18... | collective-permute-start | bytes 786440 | tf_op jit(solution)/shard_map/ppermute | solution.py:809
  10.6 10.4 %collective-permute-start.1 = (bf16[4,2,32,512]{3,2,1,0:T(8,128)(2,1)S(1)}, bf16[4,2,32,512]{3,2,1,0:T(8,128)(2,1)S(1)}, u32[]{:S(2)}, u32[]{:S(2)}) collective-permute-start(bf16[4,2,32,512]{3,2,1,0:T(8,128)(2,1)S(1)} %get-tuple-element.66), channel_id=1, source_target_pairs={{2,0},{4,2},{6,4},{8,6},{10,8},{12,10},{14,12},{16,14},{18,16},{20... | collective-permute-start | bytes 786440 | tf_op jit(solution)/shard_map/ppermute | solution.py:810
  11.9 15.0 %collective-permute-start.3 = (bf16[1,128,1024]{2,1,0:T(8,128)(2,1)S(1)}, bf16[1,128,1024]{2,1,0:T(8,128)(2,1)S(1)}, u32[]{:S(2)}, u32[]{:S(2)}) collective-permute-start(bf16[1,128,1024]{2,1,0:T(8,128)(2,1)S(1)} %collective-permute-done.2.refs_3_.refs_9_), channel_id=1, source_target_pairs={{0,4},{2,6},{4,0},{6,2},{8,12},{10,14},{12,8},{14,10},{16,20},{18,... | collective-permute-start | bytes 786440 | tf_op jit(solution)/shard_map/ppermute | solution.py:637
  20.3 9.6 %collective-permute-start.12 = (bf16[16,512]{1,0:T(8,128)(2,1)S(1)}, bf16[16,512]{1,0:T(8,128)(2,1)S(1)}, u32[]{:S(2)}, u32[]{:S(2)}) collective-permute-start(bf16[16,512]{1,0:T(8,128)(2,1)S(1)} %convert_element_type.150), channel_id=1, source_target_pairs={{0,1},{1,0},{2,3},{3,2},{4,5},{5,4},{6,7},{7,6},{8,9},{9,8},{10,11... | collective-permute-start | bytes 49160 | tf_op jit(solution)/shard_map/ppermute | solution.py:637
  25.3 28.7 %collective-permute-start.13 = (bf16[1,256,1024]{2,1,0:T(8,128)(2,1)S(1)}, bf16[1,256,1024]{2,1,0:T(8,128)(2,1)S(1)}, u32[]{:S(2)}, u32[]{:S(2)}) collective-permute-start(bf16[1,256,1024]{2,1,0:T(8,128)(2,1)S(1)} %bitcast.77), channel_id=1, source_target_pairs={{0,1},{1,0},{2,3},{3,2},{4,5},{5,4},{6,7},{7,6},{8,9},{9,8},{10,11... | collective-permute-start | bytes 1572872 | tf_op jit(solution)/shard_map/ppermute | solution.py:637
  30.0 12.9 %collective-permute-start.10 = (bf16[4,2,16,512]{3,2,1,0:T(8,128)(2,1)S(1)}, bf16[4,2,16,512]{3,2,1,0:T(8,128)(2,1)S(1)}, u32[]{:S(2)}, u32[]{:S(2)}) collective-permute-start(bf16[4,2,16,512]{3,2,1,0:T(8,128)(2,1)S(1)} %pad_maximum_fusion.6.refs_9_.refs_12_.refs_1_), channel_id=1, source_target_pairs={{0,16},{2,18},{4,20},{6,22},{8,24},{10,26},{12,28},{14,30},{16,0},... | collective-permute-start | bytes 393224 | tf_op jit(solution)/shard_map/ppermute | solution.py:637
  32.4 10.5 %collective-permute-start.11 = (bf16[4,2,16,512]{3,2,1,0:T(8,128)(2,1)S(1)}, bf16[4,2,16,512]{3,2,1,0:T(8,128)(2,1)S(1)}, u32[]{:S(2)}, u32[]{:S(2)}) collective-permute-start(bf16[4,2,16,512]{3,2,1,0:T(8,128)(2,1)S(1)} %pad_maximum_fusion.6.refs_9_.refs_12_.refs_1_), channel_id=1, source_target_pairs={{0,24},{2,26},{4,28},{6,30},{8,16},{10,18},{12,20},{14,22},{16,8},... | collective-permute-start | bytes 393224 | tf_op jit(solution)/shard_map/ppermute | solution.py:637
  32.8 23.1 %collective-permute-start.17 = (bf16[1,192,1024]{2,1,0:T(8,128)(2,1)S(1)}, bf16[1,192,1024]{2,1,0:T(8,128)(2,1)S(1)}, u32[]{:S(2)}, u32[]{:S(2)}) collective-permute-start(bf16[1,192,1024]{2,1,0:T(8,128)(2,1)S(1)} %bitcast.78), channel_id=1, source_target_pairs={{0,1},{1,0},{2,3},{3,2},{4,5},{5,4},{6,7},{7,6},{8,9},{9,8},{10,11... | collective-permute-start | bytes 1179656 | tf_op jit(solution)/shard_map/ppermute | solution.py:637
  54.0 14.9 %collective-permute-start.14 = (bf16[1,256,1024]{2,1,0:T(8,128)(2,1)S(1)}, bf16[1,256,1024]{2,1,0:T(8,128)(2,1)S(1)}, u32[]{:S(2)}, u32[]{:S(2)}) collective-permute-start(bf16[1,256,1024]{2,1,0:T(8,128)(2,1)S(1)} %collective-permute-done.13.refs_3_), channel_id=1, source_target_pairs={{0,4},{2,6},{4,0},{6,2},{8,12},{10,14},{12,8},{14,10},{16,20},{18,... | collective-permute-start | bytes 1572872 | tf_op jit(solution)/shard_map/ppermute | solution.py:637
  55.9 18.4 %collective-permute-start.18 = (bf16[1,192,1024]{2,1,0:T(8,128)(2,1)S(1)}, bf16[1,192,1024]{2,1,0:T(8,128)(2,1)S(1)}, u32[]{:S(2)}, u32[]{:S(2)}) collective-permute-start(bf16[1,192,1024]{2,1,0:T(8,128)(2,1)S(1)} %collective-permute-done.17.refs_6_), channel_id=1, source_target_pairs={{0,4},{2,6},{4,0},{6,2},{8,12},{10,14},{12,8},{14,10},{16,20},{18,... | collective-permute-start | bytes 1179656 | tf_op jit(solution)/shard_map/ppermute | solution.py:637
  56.1 30.2 %collective-permute-start.15 = (bf16[1,256,1024]{2,1,0:T(8,128)(2,1)S(1)}, bf16[1,256,1024]{2,1,0:T(8,128)(2,1)S(1)}, u32[]{:S(2)}, u32[]{:S(2)}) collective-permute-start(bf16[1,256,1024]{2,1,0:T(8,128)(2,1)S(1)} %collective-permute-done.13.refs_3_), channel_id=1, source_target_pairs={{0,2},{2,0},{4,6},{6,4},{8,10},{10,8},{12,14},{14,12},{16,18},{18,... | collective-permute-start | bytes 1572872 | tf_op jit(solution)/shard_map/ppermute | solution.py:637
  69.0 17.4 %collective-permute-start.16 = (bf16[1,256,1024]{2,1,0:T(8,128)(2,1)S(1)}, bf16[1,256,1024]{2,1,0:T(8,128)(2,1)S(1)}, u32[]{:S(2)}, u32[]{:S(2)}) collective-permute-start(bf16[1,256,1024]{2,1,0:T(8,128)(2,1)S(1)} %collective-permute-done.14.refs_4_), channel_id=1, source_target_pairs={{0,2},{2,0},{4,6},{6,4},{8,10},{10,8},{12,14},{14,12},{16,18},{18,... | collective-permute-start | bytes 1572872 | tf_op jit(solution)/shard_map/ppermute | solution.py:637
  136.7 34.4 %collective-permute-start.21 = (bf16[3,512,512]{2,1,0:T(8,128)(2,1)}, bf16[3,512,512]{2,1,0:T(8,128)(2,1)S(1)}, u32[]{:S(2)}, u32[]{:S(2)}) collective-permute-start(bf16[3,512,512]{2,1,0:T(8,128)(2,1)} %get-tuple-element.87.refs_4_), channel_id=1, source_target_pairs={{0,2},{2,0},{4,6},{6,4},{8,10},{10,8},{12,14},{14,12},{16,18},{18,... | collective-permute-start | bytes 4718600 | tf_op jit(solution)/shard_map/ppermute | solution.py:637
  137.2 33.7 %collective-permute-start.22 = (bf16[1,512,512]{2,1,0:T(8,128)(2,1)S(1)}, bf16[1,512,512]{2,1,0:T(8,128)(2,1)S(1)}, u32[]{:S(2)}, u32[]{:S(2)}) collective-permute-start(bf16[1,512,512]{2,1,0:T(8,128)(2,1)S(1)} %copy-done.32), channel_id=1, source_target_pairs={{0,2},{2,0},{4,6},{6,4},{8,10},{10,8},{12,14},{14,12},{16,18},{18,... | collective-permute-start | bytes 1572872 | tf_op jit(solution)/shard_map/ppermute | solution.py:637
  149.0 14.2 %collective-permute-start.28 = (f32[8,1024]{1,0:T(8,128)S(1)}, f32[8,1024]{1,0:T(8,128)S(1)}, u32[]{:S(2)}, u32[]{:S(2)}) collective-permute-start(f32[8,1024]{1,0:T(8,128)S(1)} %add.162), channel_id=1, source_target_pairs={{0,16},{2,18},{4,20},{6,22},{8,24},{10,26},{12,28},{14,30},{16,0},... | collective-permute-start | bytes 98312 | tf_op jit(solution)/shard_map/ppermute | solution.py:637
  171.5 18.8 %collective-permute-start.23 = (bf16[2,1,2,128,512]{4,3,2,1,0:T(8,128)(2,1)S(1)}, bf16[2,1,2,128,512]{4,3,2,1,0:T(8,128)(2,1)S(1)}, u32[]{:S(2)}, u32[]{:S(2)}) collective-permute-start(bf16[2,1,2,128,512]{4,3,2,1,0:T(8,128)(2,1)S(1)} %dynamic-slice_convert_fusion.1.refs_7_), channel_id=1, source_target_pairs={{0,1},{1,0},{2,3},{3,2},{4,5},{5,4},{6,7},{7,6},{8,9},{9,8},{10,11... | collective-permute-start | bytes 1572872 | tf_op jit(solution)/shard_map/ppermute | solution.py:637
  173.5 17.0 %collective-permute-start.24 = (bf16[2,2,1,128,512]{4,3,2,1,0:T(8,128)(2,1)S(1)}, bf16[2,2,1,128,512]{4,3,2,1,0:T(8,128)(2,1)S(1)}, u32[]{:S(2)}, u32[]{:S(2)}) collective-permute-start(bf16[2,2,1,128,512]{4,3,2,1,0:T(8,128)(2,1)S(1)} %dynamic-slice_convert_fusion.refs_8_), channel_id=1, source_target_pairs={{0,4},{2,6},{4,0},{6,2},{8,12},{10,14},{12,8},{14,10},{16,20},{18,... | collective-permute-start | bytes 1572872 | tf_op jit(solution)/shard_map/ppermute | solution.py:637
  190.8 19.6 %collective-permute-start.41 = (bf16[2,1,1,128,512]{4,3,2,1,0:T(8,128)(2,1)S(1)}, bf16[2,1,1,128,512]{4,3,2,1,0:T(8,128)(2,1)S(1)}, u32[]{:S(2)}, u32[]{:S(2)}) collective-permute-start(bf16[2,1,1,128,512]{4,3,2,1,0:T(8,128)(2,1)S(1)} %dynamic-slice_convert_fusion.5.refs_12_), channel_id=1, source_target_pairs={{0,1},{1,0},{2,3},{3,2},{4,5},{5,4},{6,7},{7,6},{8,9},{9,8},{10,11... | collective-permute-start | bytes 786440 | tf_op jit(solution)/shard_map/ppermute | solution.py:637
  191.8 18.7 %collective-permute-start.40 = (bf16[2,1,1,128,512]{4,3,2,1,0:T(8,128)(2,1)S(1)}, bf16[2,1,1,128,512]{4,3,2,1,0:T(8,128)(2,1)S(1)}, u32[]{:S(2)}, u32[]{:S(2)}) collective-permute-start(bf16[2,1,1,128,512]{4,3,2,1,0:T(8,128)(2,1)S(1)} %dynamic-slice_convert_fusion.6.refs_11_), channel_id=1, source_target_pairs={{0,4},{2,6},{4,0},{6,2},{8,12},{10,14},{12,8},{14,10},{16,20},{18,... | collective-permute-start | bytes 786440 | tf_op jit(solution)/shard_map/ppermute | solution.py:637
  210.3 27.7 %collective-permute-start.30 = (bf16[2,512,512]{2,1,0:T(8,128)(2,1)}, bf16[2,512,512]{2,1,0:T(8,128)(2,1)}, u32[]{:S(2)}, u32[]{:S(2)}) collective-permute-start(bf16[2,512,512]{2,1,0:T(8,128)(2,1)} %get-tuple-element.111), channel_id=1, source_target_pairs={{0,2},{2,0},{4,6},{6,4},{8,10},{10,8},{12,14},{14,12},{16,18},{18,... | collective-permute-start | bytes 3145736 | tf_op jit(solution)/shard_map/ppermute | solution.py:637
  211.3 9.0 %collective-permute-start.42 = (bf16[4,64,512]{2,1,0:T(8,128)(2,1)}, bf16[4,64,512]{2,1,0:T(8,128)(2,1)}, u32[]{:S(2)}, u32[]{:S(2)}) collective-permute-start(bf16[4,64,512]{2,1,0:T(8,128)(2,1)} %fusion.7), channel_id=1, source_target_pairs={{0,8},{2,10},{4,12},{6,14},{8,0},{10,2},{12,4},{14,6},{16,24},{18,... | collective-permute-start | bytes 786440 | tf_op jit(solution)/shard_map/ppermute | solution.py:637
  222.1 14.7 %collective-permute-start.43 = (bf16[4,64,512]{2,1,0:T(8,128)(2,1)}, bf16[4,64,512]{2,1,0:T(8,128)(2,1)}, u32[]{:S(2)}, u32[]{:S(2)}) collective-permute-start(bf16[4,64,512]{2,1,0:T(8,128)(2,1)} %fusion.21), channel_id=1, source_target_pairs={{0,16},{2,18},{4,20},{6,22},{8,24},{10,26},{12,28},{14,30},{16,0},... | collective-permute-start | bytes 786440 | tf_op jit(solution)/shard_map/ppermute | solution.py:637
  222.2 41.7 %collective-permute-start.29 = (f32[1,72,512]{2,1,0:T(8,128)S(1)}, f32[1,72,512]{2,1,0:T(8,128)S(1)}, u32[]{:S(2)}, u32[]{:S(2)}) collective-permute-start(f32[1,72,512]{2,1,0:T(8,128)S(1)} %bitcast.74), channel_id=1, source_target_pairs={{0,1},{1,0},{2,3},{3,2},{4,5},{5,4},{6,7},{7,6},{8,9},{9,8},{10,11... | collective-permute-start | bytes 442376 | tf_op jit(solution)/shard_map/ppermute | solution.py:637
  223.8 52.2 %collective-permute-start.47 = (bf16[256,512]{1,0:T(8,128)(2,1)S(1)}, bf16[256,512]{1,0:T(8,128)(2,1)S(1)}, u32[]{:S(2)}, u32[]{:S(2)}) collective-permute-start(bf16[256,512]{1,0:T(8,128)(2,1)S(1)} %dynamic-slice_convert_fusion.2), channel_id=1, source_target_pairs={{0,1},{1,0},{2,3},{3,2},{4,5},{5,4},{6,7},{7,6},{8,9},{9,8},{10,11... | collective-permute-start | bytes 786440 | tf_op jit(solution)/shard_map/ppermute | solution.py:637
  237.9 8.3 %collective-permute-start.44 = (bf16[4,64,512]{2,1,0:T(8,128)(2,1)S(1)}, bf16[4,64,512]{2,1,0:T(8,128)(2,1)S(1)}, u32[]{:S(2)}, u32[]{:S(2)}) collective-permute-start(bf16[4,64,512]{2,1,0:T(8,128)(2,1)S(1)} %reduce-precision_convert_fusion.1), channel_id=1, source_target_pairs={{0,8},{2,10},{4,12},{6,14},{8,0},{10,2},{12,4},{14,6},{16,24},{18,... | collective-permute-start | bytes 786440 | tf_op jit(solution)/shard_map/ppermute | solution.py:637
  239.7 8.3 %collective-permute-start.33 = (bf16[1,2,1,128,512]{4,3,0,2,1:T(8,128)(2,1)S(1)}, bf16[1,2,1,128,512]{4,3,0,2,1:T(8,128)(2,1)S(1)}, u32[]{:S(2)}, u32[]{:S(2)}) collective-permute-start(bf16[1,2,1,128,512]{4,3,0,2,1:T(8,128)(2,1)S(1)} %dynamic-slice_convert_fusion.3), channel_id=1, source_target_pairs={{0,4},{2,6},{4,0},{6,2},{8,12},{10,14},{12,8},{14,10},{16,20},{18,... | collective-permute-start | bytes 786440 | tf_op jit(solution)/shard_map/ppermute | solution.py:637
  246.3 22.5 %collective-permute-start.45 = (bf16[4,128,512]{2,1,0:T(8,128)(2,1)S(1)}, bf16[4,128,512]{2,1,0:T(8,128)(2,1)S(1)}, u32[]{:S(2)}, u32[]{:S(2)}) collective-permute-start(bf16[4,128,512]{2,1,0:T(8,128)(2,1)S(1)} %pad_maximum_fusion.3), channel_id=1, source_target_pairs={{0,4},{2,6},{4,0},{6,2},{8,12},{10,14},{12,8},{14,10},{16,20},{18,... | collective-permute-start | bytes 1572872 | tf_op jit(solution)/shard_map/ppermute | solution.py:637
  248.8 13.4 %collective-permute-start.32 = (bf16[1,1,1,128,512]{4,3,0,2,1:T(8,128)(2,1)S(1)}, bf16[1,1,1,128,512]{4,3,0,2,1:T(8,128)(2,1)S(1)}, u32[]{:S(2)}, u32[]{:S(2)}) collective-permute-start(bf16[1,1,1,128,512]{4,3,0,2,1:T(8,128)(2,1)S(1)} %dynamic-slice_convert_fusion.8), channel_id=1, source_target_pairs={{0,4},{2,6},{4,0},{6,2},{8,12},{10,14},{12,8},{14,10},{16,20},{18,... | collective-permute-start | bytes 393224 | tf_op jit(solution)/shard_map/ppermute | solution.py:637
  269.1 18.6 %collective-permute-start.46 = (bf16[4,256,512]{2,1,0:T(8,128)(2,1)S(1)}, bf16[4,256,512]{2,1,0:T(8,128)(2,1)S(1)}, u32[]{:S(2)}, u32[]{:S(2)}) collective-permute-start(bf16[4,256,512]{2,1,0:T(8,128)(2,1)S(1)} %pad_maximum_fusion.1), channel_id=1, source_target_pairs={{0,2},{2,0},{4,6},{6,4},{8,10},{10,8},{12,14},{14,12},{16,18},{18,... | collective-permute-start | bytes 3145736 | tf_op jit(solution)/shard_map/ppermute | solution.py:637
  (50 other events, 393.8 us)

commit v2 on v1

--- a/solution.py
+++ b/solution.py
@@ -57,7 +57,7 @@
     return array, SSPEC
 
 
-def call(kernel, grid, ins, outs, name, flops, scratch=(), after=(), aliases=None):
+def call(kernel, grid, ins, outs, name, micros, scratch=(), after=(), aliases=None):
     count, waits = len(ins), len(after)
 
     def body(*refs):
@@ -72,7 +72,7 @@
         scratch_shapes=scratch,
         input_output_aliases=aliases or {},
         cost_estimate=pl.CostEstimate(
-            flops=int(flops), bytes_accessed=2**12, transcendentals=0
+            flops=int(micros * 1e9), bytes_accessed=2**12, transcendentals=0
         ),
         compiler_params=pltpu.CompilerParams(vmem_limit_bytes=VMEM_LIMIT),
         name=name,
@@ -107,24 +107,23 @@
 
 
 def pack_kernel(layouts, place, *refs):
-    count = sum(map(len, layouts))
+    count = sum(len(layout) - 1 for layout in layouts)
     weights, refs = list(refs[:count]), refs[count:]
     outs, helds, sems = refs[: len(layouts)], refs[len(layouts) : -1], refs[-1]
     copies = []
-    for layout, held in zip(layouts, helds, strict=True):
-        for row, column in layout:
+    for (which, *layout), held in zip(layouts, helds, strict=True):
+        for row, column, *tap in layout:
             weight = weights.pop(0)
-            views = [weight] if len(weight.shape) == 2 else [weight.at[t] for t in range(weight.shape[0])]
-            rows = views[0].shape[0] // 4
-            start = pl.multiple_of(place[3] * rows, rows)
-            for t, view in enumerate(views):
-                copies.append(
-                    pltpu.make_async_copy(
-                        view.at[pl.ds(start, rows)],
-                        held.at[pl.ds(row + t * rows, rows), pl.ds(column, view.shape[1])],
-                        sems.at[len(copies)],
-                    )
+            view = weight.at[tap[0]] if tap else weight
+            rows = view.shape[0] // 4
+            start = pl.multiple_of(place[which] * rows, rows)
+            copies.append(
+                pltpu.make_async_copy(
+                    view.at[pl.ds(start, rows)],
+                    held.at[pl.ds(row, rows), pl.ds(column, view.shape[1])],
+                    sems.at[len(copies)],
                 )
+            )
     for copy in copies:
         copy.start()
     for copy in copies:
@@ -150,32 +149,31 @@
         copy.wait()
 
 
-def unpack_kernel(layout, members, place, *refs):
-    count = len(layout)
-    shards, (here, over, core, both) = refs[:count], refs[count : count + 4]
-    fulls, copies = refs[count + 4 : 2 * count + 4], refs[2 * count + 4 :]
-    member, quarter = place[2], place[3]
-    sources = ((here, quarter), (over, quarter ^ 1), (core, quarter ^ 2), (both, quarter ^ 3))
+def own_kernel(*refs):
+    count = len(refs) // 2
+    for shard, low in zip(refs[:count], refs[count:], strict=True):
+        low[...] = shard[...].astype(bf16)
+
+
+def assemble(place, members, layout, shards, sources, fulls):
+    member = place[2]
     for shard, full, (row, column) in zip(shards, fulls, layout, strict=True):
-        rows, width = shard.shape[-2:]
+        rows, width = shard.shape
         part = rows // 4
-        taps = 1 if len(shard.shape) == 2 else shard.shape[0]
-        for t in range(taps):
-            own = shard[...] if taps == 1 else shard[t]
-            top = t * members * rows
-            full[pl.ds(pl.multiple_of(top + member * rows, part), rows)] = own.astype(bf16)
-            at = row + t * part
-            for j in range(1, members):
-                for source, q in sources:
-                    start = pl.multiple_of(top + (member ^ j) * rows + q * part, part)
-                    full[pl.ds(start, part)] = source[j - 1, at : at + part, column : column + width]
-    for full, copy in zip(fulls, copies, strict=False):
-        copy[...] = full[...]
-
-
-def masks_kernel(rows, slot, total, place, lengths, masks, ends):
+        full[pl.ds(pl.multiple_of(member * rows, part), rows)] = shard[...]
+        for j in range(1, members):
+            for source, quarter in sources:
+                start = pl.multiple_of((member ^ j) * rows + quarter * part, part)
+                full[pl.ds(start, part)] = source[j - 1, row : row + part, column : column + width]
+
+
+def quarters_of(place, arrays, which=3):
+    return [(array, place[which] ^ k) for k, array in enumerate(arrays)]
+
+
+def masks_kernel(rows, slot, total, place, lengths, masks, hot, ends, hot_ends):
     micro, utters = lengths.shape
-    hots = masks.shape[2] - 3 * 128
+    hots = hot.shape[2]
     lane = lax.broadcasted_iota(jnp.int32, (1, hots), 1)
     lane = jnp.where(lane >= micro * slot, lane - micro * slot, lane)
     row = lax.broadcasted_iota(jnp.int32, (hots, 128), 0)
@@ -205,21 +203,23 @@
             low = dotf(here * one_hot(-DILATION), count).astype(bf16)
             high = dotf(here * one_hot(DILATION), count).astype(bf16)
             alive = (position[:, :128] < alive_until) & (position[:, :128] >= 0)
-            return jnp.concatenate(
-                [low, high, jnp.where(alive, 1.0, 0.0).astype(bf16), here], axis=1
-            )
-
-        ends[i, 0:HALO] = rows_of(first, HALO)
-        ends[i, HALO:] = rows_of(first + HALO + rows, HALO)
+            alive = jnp.where(alive, 1.0, 0.0).astype(bf16)
+            return jnp.concatenate([low, high, alive], axis=1), here
+
+        ends[i, 0:HALO], hot_ends[i, 0:HALO] = rows_of(first, HALO)
+        ends[i, HALO:], hot_ends[i, HALO:] = rows_of(first + HALO + rows, HALO)
 
         @pl.loop(0, rows // chunk)
         def _(k, i=i, rows_of=rows_of):
             at = pl.multiple_of(k * chunk, chunk)
-            masks[i, pl.ds(at, chunk)] = rows_of(first + HALO + at, chunk)
+            some, here = rows_of(first + HALO + at, chunk)
+            masks[i, pl.ds(at, chunk)] = some
+            hot[i, pl.ds(at, chunk)] = here
 
 
 def film_kernel(
-    tile, frames, cond, low, high, masks, ends, embed, w_step, w_cond, hidden, gain, film_rows
+    tile, members, layout, place, frames, cond, low, high, hots, hot_ends, embed, own_cond, own_step, here, over, core, both,
+    hidden, gain_cond, gain_step, w_cond, w_step, film_rows,
 ):
     i, j = pl.program_id(0), pl.program_id(1)
     width = frames.shape[2]
@@ -227,20 +227,23 @@
 
     @pl.when((i == 0) & (j == 0))
     def _():
+        sources = quarters_of(place, (here, over, core, both))
+        assemble(place, members, layout, (own_cond, own_step), sources, (w_cond, w_step))
         step_film = dotf(embed[...], w_step[...])
         film_rows[...] = jnp.concatenate(split_rows(step_film, 2), axis=0)
+        gain_cond[...] = w_cond[:, :width]
+        gain_step[...] = film_rows[:, :width]
 
     def film(frame_rows, cond_rows, hot):
         both = dotf(cond_rows, w_cond[...]) + dotf(hot, film_rows[...])
-        gain_rows = both[:, :width]
-        return (frame_rows.astype(f32) * (1.0 + gain_rows) + both[:, width:]).astype(bf16), gain_rows
+        return (frame_rows.astype(f32) * (1.0 + both[:, :width]) + both[:, width:]).astype(bf16)
 
     @pl.when(j == 0)
     def _():
-        edge, _ = film(
+        edge = film(
             jnp.concatenate([low[0, i], high[0, i]], axis=0),
             jnp.concatenate([low[1, i], high[1, i]], axis=0),
-            ends[i, :, 384:],
+            hot_ends[i],
         )
         nothing = jnp.zeros((DILATION, width), bf16)
         hidden[i, 0:DILATION] = nothing
@@ -249,9 +252,7 @@
         hidden[i, DILATION + 2 * HALO + rows :] = nothing
 
     base = pl.multiple_of(j * tile, tile)
-    own, gain_rows = film(frames[0], cond[0], masks[0, :, 384:])
-    hidden[i, pl.ds(DILATION + HALO + base, tile)] = own
-    gain[0] = gain_rows
+    hidden[i, pl.ds(DILATION + HALO + base, tile)] = film(frames[0], cond[0], hots[0])
 
 
 def halves_of(core, width):
@@ -261,17 +262,31 @@
 
 
 def conv_kernel(
-    tile, place, hidden, masks, mask_ends, res, skip, low, high, w_conv, w_proj, film,
-    d_conv, d_conv_copy, gated, sums, keep, send, proj_total, columns, sems,
+    tile, members, layout, place, hidden, masks, mask_ends, frames, res, skip, low, high, film, own_conv, own_proj,
+    here, over, core, both,
+    d_conv, d_conv_copy, conv_copy, sums, keep, send, res_out, skip_out,
+    w_conv, w_proj, proj_total, columns, sems,
 ):
     i, j = pl.program_id(0), pl.program_id(1)
     width = res.shape[2]
     rows = d_conv.shape[1] - 2 * HALO
     gain, shift = 1.0 + film[i, 0:1, :width], film[i, 0:1, width:]
-
-    def body(before, here, after, keep_low, keep_high, alive, res_rows, skip_rows):
+    first = (i == 0) & (j == 0)
+    weights_away = pltpu.make_async_copy(w_conv, conv_copy, sems.at[2])
+
+    @pl.when(first)
+    def _():
+        shard = own_proj.shape[0]
+        own = [own_conv.at[pl.ds(t * shard, shard)] for t in range(3)]
+        full = [w_conv.at[pl.ds(t * width, width)] for t in range(3)]
+        sources = quarters_of(place, (here, over, core, both), 4)
+        assemble(place, members, layout, [*own, own_proj], sources, [*full, w_proj])
+        weights_away.start()
+        sums[...] = jnp.zeros(sums.shape, f32)
+
+    def body(before, now, later, keep_low, keep_high, alive, res_rows, skip_rows):
         taps = jnp.concatenate(
-            [before * lanes(keep_low, width), here, after * lanes(keep_high, width)], axis=1
+            [before * lanes(keep_low, width), now, later * lanes(keep_high, width)], axis=1
         )
         conv = dotf(taps, w_conv[...])
         th = jnp.tanh(conv[:, :width])
@@ -289,7 +304,7 @@
         d_act = d_gated * gain
         left = (d_act * sg * (1.0 - th * th)).astype(bf16)
         right = (d_act * act * (1.0 - sg)).astype(bf16)
-        return act, d_gated, branch, left, right
+        return act, d_gated, branch, alive, left, right
 
     @pl.when(j == 0)
     def _():
@@ -298,7 +313,7 @@
                 [ref[i, at : at + HALO], ref[i, at + HALO + rows : at + 2 * HALO + rows]], axis=0
             )
 
-        _, _, _, left, right = body(
+        *_, left, right = body(
             ends(hidden, 0),
             ends(hidden, DILATION),
             ends(hidden, 2 * DILATION),
@@ -314,16 +329,12 @@
         d_conv[i, HALO + rows :, width:] = right[HALO:]
         columns[...] = jnp.zeros(columns.shape, f32)
 
-    @pl.when((i == 0) & (j == 0))
-    def _():
-        sums[...] = jnp.zeros(sums.shape, f32)
-
     base = pl.multiple_of(j * tile, tile)
 
     def at(ref, offset):
         return ref[i, pl.ds(base + offset, tile)]
 
-    act, d_gated, branch, left, right = body(
+    act, d_gated, branch, alive, left, right = body(
         at(hidden, HALO),
         at(hidden, HALO + DILATION),
         at(hidden, HALO + 2 * DILATION),
@@ -336,11 +347,12 @@
     d_conv[i, pl.ds(base + HALO, tile), :width] = left
     d_conv[i, pl.ds(base + HALO, tile), width:] = right
     gated_rows = (act * gain + shift).astype(bf16)
-    gated[0] = gated_rows
     columns[:, :width] += jnp.sum((d_gated * act).reshape(tile // 8, 8, width), axis=0)
     columns[:, width:] += jnp.sum(d_gated.reshape(tile // 8, 8, width), axis=0)
     part = dotf(gated_rows, branch, TN)
-    first = (i == 0) & (j == 0)
+    out = dotf(gated_rows, w_proj[...])
+    res_out[0] = ((frames[0].astype(f32) + out[:, :width]) * (SQRT_HALF * alive)).astype(bf16)
+    skip_out[0] = (out[:, width:] * alive).astype(bf16)
 
     @pl.when(first)
     def _():
@@ -357,13 +369,6 @@
     for m in range(MICRO):
         pl.when(last & (i == m))(copies[m].start)
 
-    @pl.when(last & (i == MICRO - 1))
-    def _():
-        for copy in copies:
-            copy.wait()
-
-    for m in range(MICRO):
-
         @pl.when(last & (i == m))
         def _(m=m):
             sums[m : m + 1] = jnp.sum(columns[...], axis=0, keepdims=True)
@@ -373,6 +378,8 @@
         mine, other = halves_of(place[0], width)
         send[0] = proj_total[:, pl.ds(other, width)].astype(bf16)
         keep[0] = proj_total[:, pl.ds(mine, width)]
+        for copy in (*copies, weights_away):
+            copy.wait()
 
 
 def conv_grad_kernel(place, hidden, masks, d_conv, keep, send):
@@ -398,76 +405,55 @@
                 ref[tap] = total.astype(ref.dtype)
 
 
-def hidden_grad_rows(tile, i, d_conv, masks, frames, gain, res, cond, w_conv, grad_frames, window, sems):
-    j = pl.program_id(1)
+def hidden_grad_kernel(
+    tile, place, d_conv, masks, hots, frames, res, cond, w_conv, gain_cond, gain_step, embed,
+    grad_frames, keep, send, total, window, sems,
+):
+    i, j = pl.program_id(0), pl.program_id(1)
     steps = pl.num_programs(1)
     width = frames.shape[2]
+    now = i * steps + j
 
     def fetch(step):
-        start = pl.multiple_of(HALO - DILATION + step * tile, DILATION)
+        start = pl.multiple_of(HALO - DILATION + (step % steps) * tile, DILATION)
         return pltpu.make_async_copy(
-            d_conv.at[i, pl.ds(start, tile + 2 * DILATION)], window.at[step % 2], sems.at[step % 2]
+            d_conv.at[step // steps, pl.ds(start, tile + 2 * DILATION)],
+            window.at[step % 2],
+            sems.at[step % 2],
         )
 
-    @pl.when(j == 0)
+    @pl.when(now == 0)
     def _():
         fetch(0).start()
 
-    @pl.when(j + 1 < steps)
+    @pl.when(now + 1 < MICRO * steps)
     def _():
-        fetch(j + 1).start()
-
-    fetch(j).wait()
-    slot = j % 2
+        fetch(now + 1).start()
+
+    gain = dotf(cond[0], gain_cond[...]) + dotf(hots[0], gain_step[...])
+    fetch(now).wait()
+    slot = now % 2
     d_hidden = (
         dotf(window[slot, 2 * DILATION :] * lanes(masks[0, :, 128:256], 2 * width), w_conv[0], NT)
         + dotf(window[slot, DILATION : DILATION + tile], w_conv[1], NT)
         + dotf(window[slot, 0:tile] * lanes(masks[0, :, 0:128], 2 * width), w_conv[2], NT)
     )
     alive = lanes(masks[0, :, 256:384].astype(f32), width)
-    grad_frames[0] = res[0].astype(f32) * (SQRT_HALF * alive) + d_hidden * (1.0 + gain[0])
+    grad_frames[0] = res[0].astype(f32) * (SQRT_HALF * alive) + d_hidden * (1.0 + gain)
     d_film = jnp.concatenate(
         [(d_hidden * frames[0].astype(f32)).astype(bf16), d_hidden.astype(bf16)], axis=1
     )
-    return dotf(jnp.concatenate([cond[0], masks[0, :, 384:]], axis=1), d_film, TN)
-
-
-def hidden_grad_first_kernel(
-    tile, d_conv, masks, frames, gain, res, cond, w_conv, grad_frames, total, window, sems
-):
-    part = hidden_grad_rows(
-        tile, 0, d_conv, masks, frames, gain, res, cond, w_conv, grad_frames, window, sems
-    )
-    j = pl.program_id(1)
-
-    @pl.when(j == 0)
+    part = dotf(jnp.concatenate([cond[0], hots[0]], axis=1), d_film, TN)
+
+    @pl.when(now == 0)
     def _():
         total[...] = part
 
-    @pl.when(j > 0)
+    @pl.when(now > 0)
     def _():
         total[...] += part
 
-
-def hidden_grad_last_kernel(
-    tile, place, d_conv, masks, frames, gain, res, cond, w_conv, embed, earlier, _frames_0,
-    grad_frames, keep, send, total, window, sems,
-):
-    part = hidden_grad_rows(
-        tile, 1, d_conv, masks, frames, gain, res, cond, w_conv, grad_frames, window, sems
-    )
-    j = pl.program_id(1)
-    width = frames.shape[2]
-
-    @pl.when(j == 0)
-    def _():
-        total[...] = earlier[...] + part
-
-    @pl.when(j > 0)
-    def _():
-        total[...] += part
-
-    @pl.when(j == pl.num_programs(1) - 1)
+    @pl.when(now == MICRO * steps - 1)
     def _():
         mine, other = halves_of(place[0], width)
         count = embed.shape[0]
@@ -480,24 +466,18 @@
             ref[1] = step.astype(ref.dtype)
 
 
-def out_kernel(gated, frames, masks, w_proj, res, skip):
-    width = gated.shape[2]
-    branch = dotf(gated[0], w_proj[...])
-    alive = lanes(masks[0, :, 256:384].astype(f32), width)
-    res[0] = ((frames[0].astype(f32) + branch[:, :width]) * (SQRT_HALF * alive)).astype(bf16)
-    skip[0] = (branch[:, width:] * alive).astype(bf16)
-
-
 def head_masks(width):
     column = lax.broadcasted_iota(jnp.int32, (1, width), 1)
     size = width // HEADS
     return [((column >= h * size) & (column < (h + 1) * size)).astype(f32) for h in range(HEADS)]
 
 
-def attention_kernel(groups, place, *refs):
+def attention_kernel(groups, members, layout, place, *refs):
     pieces = refs[:groups]
-    queries, w_query, w_key, w_value, w_out, w_film = refs[groups : groups + 6]
-    film, prompt, probs, keys, values, spread, summaries, totals = refs[groups + 6 :]
+    queries, *parts = refs[groups : groups + 10]
+    film, prompt, probs, keys, values, spread, summaries, totals, *fulls = refs[groups + 10 :]
+    assemble(place, members, layout, parts[:5], quarters_of(place, parts[5:]), fulls)
+    w_key, w_value, w_query, w_out, w_film = fulls
     _, micro, shard, width = pieces[0].shape
     masks = head_masks(width)
     scale = 1.0 / math.sqrt(width // HEADS)
@@ -675,15 +655,17 @@
     return lax.optimization_barrier((array, *others))[0]
 
 
-def gathered(packed, members, *others):
+def gathered(packed, members, early=(), late=(), bit_2=2):
     every = packed[None]
     for bit in bits_of("fsdp"):
         theirs = swapped(every, "fsdp", bit)
         every = theirs if members == 2 else jnp.concatenate([every, theirs], axis=0)
     here = every if members == 2 else every[1:]
-    if others:
-        here = behind(here, *others)
-    over = swapped(here, "tm", 2)
+    if early:
+        here = behind(here, *early)
+    over = swapped(here, "tm", bit_2)
+    if late:
+        over = behind(over, *late)
     return here, over, swapped(here, "tm", 1), swapped(over, "tm", 1)
 
 
@@ -698,42 +680,66 @@
             )
             parts, rows, width = total.shape
             self.totals.append(total.reshape(parts, members, 2, rows // members // 2, width))
-        self.depart()
-
-    def depart(self):
-        self.aways, self.kept = zip(
-            *[parted(t, *s[0]) for t, s in zip(self.totals, self.steps, strict=True)], strict=True
-        )
-
-    def step(self):
+        self.send()
+
+    def send(self):
+        pairs = [parted(t, *s[0]) for t, s in zip(self.totals, self.steps, strict=True)]
+        self.aways, self.kept = zip(*pairs, strict=True)
+        self.raw = [swapped(a, *s[0][:2]) for a, s in zip(self.aways, self.steps, strict=True)]
+
+    def absorb(self, *others):
         self.totals = [
-            k + swapped(a, s[0][0], s[0][1]).astype(f32)
-            for a, k, s in zip(self.aways, self.kept, self.steps, strict=True)
+            k + behind(r, *others).astype(f32) for k, r in zip(self.kept, self.raw, strict=True)
         ]
         self.steps = [s[1:] for s in self.steps]
         if self.steps[0]:
-            self.depart()
-
-    def finish(self):
+            self.send()
+
+    def absorb_all(self, *others):
         while self.steps[0]:
-            self.step()
+            self.absorb(*others)
+
+    def start_third(self):
         total = jnp.concatenate(self.totals, axis=0)
-        parts, rows, width = total.shape[0], total.shape[3], total.shape[4]
-        total = total.reshape(parts, rows, width)
-        away, kept = parted(total, "tm", 4, 1)
-        total = kept + swapped(away, "tm", 4).astype(f32)
-        for bit in bits_of("tm")[3:]:
-            own = rounded(total)
-            total = own + swapped(own.astype(bf16), "tm", bit).astype(f32)
-        own = rounded(total).astype(bf16)
-        for bit in (4, 2):
-            own = doubled(own, swapped(own, "tm", bit), "tm", bit, 1)
+        total = total.reshape(total.shape[0], total.shape[3], total.shape[4])
+        self.away, self.own = parted(total, "tm", 4, 1)
+        self.raw = swapped(self.away, "tm", 4)
+
+    def fold(self, *others):
+        self.total = self.own + behind(self.raw, *others).astype(f32)
+
+    def start_double(self, bit):
+        self.own = rounded(self.total)
+        self.away = self.own.astype(bf16)
+        self.raw = swapped(self.away, "tm", bit)
+
+    def start_gather(self):
+        self.away = rounded(self.total).astype(bf16)
+        self.raw = [swapped(self.away, "tm", bits) for bits in (4, 2, 6)]
+
+    def gather(self):
+        clear = bit_of("tm", 4) == 0
+        pairs = []
+        for one, two in ((self.away, self.raw[0]), (self.raw[1], self.raw[2])):
+            pairs.append([jnp.where(clear, one, two), jnp.where(clear, two, one)])
+        clear = bit_of("tm", 2) == 0
+        rows = [jnp.where(clear, a, b) for a, b in zip(pairs[0] + pairs[1], pairs[1] + pairs[0], strict=True)]
+        own = jnp.concatenate(rows, axis=1)
         return own, swapped(own, "tm", 1)
 
 
-def joined(pair, part):
-    own, other = (a[part] for a in pair)
-    return doubled(own, other, "tm", 1, own.ndim - 1).astype(f32)
+def join_kernel(place, own, other, *outs):
+    width = own.shape[2]
+    mine, theirs = halves_of(place[0], width)
+    first = 0
+    for out in outs:
+        for source, columns in ((own, mine), (other, theirs)):
+            if len(out.shape) == 2:
+                out[:, pl.ds(columns, width)] = source[first].astype(f32)
+            else:
+                count = out.shape[0]
+                out[:, :, pl.ds(columns, width)] = source[first : first + count].astype(f32)
+        first += 1 if len(out.shape) == 2 else out.shape[0]
 
 
 def step_embedding(pack_steps, width):
@@ -758,8 +764,8 @@
     frames, cond, res, skip = frames[:, 0], conditioning[:, 0], grad_res[:, 0], grad_skip[:, 0]
     core = tm_index % 2
     quarter = core * 2 + (tm_index // 2) % 2
-    place = jnp.stack([core, tm_index, member, quarter]).astype(jnp.int32)
-    product = 2 * MICRO * rows * width * wide
+    other_quarter = core * 2 + (tm_index // 4) % 2
+    place = jnp.stack([core, tm_index, member, quarter, other_quarter]).astype(jnp.int32)
 
     part = shard_rows // 4
 
@@ -770,30 +776,17 @@
             [scalars(place)] + [hbm(w) for w in weights],
             [new_fixed((height, wide), bf16) for height in heights],
             name,
-            10**5,
+            2,
             scratch=[pltpu.VMEM((height, wide), f32) for height in heights]
             + [pltpu.SemaphoreType.DMA((10,))],
             after=after,
         )
 
-    def unpack(weights, layout, quarters, name, *make):
-        return call(
-            functools.partial(unpack_kernel, layout, members),
-            (1,),
-            [scalars(place)] + [whole(w) for w in weights] + [whole(q) for q in quarters],
-            [m((members * math.prod(w.shape[:-1]), w.shape[-1]), bf16) for m in make for w in weights],
-            name,
-            10**5,
-        )
-
-    first_weights = [w_cond, w_step]
-    first_layout = [(0, 0), (part, 0)]
-    second_weights = [w_key, w_value, w_query, w_out, w_film]
-    second_layout = [(0, 0), (0, width), (part, 0), (part, width), (2 * part, 0)]
-    third_weights = [w_conv, w_proj]
-    third_layout = [(0, 0), (3 * part, 0)]
-    (first,) = pack(first_weights, [first_layout], [2 * part], "pack_first")
-    first_quarters = gathered(first, members)
+    layout_1 = [(0, 0), (part, 0)]
+    layout_2 = [(0, 0), (0, width), (part, 0), (part, width), (2 * part, 0)]
+    layout_3 = [(k * part, 0) for k in range(4)]
+    taps_3 = [4, (0, 0, 0), (part, 0, 1), (2 * part, 0, 2), (3 * part, 0)]
+    (first,) = pack([w_cond, w_step], [[3, *layout_1]], [2 * part], "pack_first")
 
     edge = (4, MICRO, HALO, width)
     last_rows, first_rows = call(
@@ -802,36 +795,52 @@
         [hbm(a) for a in (frames, cond, res, skip)],
         [new_fixed(edge, bf16), new_fixed(edge, bf16)],
         "edges",
-        10**5,
+        1.1,
         scratch=[pltpu.SemaphoreType.DMA((8,))],
         after=[first],
     )
     low = lax.ppermute(last_rows, "tm", [(d, d + 1) for d in range(tm_count - 1)])
     high = lax.ppermute(first_rows, "tm", [(d + 1, d) for d in range(tm_count - 1)])
 
+    second, third = pack(
+        [w_key, w_value, w_query, w_out, w_film, w_conv, w_conv, w_conv, w_proj],
+        [[3, *layout_2], taps_3],
+        [3 * part, 4 * part],
+        "pack_rest",
+        after=[last_rows],
+    )
     utters = lengths.shape[2]
     slot = -(-utters // 32) * 32
-    lane_count = 3 * 128 + 2 * MICRO * slot
-    masks, mask_ends = call(
+    hots = 2 * MICRO * slot
+    masks, hot, mask_ends, hot_ends = call(
         functools.partial(masks_kernel, rows, slot, tm_count * rows),
         (1,),
         [scalars(place), scalars(lengths[:, 0])],
-        [new((MICRO, rows, lane_count), bf16), new((MICRO, 2 * HALO, lane_count), bf16)],
+        [new((MICRO, n, lane), bf16) for n in (rows, 2 * HALO) for lane in (384, hots)],
         "masks",
-        10**5,
-        after=[last_rows],
+        5,
+        after=[second],
     )
     own = prompt[:, 0]
     across = swapped(own, "tm", 2)
     near = jnp.stack([own, swapped(own, "tm", 1), across, swapped(across, "tm", 1)])
-    second, third = pack(
-        second_weights + third_weights,
-        [second_layout, third_layout],
-        [3 * part, 4 * part],
-        "pack_rest",
-        after=[masks, first_quarters[0], low, high, near],
-    )
-
+    own_cond, own_step, *own_second, own_conv, own_proj = call(
+        own_kernel,
+        (1,),
+        [
+            whole(w)
+            for w in (w_cond, w_step, w_key, w_value, w_query, w_out, w_film, w_conv.reshape(-1, wide), w_proj)
+        ],
+        [new_fixed(w.shape, bf16) for w in (w_cond, w_step)]
+        + [
+            new(w.shape, bf16)
+            for w in (w_key, w_value, w_query, w_out, w_film, w_conv.reshape(-1, wide), w_proj)
+        ],
+        "own_shards",
+        4,
+        after=[mask_ends, near],
+    )
+    first_quarters = gathered(first, members, early=[mask_ends], late=[own_cond])
     pieces = [near] + [swapped(near, "tm", 4 * k) for k in range(1, tm_count // 4)]
     full_queries = queries.astype(bf16)
     for bit in bits_of("fsdp"):
@@ -840,42 +849,46 @@
     slots = jnp.pad(steps[:, 0], ((0, 0), (0, slot - utters))).reshape(-1)
     embed = step_embedding(slots, width).astype(bf16)
 
-    full_cond, full_step = unpack(
-        first_weights, first_layout, first_quarters, "unpack_first", new_fixed
-    )
-    hidden, gain = call(
-        functools.partial(film_kernel, tile),
+    hidden, gain_cond, gain_step = call(
+        functools.partial(film_kernel, tile, members, layout_1),
         tiles,
         [
+            scalars(place),
             blocks(frames, tile),
             blocks(cond, tile),
             whole(low),
             whole(high),
-            blocks(masks, tile),
-            whole(mask_ends),
+            blocks(hot, tile),
+            whole(hot_ends),
             whole(embed),
-            fixed(full_step),
-            fixed(full_cond),
+            fixed(own_cond),
+            fixed(own_step),
+            *[fixed(q) for q in first_quarters],
         ],
         [
             new_fixed((MICRO, rows + 2 * HALO + 2 * DILATION, width), bf16),
-            new_blocks((MICRO, rows, width), f32, tile),
+            new((width, width), bf16),
+            new((hots, width), bf16),
         ],
         "film",
-        10**5,
-        scratch=[pltpu.VMEM((2 * MICRO * slot, wide), bf16)],
+        10,
+        scratch=[
+            pltpu.VMEM((width, wide), bf16),
+            pltpu.VMEM((width, wide), bf16),
+            pltpu.VMEM((hots, wide), bf16),
+        ],
         after=[*pieces, full_queries],
     )
-
-    full_key, full_value, full_query, full_out, full_film = unpack(
-        second_weights, second_layout, gathered(second, members, hidden), "unpack_second", new
-    )
+    second_quarters = gathered(second, members, early=[own_cond], late=[gain_step])
+    third_quarters = gathered(third, members, early=[own_cond], late=[gain_step], bit_2=4)
     length = tm_count * prompt.shape[2]
-    film, prompt_full, probs, keys, values, spread, summaries, totals = call(
-        functools.partial(attention_kernel, len(pieces)),
+    film, prompt_full, probs, keys, values, spread, summaries, totals, *fulls = call(
+        functools.partial(attention_kernel, len(pieces), members, layout_2),
         (1,),
         [scalars(place)]
-        + [whole(a) for a in (*pieces, full_queries, full_query, full_key, full_value, full_out, full_film)],
+        + [whole(a) for a in (*pieces, full_queries)]
+        + [whole(a) for a in own_second]
+        + [fixed(a) for a in second_quarters],
         [
             new((MICRO, 8, wide)),
             new((MICRO, length, width), bf16),
@@ -885,93 +898,105 @@
             new((HEADS * QUERIES, width), bf16),
             new((MICRO, 8, width)),
             new((MICRO, 8, width)),
+            *[new((width, width), bf16)] * 4,
+            new((width, wide), bf16),
         ],
         "attention",
-        10**5,
-    )
-
-    full_conv, full_proj, conv_later, proj_later = unpack(
-        third_weights, third_layout, gathered(third, members, hidden), "unpack_third", new_fixed, new
-    )
-    d_conv, d_conv_copy, gated, sums, proj_keep, proj_send = call(
-        functools.partial(conv_kernel, tile),
+        5,
+    )
+
+    full_key, full_value, full_query, full_out, full_film = fulls
+
+    d_conv, d_conv_copy, conv_copy, sums, proj_keep, proj_send, res_out, skip_out = call(
+        functools.partial(conv_kernel, tile, members, layout_3),
         tiles,
         [
             scalars(place),
             fixed(hidden),
             blocks(masks, tile),
             whole(mask_ends),
+            blocks(frames, tile),
             blocks(res, tile),
             blocks(skip, tile),
             whole(low),
             whole(high),
-            fixed(full_conv),
-            fixed(full_proj),
             whole(film),
+            whole(own_conv),
+            whole(own_proj),
+            *[fixed(q) for q in third_quarters],
         ],
         [
             new_fixed((MICRO, rows + 2 * HALO, wide), bf16),
             new_hbm((MICRO, rows + 2 * HALO, wide), bf16),
+            new_hbm((3 * width, wide), bf16),
+            new((8, wide)),
+            new_fixed((1, width, width)),
+            new_fixed((1, width, width), bf16),
             new_blocks((MICRO, rows, width), bf16, tile),
-            new((8, wide)),
-            new((1, width, width)),
-            new((1, width, width), bf16),
+            new_blocks((MICRO, rows, width), bf16, tile),
         ],
         "conv",
-        5.5 * product,
+        32,
         scratch=[
+            pltpu.VMEM((3 * width, wide), bf16),
+            pltpu.VMEM((width, wide), bf16),
             pltpu.VMEM((width, wide), f32),
             pltpu.VMEM((8, wide), f32),
-            pltpu.SemaphoreType.DMA((MICRO,)),
-        ],
-    )
-
+            pltpu.SemaphoreType.DMA((3,)),
+        ],
+    )
+
+    proj_received = swapped(proj_send, "tm", 1)
+    sums_near = swapped(sums, "tm", 1)
     conv_keep, conv_send = call(
         conv_grad_kernel,
         (3,),
         [scalars(place), fixed(hidden), whole(masks), fixed(d_conv)],
-        [new((3, width, width)), new((3, width, width), bf16)],
+        [new_fixed((3, width, width)), new_fixed((3, width, width), bf16)],
         "conv_grad",
-        3 * product,
-    )
-    proj_received = swapped(proj_send, "tm", 1)
+        13.5,
+    )
     conv_received = swapped(conv_send, "tm", 1)
-
-    res_out, skip_out = call(
-        out_kernel,
-        tiles,
-        [blocks(gated, tile), blocks(frames, tile), blocks(masks, tile), whole(proj_later)],
-        [new_blocks((MICRO, rows, width), bf16, tile)] * 2,
-        "outputs",
-        product,
-        after=[conv_send],
-    )
-    for bit in bits_of("tm"):
-        sums = sums + swapped(sums, "tm", bit)
-
+    sums = sums + behind(sums_near, conv_send)
+    sums_far = swapped(sums, "tm", 2)
     conv_proj = Reduction(
         [
             ([conv_keep[:2]], [conv_received[:2]]),
             ([conv_keep[2:], proj_keep], [conv_received[2:], proj_received]),
         ]
     )
-    stream = functools.partial(blocks, tile=tile)
-    taps = conv_later.reshape(3, width, wide)
-    window = [
-        pltpu.VMEM((2, tile + 2 * DILATION, wide), bf16),
-        pltpu.SemaphoreType.DMA((2,)),
-    ]
-    film_height = width + lane_count - 3 * 128
-    grad_frames, total = call(
-        functools.partial(hidden_grad_first_kernel, tile),
-        (1, rows // tile),
-        [hbm(d_conv_copy)] + [stream(a) for a in (masks, frames, gain, res, cond)] + [whole(taps)],
-        [new_blocks((MICRO, rows, width), f32, tile), new((film_height, wide))],
-        "hidden_grad_first",
-        2.25 * product,
-        scratch=window,
-        after=[*conv_proj.aways, res_out],
-    )
+    sums = sums + behind(sums_far, *conv_proj.aways)
+    sums_far = swapped(sums, "tm", 4)
+    grad_frames, keep, send = call(
+        functools.partial(hidden_grad_kernel, tile),
+        tiles,
+        [scalars(place), hbm(d_conv_copy)]
+        + [blocks(a, tile) for a in (masks, hot, frames, res, cond)]
+        + [whole(a) for a in (conv_copy.reshape(3, width, wide), gain_cond, gain_step, embed)],
+        [
+            new_blocks((MICRO, rows, width), f32, tile),
+            new_fixed((2, width, width)),
+            new_fixed((2, width, width), bf16),
+        ],
+        "hidden_grad",
+        27,
+        scratch=[
+            pltpu.VMEM((width + hots, wide), f32),
+            pltpu.VMEM((2, tile + 2 * DILATION, wide), bf16),
+            pltpu.SemaphoreType.DMA((2,)),
+        ],
+        after=[*conv_proj.aways, sums],
+    )
+    send, sums_far, *conv_proj.raw = lax.optimization_barrier((send, sums_far, *conv_proj.raw))
+    received = swapped(send, "tm", 1)
+    conv_proj.absorb()
+    sums = sums + sums_far
+    for bit in bits_of("tm")[3:-1]:
+        sums = sums + swapped(sums, "tm", bit)
+    sums_far = swapped(sums, "tm", bits_of("tm")[-1])
+    received = behind(received, *conv_proj.aways, sums)
+    cond_step = Reduction([([keep[:1]], [received[:1]]), ([keep[1:]], [received[1:]])])
+    sums = sums + behind(sums_far, *cond_step.aways)
     grad_prompt, pair, small = call(
         attention_grad_kernel,
         (1,),
@@ -985,29 +1010,15 @@
         ],
         [new((MICRO, length // tm_count, width)), new((width, width)), new((SMALL_ROWS, width))],
         "attention_grad",
-        product / 2,
+        7,
         scratch=[pltpu.VMEM((MICRO, length, wide), bf16)],
     )
-    conv_proj.step()
-    grad_frames, keep, send = call(
-        functools.partial(hidden_grad_last_kernel, tile),
-        (1, rows // tile),
-        [scalars(place), hbm(d_conv_copy)]
-        + [stream(a, first=1) for a in (masks, frames, gain, res, cond)]
-        + [whole(taps), whole(embed), whole(total), hbm(grad_frames)],
-        [
-            new_blocks((MICRO, rows, width), f32, tile, first=1),
-            new((2, width, width)),
-            new((2, width, width), bf16),
-        ],
-        "hidden_grad_last",
-        2.25 * product,
-        scratch=[pltpu.VMEM((film_height, wide), f32), *window],
-        after=[*conv_proj.aways, small],
-        aliases={10: 0},
-    )
-    received = swapped(send, "tm", 1)
-    cond_step = Reduction([([keep[:1]], [received[:1]]), ([keep[1:]], [received[1:]])])
+    small, pair, *raw = lax.optimization_barrier((small, pair, *conv_proj.raw, *cond_step.raw))
+    conv_proj.raw, cond_step.raw = raw[:2], raw[2:]
+    conv_proj.absorb_all()
+    conv_proj.start_third()
+    cond_step.absorb_all(conv_proj.away)
+    cond_step.start_third()
 
     for bit in reversed(bits_of("fsdp")):
         away, pair = parted(pair, "fsdp", bit, 0)
@@ -1032,27 +1043,49 @@
             new((shard_rows, wide)),
         ],
         "small_grads",
-        product / 10,
+        3.3,
         scratch=[pltpu.VMEM((width, wide), f32), pltpu.VMEM((QUERIES, width), f32)],
     )
 
-    conv_proj = conv_proj.finish()
-    cond_step = cond_step.finish()
+    def join(halves, shapes, name):
+        return call(
+            join_kernel,
+            (1,),
+            [scalars(place)] + [fixed(a) for a in halves],
+            [new(shape) for shape in shapes],
+            name,
+            3,
+        )
+
+    flat, tall = (shard_rows, wide), (3, shard_rows, wide)
+    conv_proj.fold()
+    for bit in bits_of("tm")[3:]:
+        conv_proj.start_double(bit)
+        cond_step.fold(grad_queries)
+        cond_step.start_double(bit)
+        conv_proj.fold(cond_step.away)
+    conv_proj.start_gather()
+    cond_step.fold(conv_proj.away)
+    cond_step.start_gather()
+    conv_proj = conv_proj.gather()
+    cond_step = cond_step.gather()
+    grad_cond, grad_step = join(cond_step, [flat, flat], "join_cond_step")
+    grad_conv, grad_proj = join(conv_proj, [tall, flat], "join_conv_proj")
     return (
         res_out[:, None],
         skip_out[:, None],
         grad_frames[:, None],
         grad_prompt[:, None],
         grad_queries,
-        joined(cond_step, 1),
-        joined(cond_step, 0),
-        joined(conv_proj, slice(0, 3)),
+        grad_step,
+        grad_cond,
+        grad_conv,
         grad_query,
         grad_key,
         grad_value,
         grad_out,
         grad_film,
-        joined(conv_proj, 3),
+        grad_proj,
     )
 
 

time: 294 us -> 237 us (0.81)
  waiting for transfers between devices: 87.4 us -> 42.1 us
  Pallas kernels: 134 us -> 119 us
  starting transfers between devices: 45.6 us -> 51.2 us
  other arithmetic: 16.4 us -> 13.3 us
    ppermute x47 -> x49, waiting for transfers between devices: 87.4 us -> 42 us  [swapped(): return lax.ppermute(array, axis, [(i, i ^ bit) for i in range(count)])]
    pallas_call x16 -> x14, Pallas kernels: 134 us -> 119 us  [call(): pl.pallas_call(body, grid=grid, in_specs=[spec for _, spec in ins] + [ANY...]
    convert_element_type x7 -> x4, other arithmetic: 7.77 us -> 0.28 us  [the longest x2 0.18 us: start_gather(): self.away = rounded(self.total).astype(bf16)]
    ppermute x47 -> x49, starting transfers between devices: 41.9 us -> 48.6 us  [swapped(): return lax.ppermute(array, axis, [(i, i ^ bit) for i in range(count)])]
    add x4, other arithmetic: 2.27 us -> 5.89 us  [__init__(): k + r.astype(f32)]
    unnamed x66 -> x50, local copies, waits for them, and re-layouts: 6.74 us -> 6.68 us
  transfers between devices with their start and end apart: 49 -> 51, of which waited for: 17 -> 14; matrix products, arithmetic and copies ran while one was open for 5% -> 6% of each run, Pallas kernels for 29% -> 30%
where the time goes in v2:
time: 237 us; the launch traced here: 235 us
  Pallas kernels  119 us (50%)
  starting transfers between devices  51.2 us (22%)
  waiting for transfers between devices  42.1 us (18%)
  other arithmetic  13.3 us (6%)
  local copies, waits for them, and re-layouts  8.36 us (4%)
    pallas_call x14, Pallas kernels, call(): pl.pallas_call(body, grid=grid, in_specs=[spec for _, spec in ins] + [ANY...  119 us
    ppermute x49, starting transfers between devices, swapped(): return lax.ppermute(array, axis, [(i, i ^ bit) for i in range(count)])  48.6 us
    ppermute x49, waiting for transfers between devices, swapped(): return lax.ppermute(array, axis, [(i, i ^ bit) for i in range(count)])  42 us
    unnamed x50, local copies, waits for them, and re-layouts  6.68 us
    add x4, other arithmetic, __init__(): k + r.astype(f32)  5.89 us
  transfers between devices with their start and end apart: 51, of which 14 were waited for; matrix products, arithmetic and copies ran while one was open for 6% of the time, Pallas kernels for 30%

profile of v2, /device:TPU:0, one launch (start us, length us, event | category | flops | bytes accessed | tf_op | source)
XLA Modules:
  0.0 234.9 jit_solution(12772060355103364924)
XLA Ops:
  0.6 3.0 %collective-permute-start.3 = (bf16[2,16,512]{2,1,0:T(8,128)(2,1)}, bf16[2,16,512]{2,1,0:T(8,128)(2,1)S(1)}, u32[]{:S(2)}, u32[]{:S(2)}) collective-permute-start(bf16[2,16,512]{2,1,0:T(8,128)(2,1)} %bitcast.89), channel_id=1, source_target_pairs={{0,4},{2,6},{4,0},{6,2},{8,12},{10,14},{12,8},{14,10},{16,20},{18,... | collective-permute-start | bytes 98312 | tf_op jit(solution)/shard_map/ppermute | solution.py:617
  8.7 2.3 pack_rest.1
  12.5 5.1 %masks.1 = (bf16[2,1536,384]{2,1,0:T(8,128)(2,1)}, bf16[2,1536,128]{2,1,0:T(8,128)(2,1)}, bf16[2,64,384]{2,1,0:T(8,128)(2,1)}, bf16[2,64,128]{2,1,0:T(8,128)(2,1)}) custom-call(s32[5]{0:T(128)S(1)} %stack.35.refs_0_, s32[2,30]{1,0:T(2,128)S(1)} %bitcast.65, bf16[192,1024]{1,0:T(8,128)(2,1)S(1)} %get-tuple-element.100.refs_2_), custom_call_target="tpu_custom_call" | custom-call | flops 5000000000 | bytes 4096 | tf_op jit(solution)/shard_map/masks/pallas_call | solution.py:66
  20.0 2.7 %collective-permute-start.10 = (bf16[4,2,16,512]{3,2,1,0:T(8,128)(2,1)S(1)}, bf16[4,2,16,512]{3,2,1,0:T(8,128)(2,1)S(1)}, u32[]{:S(2)}, u32[]{:S(2)}) collective-permute-start(bf16[4,2,16,512]{3,2,1,0:T(8,128)(2,1)S(1)} %pad_maximum_fusion.4.refs_10_.refs_14_.refs_1_), channel_id=1, source_target_pairs={{0,16},{2,18},{4,20},{6,22},{8,24},{10,26},{12,28},{14,30},{16,0},... | collective-permute-start | bytes 393224 | tf_op jit(solution)/shard_map/ppermute | solution.py:617
  22.7 3.1 %collective-permute-done.6.refs_11_ = bf16[1,128,1024]{2,1,0:T(8,128)(2,1)S(1)} collective-permute-done((bf16[1,128,1024]{2,1,0:T(8,128)(2,1)S(1)}, bf16[1,128,1024]{2,1,0:T(8,128)(2,1)S(1)}, u32[]{:S(2)}, u32[]{:S(2)}) %collective-permute-start.6) | collective-permute-done | bytes 262176 | tf_op jit(solution)/shard_map/ppermute | solution.py:617
  25.7 3.6 %collective-permute-start.11 = (bf16[4,2,16,512]{3,2,1,0:T(8,128)(2,1)S(1)}, bf16[4,2,16,512]{3,2,1,0:T(8,128)(2,1)S(1)}, u32[]{:S(2)}, u32[]{:S(2)}) collective-permute-start(bf16[4,2,16,512]{3,2,1,0:T(8,128)(2,1)S(1)} %pad_maximum_fusion.4.refs_10_.refs_14_.refs_1_), channel_id=1, source_target_pairs={{0,24},{2,26},{4,28},{6,30},{8,16},{10,18},{12,20},{14,22},{16,8},... | collective-permute-start | bytes 393224 | tf_op jit(solution)/shard_map/ppermute | solution.py:617
  30.2 5.5 %own_shards.1 = (bf16[256,1024]{1,0:T(8,128)(2,1)S(1)}, bf16[256,1024]{1,0:T(8,128)(2,1)S(1)}, bf16[256,512]{1,0:T(8,128)(2,1)}, bf16[256,512]{1,0:T(8,128)(2,1)...) custom-call(f32[256,1024]{1,0:T(8,128)} %refs_0_.1, ...), custom_call_target="tpu_custom_call" | custom-call | flops 4000000000 | bytes 4096 | tf_op jit(solution)/shard_map/own_shards/pallas_call | solution.py:66
  38.4 3.5 %collective-permute-start.9 = (bf16[4,2,16,512]{3,2,1,0:T(8,128)(2,1)S(1)}, bf16[4,2,16,512]{3,2,1,0:T(8,128)(2,1)S(1)}, u32[]{:S(2)}, u32[]{:S(2)}) collective-permute-start(bf16[4,2,16,512]{3,2,1,0:T(8,128)(2,1)S(1)} %pad_maximum_fusion.4.refs_10_.refs_14_.refs_1_), channel_id=1, source_target_pairs={{0,8},{2,10},{4,12},{6,14},{8,0},{10,2},{12,4},{14,6},{16,24},{18,... | collective-permute-start | bytes 393224 | tf_op jit(solution)/shard_map/ppermute | solution.py:617
  42.4 6.1 %collective-permute-done.9.refs_15_.refs_2_ = bf16[4,2,16,512]{3,2,1,0:T(8,128)(2,1)S(1)} collective-permute-done((bf16[4,2,16,512]{3,2,1,0:T(8,128)(2,1)S(1)}, bf16[4,2,16,512]{3,2,1,0:T(8,128)(2,1)S(1)}, u32[]{:S(2)}, u32[]{:S(2)}) %collective-permute-start.9) | collective-permute-done | bytes 131104 | tf_op jit(solution)/shard_map/ppermute | solution.py:617
  49.4 9.9 %film.1 = (bf16[2,1632,512]{2,1,0:T(8,128)(2,1)S(1)}, bf16[512,512]{1,0:T(8,128)(2,1)}, bf16[128,512]{1,0:T(8,128)(2,1)}) custom-call(s32[5]{0:T(128)S(1)} %stack.35.refs_0_, bf16[2,1536,512]{2,1,0:T(8,128)(2,1)} %bitcast.78, bf16[2,1536,512]{2,1,0:T(8,128)(2,1)} %bitcast.82, bf16[4,2,32,512]{3,2,1,0:T(8,128)(2,1)} %copy-done.22, ...), custom_call_target="tpu_custom_call" | custom-call | flops 10000000000 | bytes 4096 | tf_op jit(solution)/shard_map/film/pallas_call | solution.py:66
  60.0 3.0 %collective-permute-done.18.refs_13_ = bf16[1,256,1024]{2,1,0:T(8,128)(2,1)S(1)} collective-permute-done((bf16[1,256,1024]{2,1,0:T(8,128)(2,1)S(1)}, bf16[1,256,1024]{2,1,0:T(8,128)(2,1)S(1)}, u32[]{:S(2)}, u32[]{:S(2)}) %collective-permute-start.18) | collective-permute-done | bytes 524320 | tf_op jit(solution)/shard_map/ppermute | solution.py:617
  63.0 5.2 %attention.1 = (f32[2,8,1024]{2,1,0:T(8,128)}, bf16[2,256,512]{2,1,0:T(8,128)(2,1)}, f32[2,256,256]{2,1,0:T(8,128)}, bf16[2,256,512]{2,1,0:T(8,128)(2,1)}, bf16[...) custom-call(s32[5]{0:T(128)S(1)} %stack.35.refs_0_, ...), custom_call_target="tpu_custom_call" | custom-call | flops 5000000000 | bytes 4096 | tf_op jit(solution)/shard_map/attention/pallas_call | solution.py:66
  68.3 32.7 %conv.1 = (bf16[2,1600,1024]{2,1,0:T(8,128)(2,1)S(1)}, bf16[2,1600,1024]{2,1,0:T(8,128)(2,1)}, bf16[1536,1024]{1,0:T(8,128)(2,1)}, f32[8,1024]{1,0:T(8,128)}, f3...) custom-call(s32[5]{0:T(128)S(1)} %stack.35.refs_0_, ...), custom_call_target="tpu_custom_call" | custom-call | flops 32000000000 | bytes 4096 | tf_op jit(solution)/shard_map/conv/pallas_call | solution.py:66
  101.9 13.2 %conv_grad.1 = (f32[3,512,512]{2,1,0:T(8,128)S(1)}, bf16[3,512,512]{2,1,0:T(8,128)(2,1)}) custom-call(s32[5]{0:T(128)} %copy-done.3, bf16[2,1632,512]{2,1,0:T(8,128)(2,1)S(1)} %get-tuple-element.108.refs_1_, bf16[2,1536,384]{2,1,0:T(8,128)(2,1)} %get-tuple-element.109.refs_2_, bf16[2,1600,1024]{2,1,0:T(8,128)(2,1)S(1)} %get-tuple-element.129.refs_3_), custom_call_target="tpu_custom_call" | custom-call | flops 13500000256 | bytes 4096 | tf_op jit(solution)/shard_map/conv_grad/pallas_call | solution.py:66
  116.1 2.6 %collective-permute-done.23 = f32[8,1024]{1,0:T(8,128)S(1)} collective-permute-done((f32[8,1024]{1,0:T(8,128)S(1)}, f32[8,1024]{1,0:T(8,128)S(1)}, u32[]{:S(2)}, u32[]{:S(2)}) %collective-permute-start.23) | collective-permute-done | bytes 32800 | tf_op jit(solution)/shard_map/ppermute | solution.py:617
  118.8 2.0 collective-permute-start.24
  130.2 26.8 %hidden_grad.1 = (f32[2,1536,512]{2,1,0:T(8,128)}, f32[2,512,512]{2,1,0:T(8,128)S(1)}, bf16[2,512,512]{2,1,0:T(8,128)(2,1)S(1)}) custom-call(s32[5]{0:T(128)S(1)} %copy-done.4, bf16[2,1600,1024]{2,1,0:T(8,128)(2,1)} %get-tuple-element.126.refs_1_, bf16[2,1536,384]{2,1,0:T(8,128)(2,1)} %get-tuple-element.109.refs_2_, ...), custom_call_target="tpu_custom_call" | custom-call | flops 27000000512 | bytes 4096 | tf_op jit(solution)/shard_map/hidden_grad/pallas_call | solution.py:66
  167.4 6.8 %attention_grad.1 = (f32[2,16,512]{2,1,0:T(8,128)}, f32[512,512]{1,0:T(8,128)}, f32[72,512]{1,0:T(8,128)}) custom-call(s32[5]{0:T(128)S(1)} %copy-done.4, f32[8,1024]{1,0:T(8,128)} %add.167.refs_1_, bf16[2,256,512]{2,1,0:T(8,128)(2,1)} %get-tuple-element.146.refs_2_, f32[2,256,256]{2,1,0:T(8,128)} %get-tuple-element.147.refs_3_, ...), custom_call_target="tpu_custom_call" | custom-call | flops 7000000000 | bytes 4096 | tf_op jit(solution)/shard_map/attention_grad/pallas_call | solution.py:66
  174.2 2.1 collective-permute-done.33
  178.2 1.8 collective-permute-start.39
  183.4 1.8 collective-permute-done.35
  185.2 4.1 %collective-permute-done.36 = bf16[1,1,1,128,512]{4,3,0,2,1:T(8,128)(2,1)S(1)} collective-permute-done((bf16[1,1,1,128,512]{4,3,0,2,1:T(8,128)(2,1)S(1)}, bf16[1,1,1,128,512]{4,3,0,2,1:T(8,128)(2,1)S(1)}, u32[]{:S(2)}, u32[]{:S(2)}) %collective-permute-start.36) | collective-permute-done | bytes 131104 | tf_op jit(solution)/shard_map/ppermute | solution.py:617
  189.4 1.8 collective-permute-start.37
  192.0 2.4 %collective-permute-start.40 = (bf16[4,64,512]{2,1,0:T(8,128)(2,1)S(1)}, bf16[4,64,512]{2,1,0:T(8,128)(2,1)S(1)}, u32[]{:S(2)}, u32[]{:S(2)}) collective-permute-start(bf16[4,64,512]{2,1,0:T(8,128)(2,1)S(1)} %fusion.17), channel_id=1, source_target_pairs={{0,16},{2,18},{4,20},{6,22},{8,24},{10,26},{12,28},{14,30},{16,0},... | collective-permute-start | bytes 786440 | tf_op jit(solution)/shard_map/ppermute | solution.py:617
  194.4 3.4 %small_grads.1 = (f32[16,512]{1,0:T(8,128)}, f32[256,512]{1,0:T(8,128)}, f32[256,512]{1,0:T(8,128)}, f32[256,1024]{1,0:T(8,128)}) custom-call(s32[5]{0:T(128)S(1)} %copy-done.4, f32[2,72,512]{2,1,0:T(8,128)} %pad_maximum_fusion.3.refs_1_, bf16[32,512]{1,0:T(8,128)(2,1)} %copy-done.2, bf16[512,512]{1,0:T(8,128)(2,1)} %get-tuple-element.161.refs_3_), custom_call_target="tpu_custom_call" | custom-call | flops 3300000000 | bytes 4096 | tf_op jit(solution)/shard_map/small_grads/pallas_call | solution.py:66
  198.5 10.6 %collective-permute-done.40 = bf16[4,64,512]{2,1,0:T(8,128)(2,1)S(1)} collective-permute-done((bf16[4,64,512]{2,1,0:T(8,128)(2,1)S(1)}, bf16[4,64,512]{2,1,0:T(8,128)(2,1)S(1)}, u32[]{:S(2)}, u32[]{:S(2)}) %collective-permute-start.40) | collective-permute-done | bytes 262176 | tf_op jit(solution)/shard_map/ppermute | solution.py:617
  210.5 2.3 collective-permute-start.47
  213.3 5.2 %collective-permute-done.45 = bf16[4,64,512]{2,1,0:T(8,128)(2,1)S(1)} collective-permute-done((bf16[4,64,512]{2,1,0:T(8,128)(2,1)S(1)}, bf16[4,64,512]{2,1,0:T(8,128)(2,1)S(1)}, u32[]{:S(2)}, u32[]{:S(2)}) %collective-permute-start.45) | collective-permute-done | bytes 262176 | tf_op jit(solution)/shard_map/ppermute | solution.py:617
  219.8 5.2 %collective-permute-start.43 = (bf16[2,64,512]{2,1,0:T(8,128)(2,1)S(1)}, bf16[2,64,512]{2,1,0:T(8,128)(2,1)S(1)}, u32[]{:S(2)}, u32[]{:S(2)}) collective-permute-start(bf16[2,64,512]{2,1,0:T(8,128)(2,1)S(1)} %reduce-precision_convert_fusion.2), channel_id=1, source_target_pairs={{0,12},{2,14},{4,8},{6,10},{8,4},{10,6},{12,0},{14,2},{16,28},{18,... | collective-permute-start | bytes 393224 | tf_op jit(solution)/shard_map/ppermute | solution.py:617
  228.1 2.0 select_convert_fusion
  230.1 2.0 join_cond_step.1
  232.1 2.8 %join_conv_proj.1 = (f32[3,256,1024]{2,1,0:T(8,128)}, f32[256,1024]{1,0:T(8,128)}) custom-call(s32[5]{0:T(128)S(1)} %copy-done.4, bf16[4,256,512]{2,1,0:T(8,128)(2,1)S(1)} %pad_maximum_fusion.1.refs_1_, bf16[4,256,512]{2,1,0:T(8,128)(2,1)S(1)} %collective-permute-done.48.refs_2_), custom_call_target="tpu_custom_call" | custom-call | flops 3000000000 | bytes 4096 | tf_op jit(solution)/shard_map/join_conv_proj/pallas_call | solution.py:66
  (185 shorter events, 49.0 us)
Async XLA Ops:
  0.6 18.1 %collective-permute-start.3 = (bf16[2,16,512]{2,1,0:T(8,128)(2,1)}, bf16[2,16,512]{2,1,0:T(8,128)(2,1)S(1)}, u32[]{:S(2)}, u32[]{:S(2)}) collective-permute-start(bf16[2,16,512]{2,1,0:T(8,128)(2,1)} %bitcast.89), channel_id=1, source_target_pairs={{0,4},{2,6},{4,0},{6,2},{8,12},{10,14},{12,8},{14,10},{16,20},{18,... | collective-permute-start | bytes 98312 | tf_op jit(solution)/shard_map/ppermute | solution.py:617
  3.6 15.8 %collective-permute-start.2 = (bf16[2,16,512]{2,1,0:T(8,128)(2,1)}, bf16[2,16,512]{2,1,0:T(8,128)(2,1)S(1)}, u32[]{:S(2)}, u32[]{:S(2)}) collective-permute-start(bf16[2,16,512]{2,1,0:T(8,128)(2,1)} %bitcast.90), channel_id=1, source_target_pairs={{0,2},{2,0},{4,6},{6,4},{8,10},{10,8},{12,14},{14,12},{16,18},{18,... | collective-permute-start | bytes 98312 | tf_op jit(solution)/shard_map/ppermute | solution.py:617
  5.4 12.4 %collective-permute-start.5 = (bf16[1,128,1024]{2,1,0:T(8,128)(2,1)S(1)}, bf16[1,128,1024]{2,1,0:T(8,128)(2,1)S(1)}, u32[]{:S(2)}, u32[]{:S(2)}) collective-permute-start(bf16[1,128,1024]{2,1,0:T(8,128)(2,1)S(1)} %bitcast.62), channel_id=1, source_target_pairs={{0,1},{1,0},{2,3},{3,2},{4,5},{5,4},{6,7},{7,6},{8,9},{9,8},{10,11... | collective-permute-start | bytes 786440 | tf_op jit(solution)/shard_map/ppermute | solution.py:617
  7.0 28.7 %collective-permute-start.12 = (bf16[16,512]{1,0:T(8,128)(2,1)S(1)}, bf16[16,512]{1,0:T(8,128)(2,1)S(1)}, u32[]{:S(2)}, u32[]{:S(2)}) collective-permute-start(bf16[16,512]{1,0:T(8,128)(2,1)S(1)} %convert_element_type.138), channel_id=1, source_target_pairs={{0,1},{1,0},{2,3},{3,2},{4,5},{5,4},{6,7},{7,6},{8,9},{9,8},{10,11... | collective-permute-start | bytes 49160 | tf_op jit(solution)/shard_map/ppermute | solution.py:617
  10.9 30.9 %collective-permute-start.17 = (bf16[1,256,1024]{2,1,0:T(8,128)(2,1)S(1)}, bf16[1,256,1024]{2,1,0:T(8,128)(2,1)S(1)}, u32[]{:S(2)}, u32[]{:S(2)}) collective-permute-start(bf16[1,256,1024]{2,1,0:T(8,128)(2,1)S(1)} %bitcast.63), channel_id=1, source_target_pairs={{0,1},{1,0},{2,3},{3,2},{4,5},{5,4},{6,7},{7,6},{8,9},{9,8},{10,11... | collective-permute-start | bytes 1572872 | tf_op jit(solution)/shard_map/ppermute | solution.py:617
  19.4 22.5 %collective-permute-start.13 = (bf16[1,192,1024]{2,1,0:T(8,128)(2,1)S(1)}, bf16[1,192,1024]{2,1,0:T(8,128)(2,1)S(1)}, u32[]{:S(2)}, u32[]{:S(2)}) collective-permute-start(bf16[1,192,1024]{2,1,0:T(8,128)(2,1)S(1)} %bitcast.64), channel_id=1, source_target_pairs={{0,1},{1,0},{2,3},{3,2},{4,5},{5,4},{6,7},{7,6},{8,9},{9,8},{10,11... | collective-permute-start | bytes 1179656 | tf_op jit(solution)/shard_map/ppermute | solution.py:617
  20.0 17.0 %collective-permute-start.10 = (bf16[4,2,16,512]{3,2,1,0:T(8,128)(2,1)S(1)}, bf16[4,2,16,512]{3,2,1,0:T(8,128)(2,1)S(1)}, u32[]{:S(2)}, u32[]{:S(2)}) collective-permute-start(bf16[4,2,16,512]{3,2,1,0:T(8,128)(2,1)S(1)} %pad_maximum_fusion.4.refs_10_.refs_14_.refs_1_), channel_id=1, source_target_pairs={{0,16},{2,18},{4,20},{6,22},{8,24},{10,26},{12,28},{14,30},{16,0},... | collective-permute-start | bytes 393224 | tf_op jit(solution)/shard_map/ppermute | solution.py:617
  25.7 12.6 %collective-permute-start.11 = (bf16[4,2,16,512]{3,2,1,0:T(8,128)(2,1)S(1)}, bf16[4,2,16,512]{3,2,1,0:T(8,128)(2,1)S(1)}, u32[]{:S(2)}, u32[]{:S(2)}) collective-permute-start(bf16[4,2,16,512]{3,2,1,0:T(8,128)(2,1)S(1)} %pad_maximum_fusion.4.refs_10_.refs_14_.refs_1_), channel_id=1, source_target_pairs={{0,24},{2,26},{4,28},{6,30},{8,16},{10,18},{12,20},{14,22},{16,8},... | collective-permute-start | bytes 393224 | tf_op jit(solution)/shard_map/ppermute | solution.py:617
  35.8 12.8 %collective-permute-start = (bf16[4,2,32,512]{3,2,1,0:T(8,128)(2,1)S(1)}, bf16[4,2,32,512]{3,2,1,0:T(8,128)(2,1)S(1)}, u32[]{:S(2)}, u32[]{:S(2)}) collective-permute-start(bf16[4,2,32,512]{3,2,1,0:T(8,128)(2,1)S(1)} %get-tuple-element.98.refs_10_), channel_id=1, source_target_pairs={{0,2},{2,4},{4,6},{6,8},{8,10},{10,12},{12,14},{14,16},{16,18},{18... | collective-permute-start | bytes 786440 | tf_op jit(solution)/shard_map/ppermute | solution.py:802
  37.1 11.6 %collective-permute-start.1 = (bf16[4,2,32,512]{3,2,1,0:T(8,128)(2,1)S(1)}, bf16[4,2,32,512]{3,2,1,0:T(8,128)(2,1)S(1)}, u32[]{:S(2)}, u32[]{:S(2)}) collective-permute-start(bf16[4,2,32,512]{3,2,1,0:T(8,128)(2,1)S(1)} %get-tuple-element.99), channel_id=1, source_target_pairs={{2,0},{4,2},{6,4},{8,6},{10,8},{12,10},{14,12},{16,14},{18,16},{20... | collective-permute-start | bytes 786440 | tf_op jit(solution)/shard_map/ppermute | solution.py:803
  38.4 10.2 %collective-permute-start.9 = (bf16[4,2,16,512]{3,2,1,0:T(8,128)(2,1)S(1)}, bf16[4,2,16,512]{3,2,1,0:T(8,128)(2,1)S(1)}, u32[]{:S(2)}, u32[]{:S(2)}) collective-permute-start(bf16[4,2,16,512]{3,2,1,0:T(8,128)(2,1)S(1)} %pad_maximum_fusion.4.refs_10_.refs_14_.refs_1_), channel_id=1, source_target_pairs={{0,8},{2,10},{4,12},{6,14},{8,0},{10,2},{12,4},{14,6},{16,24},{18,... | collective-permute-start | bytes 393224 | tf_op jit(solution)/shard_map/ppermute | solution.py:617
  48.6 10.9 %collective-permute-start.14 = (bf16[1,192,1024]{2,1,0:T(8,128)(2,1)S(1)}, bf16[1,192,1024]{2,1,0:T(8,128)(2,1)S(1)}, u32[]{:S(2)}, u32[]{:S(2)}) collective-permute-start(bf16[1,192,1024]{2,1,0:T(8,128)(2,1)S(1)} %collective-permute-done.13.refs_11_), channel_id=1, source_target_pairs={{0,4},{2,6},{4,0},{6,2},{8,12},{10,14},{12,8},{14,10},{16,20},{18,... | collective-permute-start | bytes 1179656 | tf_op jit(solution)/shard_map/ppermute | solution.py:617
  48.6 14.4 %collective-permute-start.15 = (bf16[1,192,1024]{2,1,0:T(8,128)(2,1)S(1)}, bf16[1,192,1024]{2,1,0:T(8,128)(2,1)S(1)}, u32[]{:S(2)}, u32[]{:S(2)}) collective-permute-start(bf16[1,192,1024]{2,1,0:T(8,128)(2,1)S(1)} %collective-permute-done.13.refs_11_), channel_id=1, source_target_pairs={{0,2},{2,0},{4,6},{6,4},{8,10},{10,8},{12,14},{14,12},{16,18},{18,... | collective-permute-start | bytes 1179656 | tf_op jit(solution)/shard_map/ppermute | solution.py:617
  48.7 14.3 %collective-permute-start.18 = (bf16[1,256,1024]{2,1,0:T(8,128)(2,1)S(1)}, bf16[1,256,1024]{2,1,0:T(8,128)(2,1)S(1)}, u32[]{:S(2)}, u32[]{:S(2)}) collective-permute-start(bf16[1,256,1024]{2,1,0:T(8,128)(2,1)S(1)} %collective-permute-done.17.refs_12_), channel_id=1, source_target_pairs={{0,8},{2,10},{4,12},{6,14},{8,0},{10,2},{12,4},{14,6},{16,24},{18,... | collective-permute-start | bytes 1572872 | tf_op jit(solution)/shard_map/ppermute | solution.py:617
  118.8 11.1 %collective-permute-start.24 = (f32[8,1024]{1,0:T(8,128)S(1)}, f32[8,1024]{1,0:T(8,128)S(1)}, u32[]{:S(2)}, u32[]{:S(2)}) collective-permute-start(f32[8,1024]{1,0:T(8,128)S(1)} %add.158), channel_id=1, source_target_pairs={{0,4},{2,6},{4,0},{6,2},{8,12},{10,14},{12,8},{14,10},{16,20},{18,... | collective-permute-start | bytes 98312 | tf_op jit(solution)/shard_map/ppermute | solution.py:617
  125.1 31.9 %collective-permute-start.27 = (bf16[2,2,1,128,512]{4,3,0,2,1:T(8,128)(2,1)S(1)}, bf16[2,2,1,128,512]{4,3,0,2,1:T(8,128)(2,1)S(1)}, u32[]{:S(2)}, u32[]{:S(2)}) collective-permute-start(bf16[2,2,1,128,512]{4,3,0,2,1:T(8,128)(2,1)S(1)} %copy.55), channel_id=1, source_target_pairs={{0,4},{2,6},{4,0},{6,2},{8,12},{10,14},{12,8},{14,10},{16,20},{18,... | collective-permute-start | bytes 1572872 | tf_op jit(solution)/shard_map/ppermute | solution.py:617
  129.2 27.7 %collective-permute-start.26 = (bf16[2,1,2,128,512]{4,3,0,2,1:T(8,128)(2,1)S(1)}, bf16[2,1,2,128,512]{4,3,0,2,1:T(8,128)(2,1)S(1)}, u32[]{:S(2)}, u32[]{:S(2)}) collective-permute-start(bf16[2,1,2,128,512]{4,3,0,2,1:T(8,128)(2,1)S(1)} %copy.56), channel_id=1, source_target_pairs={{0,1},{1,0},{2,3},{3,2},{4,5},{5,4},{6,7},{7,6},{8,9},{9,8},{10,11... | collective-permute-start | bytes 1572872 | tf_op jit(solution)/shard_map/ppermute | solution.py:617
  129.8 27.1 %collective-permute-start.25 = (f32[8,1024]{1,0:T(8,128)S(1)}, f32[8,1024]{1,0:T(8,128)S(1)}, u32[]{:S(2)}, u32[]{:S(2)}) collective-permute-start(f32[8,1024]{1,0:T(8,128)S(1)} %add.159.refs_13_), channel_id=1, source_target_pairs={{0,8},{2,10},{4,12},{6,14},{8,0},{10,2},{12,4},{14,6},{16,24},{18,... | collective-permute-start | bytes 98312 | tf_op jit(solution)/shard_map/ppermute | solution.py:617
  160.6 13.6 %collective-permute-start.31 = (bf16[2,1,1,128,512]{4,3,0,2,1:T(8,128)(2,1)S(1)}, bf16[2,1,1,128,512]{4,3,0,2,1:T(8,128)(2,1)S(1)}, u32[]{:S(2)}, u32[]{:S(2)}) collective-permute-start(bf16[2,1,1,128,512]{4,3,0,2,1:T(8,128)(2,1)S(1)} %dynamic-slice_convert_fusion.3), channel_id=1, source_target_pairs={{0,1},{1,0},{2,3},{3,2},{4,5},{5,4},{6,7},{7,6},{8,9},{9,8},{10,11... | collective-permute-start | bytes 786440 | tf_op jit(solution)/shard_map/ppermute | solution.py:617
  162.4 11.8 %collective-permute-start.30 = (bf16[2,1,1,128,512]{4,3,0,2,1:T(8,128)(2,1)S(1)}, bf16[2,1,1,128,512]{4,3,0,2,1:T(8,128)(2,1)S(1)}, u32[]{:S(2)}, u32[]{:S(2)}) collective-permute-start(bf16[2,1,1,128,512]{4,3,0,2,1:T(8,128)(2,1)S(1)} %dynamic-slice_convert_fusion.4), channel_id=1, source_target_pairs={{0,4},{2,6},{4,0},{6,2},{8,12},{10,14},{12,8},{14,10},{16,20},{18,... | collective-permute-start | bytes 786440 | tf_op jit(solution)/shard_map/ppermute | solution.py:617
  165.1 11.2 %collective-permute-start.33 = (bf16[1,2,1,128,512]{4,3,0,2,1:T(8,128)(2,1)S(1)}, bf16[1,2,1,128,512]{4,3,0,2,1:T(8,128)(2,1)S(1)}, u32[]{:S(2)}, u32[]{:S(2)}) collective-permute-start(bf16[1,2,1,128,512]{4,3,0,2,1:T(8,128)(2,1)S(1)} %dynamic-slice_convert_fusion.1), channel_id=1, source_target_pairs={{0,4},{2,6},{4,0},{6,2},{8,12},{10,14},{12,8},{14,10},{16,20},{18,... | collective-permute-start | bytes 786440 | tf_op jit(solution)/shard_map/ppermute | solution.py:617
  166.2 10.1 %collective-permute-start.32 = (bf16[1,1,2,128,512]{4,3,0,2,1:T(8,128)(2,1)S(1)}, bf16[1,1,2,128,512]{4,3,0,2,1:T(8,128)(2,1)S(1)}, u32[]{:S(2)}, u32[]{:S(2)}) collective-permute-start(bf16[1,1,2,128,512]{4,3,0,2,1:T(8,128)(2,1)S(1)} %dynamic-slice_convert_fusion.2), channel_id=1, source_target_pairs={{0,1},{1,0},{2,3},{3,2},{4,5},{5,4},{6,7},{7,6},{8,9},{9,8},{10,11... | collective-permute-start | bytes 786440 | tf_op jit(solution)/shard_map/ppermute | solution.py:617
  177.4 35.4 %collective-permute-start.49 = (bf16[256,512]{1,0:T(8,128)(2,1)S(1)}, bf16[256,512]{1,0:T(8,128)(2,1)S(1)}, u32[]{:S(2)}, u32[]{:S(2)}) collective-permute-start(bf16[256,512]{1,0:T(8,128)(2,1)S(1)} %dynamic-slice_convert_fusion), channel_id=1, source_target_pairs={{0,1},{1,0},{2,3},{3,2},{4,5},{5,4},{6,7},{7,6},{8,9},{9,8},{10,11... | collective-permute-start | bytes 786440 | tf_op jit(solution)/shard_map/ppermute | solution.py:617
  178.2 13.7 %collective-permute-start.39 = (bf16[4,64,512]{2,1,0:T(8,128)(2,1)S(1)}, bf16[4,64,512]{2,1,0:T(8,128)(2,1)S(1)}, u32[]{:S(2)}, u32[]{:S(2)}) collective-permute-start(bf16[4,64,512]{2,1,0:T(8,128)(2,1)S(1)} %fusion.6), channel_id=1, source_target_pairs={{0,8},{2,10},{4,12},{6,14},{8,0},{10,2},{12,4},{14,6},{16,24},{18,... | collective-permute-start | bytes 786440 | tf_op jit(solution)/shard_map/ppermute | solution.py:617
  189.4 8.4 %collective-permute-start.37 = (bf16[2,64,512]{2,1,0:T(8,128)(2,1)S(1)}, bf16[2,64,512]{2,1,0:T(8,128)(2,1)S(1)}, u32[]{:S(2)}, u32[]{:S(2)}) collective-permute-start(bf16[2,64,512]{2,1,0:T(8,128)(2,1)S(1)} %fusion.13), channel_id=1, source_target_pairs={{0,8},{2,10},{4,12},{6,14},{8,0},{10,2},{12,4},{14,6},{16,24},{18,... | collective-permute-start | bytes 393224 | tf_op jit(solution)/shard_map/ppermute | solution.py:617
  192.0 17.1 %collective-permute-start.40 = (bf16[4,64,512]{2,1,0:T(8,128)(2,1)S(1)}, bf16[4,64,512]{2,1,0:T(8,128)(2,1)S(1)}, u32[]{:S(2)}, u32[]{:S(2)}) collective-permute-start(bf16[4,64,512]{2,1,0:T(8,128)(2,1)S(1)} %fusion.17), channel_id=1, source_target_pairs={{0,16},{2,18},{4,20},{6,22},{8,24},{10,26},{12,28},{14,30},{16,0},... | collective-permute-start | bytes 786440 | tf_op jit(solution)/shard_map/ppermute | solution.py:617
  197.9 15.1 %collective-permute-start.38 = (bf16[2,64,512]{2,1,0:T(8,128)(2,1)S(1)}, bf16[2,64,512]{2,1,0:T(8,128)(2,1)S(1)}, u32[]{:S(2)}, u32[]{:S(2)}) collective-permute-start(bf16[2,64,512]{2,1,0:T(8,128)(2,1)S(1)} %fusion.16), channel_id=1, source_target_pairs={{0,16},{2,18},{4,20},{6,22},{8,24},{10,26},{12,28},{14,30},{16,0},... | collective-permute-start | bytes 393224 | tf_op jit(solution)/shard_map/ppermute | solution.py:617
  209.2 9.3 %collective-permute-start.45 = (bf16[4,64,512]{2,1,0:T(8,128)(2,1)S(1)}, bf16[4,64,512]{2,1,0:T(8,128)(2,1)S(1)}, u32[]{:S(2)}, u32[]{:S(2)}) collective-permute-start(bf16[4,64,512]{2,1,0:T(8,128)(2,1)S(1)} %reduce-precision_convert_fusion.1), channel_id=1, source_target_pairs={{0,8},{2,10},{4,12},{6,14},{8,0},{10,2},{12,4},{14,6},{16,24},{18,... | collective-permute-start | bytes 786440 | tf_op jit(solution)/shard_map/ppermute | solution.py:617
  209.6 10.2 %collective-permute-start.46 = (bf16[4,64,512]{2,1,0:T(8,128)(2,1)S(1)}, bf16[4,64,512]{2,1,0:T(8,128)(2,1)S(1)}, u32[]{:S(2)}, u32[]{:S(2)}) collective-permute-start(bf16[4,64,512]{2,1,0:T(8,128)(2,1)S(1)} %reduce-precision_convert_fusion.1), channel_id=1, source_target_pairs={{0,4},{2,6},{4,0},{6,2},{8,12},{10,14},{12,8},{14,10},{16,20},{18,... | collective-permute-start | bytes 786440 | tf_op jit(solution)/shard_map/ppermute | solution.py:617
  210.5 14.4 %collective-permute-start.47 = (bf16[4,64,512]{2,1,0:T(8,128)(2,1)S(1)}, bf16[4,64,512]{2,1,0:T(8,128)(2,1)S(1)}, u32[]{:S(2)}, u32[]{:S(2)}) collective-permute-start(bf16[4,64,512]{2,1,0:T(8,128)(2,1)S(1)} %reduce-precision_convert_fusion.1), channel_id=1, source_target_pairs={{0,12},{2,14},{4,8},{6,10},{8,4},{10,6},{12,0},{14,2},{16,28},{18,... | collective-permute-start | bytes 786440 | tf_op jit(solution)/shard_map/ppermute | solution.py:617
  212.9 15.2 %collective-permute-start.50 = (bf16[256,512]{1,0:T(8,128)(2,1)S(1)}, bf16[256,512]{1,0:T(8,128)(2,1)}, u32[]{:S(2)}, u32[]{:S(2)}) collective-permute-start(bf16[256,512]{1,0:T(8,128)(2,1)S(1)} %reduce-precision_convert_fusion), channel_id=1, source_target_pairs={{0,2},{2,0},{4,6},{6,4},{8,10},{10,8},{12,14},{14,12},{16,18},{18,... | collective-permute-start | bytes 786440 | tf_op jit(solution)/shard_map/ppermute | solution.py:617
  213.0 12.9 %collective-permute-start.41 = (bf16[2,64,512]{2,1,0:T(8,128)(2,1)S(1)}, bf16[2,64,512]{2,1,0:T(8,128)(2,1)S(1)}, u32[]{:S(2)}, u32[]{:S(2)}) collective-permute-start(bf16[2,64,512]{2,1,0:T(8,128)(2,1)S(1)} %reduce-precision_convert_fusion.2), channel_id=1, source_target_pairs={{0,8},{2,10},{4,12},{6,14},{8,0},{10,2},{12,4},{14,6},{16,24},{18,... | collective-permute-start | bytes 393224 | tf_op jit(solution)/shard_map/ppermute | solution.py:617
  (43 other events, 349.4 us)

commit v3 on v2

--- a/solution.py
+++ b/solution.py
@@ -16,6 +16,8 @@
 
 SQRT_HALF = 0.7071067811865476
 VMEM_LIMIT = 40 * 2**20
+CONV_TILE, CONV_SUBS = 768, 1
+HIDDEN_TILE, HIDDEN_SUBS = 768, 1
 NT = ((1,), (1,))
 TN = ((0,), (0,))
 bf16 = jnp.bfloat16
@@ -149,18 +151,12 @@
         copy.wait()
 
 
-def own_kernel(*refs):
-    count = len(refs) // 2
-    for shard, low in zip(refs[:count], refs[count:], strict=True):
-        low[...] = shard[...].astype(bf16)
-
-
 def assemble(place, members, layout, shards, sources, fulls):
     member = place[2]
     for shard, full, (row, column) in zip(shards, fulls, layout, strict=True):
         rows, width = shard.shape
         part = rows // 4
-        full[pl.ds(pl.multiple_of(member * rows, part), rows)] = shard[...]
+        full[pl.ds(pl.multiple_of(member * rows, part), rows)] = shard[...].astype(bf16)
         for j in range(1, members):
             for source, quarter in sources:
                 start = pl.multiple_of((member ^ j) * rows + quarter * part, part)
@@ -276,8 +272,7 @@
 
     @pl.when(first)
     def _():
-        shard = own_proj.shape[0]
-        own = [own_conv.at[pl.ds(t * shard, shard)] for t in range(3)]
+        own = [own_conv.at[t] for t in range(3)]
         full = [w_conv.at[pl.ds(t * width, width)] for t in range(3)]
         sources = quarters_of(place, (here, over, core, both), 4)
         assemble(place, members, layout, [*own, own_proj], sources, [*full, w_proj])
@@ -331,28 +326,36 @@
 
     base = pl.multiple_of(j * tile, tile)
 
-    def at(ref, offset):
-        return ref[i, pl.ds(base + offset, tile)]
-
-    act, d_gated, branch, alive, left, right = body(
-        at(hidden, HALO),
-        at(hidden, HALO + DILATION),
-        at(hidden, HALO + 2 * DILATION),
-        masks[0, :, 0:128],
-        masks[0, :, 128:256],
-        masks[0, :, 256:384],
-        res[0],
-        skip[0],
-    )
-    d_conv[i, pl.ds(base + HALO, tile), :width] = left
-    d_conv[i, pl.ds(base + HALO, tile), width:] = right
-    gated_rows = (act * gain + shift).astype(bf16)
-    columns[:, :width] += jnp.sum((d_gated * act).reshape(tile // 8, 8, width), axis=0)
-    columns[:, width:] += jnp.sum(d_gated.reshape(tile // 8, 8, width), axis=0)
-    part = dotf(gated_rows, branch, TN)
-    out = dotf(gated_rows, w_proj[...])
-    res_out[0] = ((frames[0].astype(f32) + out[:, :width]) * (SQRT_HALF * alive)).astype(bf16)
-    skip_out[0] = (out[:, width:] * alive).astype(bf16)
+    size = tile // CONV_SUBS
+    gated_all, branch_all = [], []
+    for low_row in range(0, tile, size):
+        part_rows = slice(low_row, low_row + size)
+
+        def at(ref, offset, low_row=low_row):
+            return ref[i, pl.ds(base + offset + low_row, size)]
+
+        act, d_gated, branch, alive, left, right = body(
+            at(hidden, HALO),
+            at(hidden, HALO + DILATION),
+            at(hidden, HALO + 2 * DILATION),
+            masks[0, part_rows, 0:128],
+            masks[0, part_rows, 128:256],
+            masks[0, part_rows, 256:384],
+            res[0, part_rows],
+            skip[0, part_rows],
+        )
+        d_conv[i, pl.ds(base + HALO + low_row, size), :width] = left
+        d_conv[i, pl.ds(base + HALO + low_row, size), width:] = right
+        gated_rows = (act * gain + shift).astype(bf16)
+        columns[:, :width] += jnp.sum((d_gated * act).reshape(size // 8, 8, width), axis=0)
+        columns[:, width:] += jnp.sum(d_gated.reshape(size // 8, 8, width), axis=0)
+        out = dotf(gated_rows, w_proj[...])
+        frame_rows = frames[0, part_rows].astype(f32)
+        res_out[0, part_rows] = ((frame_rows + out[:, :width]) * (SQRT_HALF * alive)).astype(bf16)
+        skip_out[0, part_rows] = (out[:, width:] * alive).astype(bf16)
+        gated_all.append(gated_rows)
+        branch_all.append(branch)
+    part = dotf(jnp.concatenate(gated_all, axis=0), jnp.concatenate(branch_all, axis=0), TN)
 
     @pl.when(first)
     def _():
@@ -430,20 +433,33 @@
     def _():
         fetch(now + 1).start()
 
-    gain = dotf(cond[0], gain_cond[...]) + dotf(hots[0], gain_step[...])
     fetch(now).wait()
     slot = now % 2
-    d_hidden = (
-        dotf(window[slot, 2 * DILATION :] * lanes(masks[0, :, 128:256], 2 * width), w_conv[0], NT)
-        + dotf(window[slot, DILATION : DILATION + tile], w_conv[1], NT)
-        + dotf(window[slot, 0:tile] * lanes(masks[0, :, 0:128], 2 * width), w_conv[2], NT)
-    )
-    alive = lanes(masks[0, :, 256:384].astype(f32), width)
-    grad_frames[0] = res[0].astype(f32) * (SQRT_HALF * alive) + d_hidden * (1.0 + gain)
-    d_film = jnp.concatenate(
-        [(d_hidden * frames[0].astype(f32)).astype(bf16), d_hidden.astype(bf16)], axis=1
-    )
-    part = dotf(jnp.concatenate([cond[0], hots[0]], axis=1), d_film, TN)
+    size = tile // HIDDEN_SUBS
+    films = []
+    for low_row in range(0, tile, size):
+        part_rows = slice(low_row, low_row + size)
+        gain = dotf(cond[0, part_rows], gain_cond[...]) + dotf(hots[0, part_rows], gain_step[...])
+        taps = []
+        for tap, lane in ((2, 0), (1, None), (0, 128)):
+            start = low_row + (2 - tap) * DILATION
+            rows = window[slot, start : start + size]
+            if lane is not None:
+                rows = rows * lanes(masks[0, part_rows, lane : lane + 128], 2 * width)
+            taps.append(dotf(rows, w_conv[tap], NT))
+        d_hidden = taps[0] + taps[1] + taps[2]
+        alive = lanes(masks[0, part_rows, 256:384].astype(f32), width)
+        grad_frames[0, part_rows] = res[0, part_rows].astype(f32) * (SQRT_HALF * alive) + d_hidden * (
+            1.0 + gain
+        )
+        films.append(
+            jnp.concatenate(
+                [(d_hidden * frames[0, part_rows].astype(f32)).astype(bf16), d_hidden.astype(bf16)], axis=1
+            )
+        )
+    part = dotf(
+        jnp.concatenate([cond[0], hots[0]], axis=1), jnp.concatenate(films, axis=0), TN
+    )
 
     @pl.when(now == 0)
     def _():
@@ -472,20 +488,24 @@
     return [((column >= h * size) & (column < (h + 1) * size)).astype(f32) for h in range(HEADS)]
 
 
-def attention_kernel(groups, members, layout, place, *refs):
-    pieces = refs[:groups]
-    queries, *parts = refs[groups : groups + 10]
-    film, prompt, probs, keys, values, spread, summaries, totals, *fulls = refs[groups + 10 :]
-    assemble(place, members, layout, parts[:5], quarters_of(place, parts[5:]), fulls)
-    w_key, w_value, w_query, w_out, w_film = fulls
-    _, micro, shard, width = pieces[0].shape
+def attention_kernel(
+    members, layout, place, every_prompt, queries, own_key, own_value, own_query, own_out, own_film, here, over, core, both,
+    film, prompt, probs, keys, values, spread, summaries, totals, w_key, w_value, w_query, w_out, w_film,
+):
+    count, micro, shard, width = every_prompt.shape
+    assemble(
+        place,
+        members,
+        layout,
+        (own_key, own_value, own_query, own_out, own_film),
+        quarters_of(place, (here, over, core, both)),
+        (w_key, w_value, w_query, w_out, w_film),
+    )
     masks = head_masks(width)
     scale = 1.0 / math.sqrt(width // HEADS)
-    for g, four in enumerate(pieces):
-        for k in range(4):
-            start = pl.multiple_of((place[1] ^ (4 * g + k)) * shard, shard)
-            for i in range(micro):
-                prompt[i, pl.ds(start, shard)] = four[k, i]
+    for d in range(count):
+        for i in range(micro):
+            prompt[i, d * shard : (d + 1) * shard] = every_prompt[d, i]
     query = dotf(queries[...], w_query[...])
     spread[...] = jnp.concatenate([(query * mask).astype(bf16) for mask in masks], axis=0)
     for i in range(micro):
@@ -757,6 +777,7 @@
     wide = 2 * width
     tile = rows // 3 if rows % 48 == 0 else rows
     tiles = (MICRO, rows // tile)
+    conv_tile, hidden_tile = CONV_TILE, HIDDEN_TILE
     tm_count, tm_index = lax.axis_size("tm"), lax.axis_index("tm")
     members, member = lax.axis_size("fsdp"), lax.axis_index("fsdp")
     shard_rows = w_cond.shape[0]
@@ -795,7 +816,7 @@
         [hbm(a) for a in (frames, cond, res, skip)],
         [new_fixed(edge, bf16), new_fixed(edge, bf16)],
         "edges",
-        1.1,
+        1,
         scratch=[pltpu.SemaphoreType.DMA((8,))],
         after=[first],
     )
@@ -821,28 +842,10 @@
         5,
         after=[second],
     )
-    own = prompt[:, 0]
-    across = swapped(own, "tm", 2)
-    near = jnp.stack([own, swapped(own, "tm", 1), across, swapped(across, "tm", 1)])
-    own_cond, own_step, *own_second, own_conv, own_proj = call(
-        own_kernel,
-        (1,),
-        [
-            whole(w)
-            for w in (w_cond, w_step, w_key, w_value, w_query, w_out, w_film, w_conv.reshape(-1, wide), w_proj)
-        ],
-        [new_fixed(w.shape, bf16) for w in (w_cond, w_step)]
-        + [
-            new(w.shape, bf16)
-            for w in (w_key, w_value, w_query, w_out, w_film, w_conv.reshape(-1, wide), w_proj)
-        ],
-        "own_shards",
-        4,
-        after=[mask_ends, near],
-    )
-    first_quarters = gathered(first, members, early=[mask_ends], late=[own_cond])
-    pieces = [near] + [swapped(near, "tm", 4 * k) for k in range(1, tm_count // 4)]
-    full_queries = queries.astype(bf16)
+    first_quarters = gathered(first, members, early=[second], late=[mask_ends])
+    every_prompt = jnp.broadcast_to(behind(prompt, second)[None, :, 0], (tm_count, MICRO, *prompt.shape[2:]))
+    every_prompt = lax.all_to_all(every_prompt, "tm", 0, 0)
+    full_queries = behind(queries, second).astype(bf16)
     for bit in bits_of("fsdp"):
         full_queries = doubled(full_queries, swapped(full_queries, "fsdp", bit), "fsdp", bit, 0)
 
@@ -861,8 +864,8 @@
             blocks(hot, tile),
             whole(hot_ends),
             whole(embed),
-            fixed(own_cond),
-            fixed(own_step),
+            whole(w_cond),
+            whole(w_step),
             *[fixed(q) for q in first_quarters],
         ],
         [
@@ -871,23 +874,23 @@
             new((hots, width), bf16),
         ],
         "film",
-        10,
+        1,
         scratch=[
             pltpu.VMEM((width, wide), bf16),
             pltpu.VMEM((width, wide), bf16),
             pltpu.VMEM((hots, wide), bf16),
         ],
-        after=[*pieces, full_queries],
-    )
-    second_quarters = gathered(second, members, early=[own_cond], late=[gain_step])
-    third_quarters = gathered(third, members, early=[own_cond], late=[gain_step], bit_2=4)
+        after=[full_queries],
+    )
+    second_quarters = gathered(second, members, early=[mask_ends], late=[gain_step])
+    third_quarters = gathered(third, members, early=[mask_ends], late=[gain_step], bit_2=4)
     length = tm_count * prompt.shape[2]
     film, prompt_full, probs, keys, values, spread, summaries, totals, *fulls = call(
-        functools.partial(attention_kernel, len(pieces), members, layout_2),
+        functools.partial(attention_kernel, members, layout_2),
         (1,),
         [scalars(place)]
-        + [whole(a) for a in (*pieces, full_queries)]
-        + [whole(a) for a in own_second]
+        + [whole(a) for a in (every_prompt, full_queries)]
+        + [whole(w) for w in (w_key, w_value, w_query, w_out, w_film)]
         + [fixed(a) for a in second_quarters],
         [
             new((MICRO, 8, wide)),
@@ -908,21 +911,21 @@
     full_key, full_value, full_query, full_out, full_film = fulls
 
     d_conv, d_conv_copy, conv_copy, sums, proj_keep, proj_send, res_out, skip_out = call(
-        functools.partial(conv_kernel, tile, members, layout_3),
-        tiles,
+        functools.partial(conv_kernel, conv_tile, members, layout_3),
+        (MICRO, rows // conv_tile),
         [
             scalars(place),
             fixed(hidden),
-            blocks(masks, tile),
+            blocks(masks, conv_tile),
             whole(mask_ends),
-            blocks(frames, tile),
-            blocks(res, tile),
-            blocks(skip, tile),
+            blocks(frames, conv_tile),
+            blocks(res, conv_tile),
+            blocks(skip, conv_tile),
             whole(low),
             whole(high),
             whole(film),
-            whole(own_conv),
-            whole(own_proj),
+            whole(w_conv),
+            whole(w_proj),
             *[fixed(q) for q in third_quarters],
         ],
         [
@@ -932,8 +935,8 @@
             new((8, wide)),
             new_fixed((1, width, width)),
             new_fixed((1, width, width), bf16),
-            new_blocks((MICRO, rows, width), bf16, tile),
-            new_blocks((MICRO, rows, width), bf16, tile),
+            new_blocks((MICRO, rows, width), bf16, conv_tile),
+            new_blocks((MICRO, rows, width), bf16, conv_tile),
         ],
         "conv",
         32,
@@ -968,13 +971,13 @@
     sums = sums + behind(sums_far, *conv_proj.aways)
     sums_far = swapped(sums, "tm", 4)
     grad_frames, keep, send = call(
-        functools.partial(hidden_grad_kernel, tile),
-        tiles,
+        functools.partial(hidden_grad_kernel, hidden_tile),
+        (MICRO, rows // hidden_tile),
         [scalars(place), hbm(d_conv_copy)]
-        + [blocks(a, tile) for a in (masks, hot, frames, res, cond)]
+        + [blocks(a, hidden_tile) for a in (masks, hot, frames, res, cond)]
         + [whole(a) for a in (conv_copy.reshape(3, width, wide), gain_cond, gain_step, embed)],
         [
-            new_blocks((MICRO, rows, width), f32, tile),
+            new_blocks((MICRO, rows, width), f32, hidden_tile),
             new_fixed((2, width, width)),
             new_fixed((2, width, width), bf16),
         ],
@@ -982,7 +985,7 @@
         27,
         scratch=[
             pltpu.VMEM((width + hots, wide), f32),
-            pltpu.VMEM((2, tile + 2 * DILATION, wide), bf16),
+            pltpu.VMEM((2, hidden_tile + 2 * DILATION, wide), bf16),
             pltpu.SemaphoreType.DMA((2,)),
         ],
         after=[*conv_proj.aways, sums],
@@ -996,7 +999,17 @@
     sums_far = swapped(sums, "tm", bits_of("tm")[-1])
     received = behind(received, *conv_proj.aways, sums)
     cond_step = Reduction([([keep[:1]], [received[:1]]), ([keep[1:]], [received[1:]])])
-    sums = sums + behind(sums_far, *cond_step.aways)
+    sums_far = behind(sums_far, *cond_step.aways)
+    conv_proj.absorb_all(*cond_step.aways)
+    conv_proj.start_third()
+    cond_step.absorb_all(conv_proj.away)
+    cond_step.start_third()
+    conv_proj.fold(cond_step.away)
+    first_bit, *more_bits = bits_of("tm")[3:]
+    conv_proj.start_double(first_bit)
+    cond_step.fold(conv_proj.away)
+    cond_step.start_double(first_bit)
+    sums = sums + behind(sums_far, cond_step.away)
     grad_prompt, pair, small = call(
         attention_grad_kernel,
         (1,),
@@ -1013,13 +1026,7 @@
         7,
         scratch=[pltpu.VMEM((MICRO, length, wide), bf16)],
     )
-    small, pair, *raw = lax.optimization_barrier((small, pair, *conv_proj.raw, *cond_step.raw))
-    conv_proj.raw, cond_step.raw = raw[:2], raw[2:]
-    conv_proj.absorb_all()
-    conv_proj.start_third()
-    cond_step.absorb_all(conv_proj.away)
-    cond_step.start_third()
-
+    small, pair, conv_proj.raw = lax.optimization_barrier((small, pair, conv_proj.raw))
     for bit in reversed(bits_of("fsdp")):
         away, pair = parted(pair, "fsdp", bit, 0)
         pair = pair + swapped(away, "fsdp", bit).astype(f32)
@@ -1058,14 +1065,14 @@
         )
 
     flat, tall = (shard_rows, wide), (3, shard_rows, wide)
+    for bit in more_bits:
+        conv_proj.fold(cond_step.away)
+        conv_proj.start_double(bit)
+        cond_step.fold(conv_proj.away)
+        cond_step.start_double(bit)
     conv_proj.fold()
-    for bit in bits_of("tm")[3:]:
-        conv_proj.start_double(bit)
-        cond_step.fold(grad_queries)
-        cond_step.start_double(bit)
-        conv_proj.fold(cond_step.away)
     conv_proj.start_gather()
-    cond_step.fold(conv_proj.away)
+    cond_step.fold(conv_proj.away, grad_queries)
     cond_step.start_gather()
     conv_proj = conv_proj.gather()
     cond_step = cond_step.gather()

time: 237 us -> 222 us (0.937)
  waiting for transfers between devices: 42.1 us -> 35.1 us
  Pallas kernels: 119 us -> 114 us
  starting transfers between devices: 51.2 us -> 47.6 us
    ppermute x49 -> x43, starting transfers between devices: 48.6 us -> 38.2 us  [swapped(): return lax.ppermute(array, axis, [(i, i ^ bit) for i in range(count)])]
    ppermute x49 -> x43, waiting for transfers between devices: 42 us -> 35.1 us  [swapped(): return lax.ppermute(array, axis, [(i, i ^ bit) for i in range(count)])]
    all_to_all x0 -> x1, starting transfers between devices: none -> 6.59 us  [per_device(): every_prompt = lax.all_to_all(every_prompt, 'tm', 0, 0)]
    pallas_call x14 -> x13, Pallas kernels: 119 us -> 114 us  [call(): pl.pallas_call(body, grid=grid, in_specs=[spec for _, spec in ins] + [ANY...]
    unnamed x50 -> x46, local copies, waits for them, and re-layouts: 6.68 us -> 7.87 us
  transfers between devices with their start and end apart: 51 -> 46, of which waited for: 14 -> 16; matrix products, arithmetic and copies ran while one was open for 6% -> 7% of each run, Pallas kernels for 30% -> 29%
where the time goes in v3:
time: 222 us; the launch traced here: 221 us
  Pallas kernels  114 us (51%)
  starting transfers between devices  47.6 us (21%)
  waiting for transfers between devices  35.1 us (16%)
  other arithmetic  13.1 us (6%)
  local copies, waits for them, and re-layouts  10.4 us (5%)
    pallas_call x13, Pallas kernels, call(): pl.pallas_call(body, grid=grid, in_specs=[spec for _, spec in ins] + [ANY...  114 us
    ppermute x43, starting transfers between devices, swapped(): return lax.ppermute(array, axis, [(i, i ^ bit) for i in range(count)])  38.2 us
    ppermute x43, waiting for transfers between devices, swapped(): return lax.ppermute(array, axis, [(i, i ^ bit) for i in range(count)])  35.1 us
    unnamed x46, local copies, waits for them, and re-layouts  7.87 us
    all_to_all x1, starting transfers between devices, per_device(): every_prompt = lax.all_to_all(every_prompt, 'tm', 0, 0)  6.59 us
    add x4, other arithmetic, __init__(): k + r.astype(f32)  5.83 us
  transfers between devices with their start and end apart: 46, of which 16 were waited for; matrix products, arithmetic and copies ran while one was open for 7% of the time, Pallas kernels for 29%

profile of v3, /device:TPU:0, one launch (start us, length us, event | category | flops | bytes accessed | tf_op | source)
XLA Modules:
  0.0 221.2 jit_solution(17278035320465662355)
XLA Ops:
  0.8 1.7 pack_first.1.refs_4_
  2.5 3.0 %collective-permute-start.2 = (bf16[1,128,1024]{2,1,0:T(8,128)(2,1)S(1)}, bf16[1,128,1024]{2,1,0:T(8,128)(2,1)S(1)}, u32[]{:S(2)}, u32[]{:S(2)}) collective-permute-start(bf16[1,128,1024]{2,1,0:T(8,128)(2,1)S(1)} %bitcast.57), channel_id=1, source_target_pairs={{0,1},{1,0},{2,3},{3,2},{4,5},{5,4},{6,7},{7,6},{8,9},{9,8},{10,11... | collective-permute-start | bytes 786440 | tf_op jit(solution)/shard_map/ppermute | solution.py:637
  8.0 2.3 %pack_rest.1 = (bf16[192,1024]{1,0:T(8,128)(2,1)S(1)}, bf16[256,1024]{1,0:T(8,128)(2,1)S(1)}) custom-call(s32[5]{0:T(128)S(1)} %stack.23.refs_0_, f32[256,512]{1,0:T(8,128)} %refs_3_.3, f32[256,512]{1,0:T(8,128)} %refs_4_.3, f32[256,512]{1,0:T(8,128)} %refs_5_.3, f32[256,512]{1,0:T(8,128)} %refs_6_.3, f32[256,1024]{1,0:T(8,128)} %refs_7_.3, ...), custom_call_target="tpu_custom_call" | custom-call | flops 2000000000 | bytes 4096 | tf_op jit(solution)/shard_map/pack_rest/pallas_call | solution.py:68
  10.4 2.0 collective-permute-start.7
  13.2 6.6 %all-to-all-start = ((bf16[16,2,16,512]{3,2,1,0:T(8,128)(2,1)}), bf16[16,2,16,512]{3,2,1,0:T(8,128)(2,1)}, u32[]{:S(2)}, u32[]{:S(2)}) async-start(bf16[16,2,16,512]{3,2,1,0:T(8,128)(2,1)} %broadcast_in_dim.35), calls=%async_computation | async-start | bytes 1048576 | tf_op jit(solution)/shard_map/all_to_all | solution.py:847
  20.4 5.1 %masks.1 = (bf16[2,1536,384]{2,1,0:T(8,128)(2,1)}, bf16[2,1536,128]{2,1,0:T(8,128)(2,1)}, bf16[2,64,384]{2,1,0:T(8,128)(2,1)}, bf16[2,64,128]{2,1,0:T(8,128)(2,1)}) custom-call(s32[5]{0:T(128)S(1)} %stack.23.refs_0_, s32[2,30]{1,0:T(2,128)S(1)} %bitcast.60, bf16[192,1024]{1,0:T(8,128)(2,1)S(1)} %get-tuple-element.93.refs_2_), custom_call_target="tpu_custom_call" | custom-call | flops 5000000000 | bytes 4096 | tf_op jit(solution)/shard_map/masks/pallas_call | solution.py:68
  25.7 1.8 collective-permute-start.3
  29.9 6.1 %collective-permute-done.3.refs_11_ = bf16[1,128,1024]{2,1,0:T(8,128)(2,1)S(1)} collective-permute-done((bf16[1,128,1024]{2,1,0:T(8,128)(2,1)S(1)}, bf16[1,128,1024]{2,1,0:T(8,128)(2,1)S(1)}, u32[]{:S(2)}, u32[]{:S(2)}) %collective-permute-start.3) | collective-permute-done | bytes 262176 | tf_op jit(solution)/shard_map/ppermute | solution.py:637
  36.0 1.9 collective-permute-start.8
  38.2 3.1 %collective-permute-start.12 = (bf16[1,256,1024]{2,1,0:T(8,128)(2,1)S(1)}, bf16[1,256,1024]{2,1,0:T(8,128)(2,1)S(1)}, u32[]{:S(2)}, u32[]{:S(2)}) collective-permute-start(bf16[1,256,1024]{2,1,0:T(8,128)(2,1)S(1)} %collective-permute-done.11.refs_12_), channel_id=1, source_target_pairs={{0,8},{2,10},{4,12},{6,14},{8,0},{10,2},{12,4},{14,6},{16,24},{18,... | collective-permute-start | bytes 1572872 | tf_op jit(solution)/shard_map/ppermute | solution.py:637
  42.1 10.7 %film.1 = (bf16[2,1632,512]{2,1,0:T(8,128)(2,1)S(1)}, bf16[512,512]{1,0:T(8,128)(2,1)}, bf16[128,512]{1,0:T(8,128)(2,1)}) custom-call(s32[5]{0:T(128)S(1)} %stack.23.refs_0_, bf16[2,1536,512]{2,1,0:T(8,128)(2,1)} %bitcast.62, bf16[2,1536,512]{2,1,0:T(8,128)(2,1)} %bitcast.66, bf16[4,2,32,512]{3,2,1,0:T(8,128)(2,1)} %copy-done.16, ...), custom_call_target="tpu_custom_call" | custom-call | flops 1000000000 | bytes 4096 | tf_op jit(solution)/shard_map/film/pallas_call | solution.py:68
  52.8 1.7 copy-done.4
  57.9 5.8 %attention.1 = (f32[2,8,1024]{2,1,0:T(8,128)}, bf16[2,256,512]{2,1,0:T(8,128)(2,1)}, f32[2,256,256]{2,1,0:T(8,128)}, bf16[2,256,512]{2,1,0:T(8,128)(2,1)}, bf16[...) custom-call(s32[5]{0:T(128)S(1)} %stack.23.refs_0_, ...), custom_call_target="tpu_custom_call" | custom-call | flops 5000000000 | bytes 4096 | tf_op jit(solution)/shard_map/attention/pallas_call | solution.py:68
  63.7 1.9 copy-done.5
  65.7 32.8 %conv.1 = (bf16[2,1600,1024]{2,1,0:T(8,128)(2,1)S(1)}, bf16[2,1600,1024]{2,1,0:T(8,128)(2,1)}, bf16[1536,1024]{1,0:T(8,128)(2,1)}, f32[8,1024]{1,0:T(8,128)}, f3...) custom-call(s32[5]{0:T(128)S(1)} %stack.23.refs_0_, ...), custom_call_target="tpu_custom_call" | custom-call | flops 32000000000 | bytes 4096 | tf_op jit(solution)/shard_map/conv/pallas_call | solution.py:68
  99.5 13.2 %conv_grad.1 = (f32[3,512,512]{2,1,0:T(8,128)S(1)}, bf16[3,512,512]{2,1,0:T(8,128)(2,1)}) custom-call(s32[5]{0:T(128)} %copy-done.2, bf16[2,1632,512]{2,1,0:T(8,128)(2,1)S(1)} %copy-done.5, bf16[2,1536,384]{2,1,0:T(8,128)(2,1)} %get-tuple-element.101.refs_2_, bf16[2,1600,1024]{2,1,0:T(8,128)(2,1)S(1)} %get-tuple-element.115.refs_3_), custom_call_target="tpu_custom_call" | custom-call | flops 13500000256 | bytes 4096 | tf_op jit(solution)/shard_map/conv_grad/pallas_call | solution.py:68
  113.4 2.9 %collective-permute-done.17 = f32[8,1024]{1,0:T(8,128)S(1)} collective-permute-done((f32[8,1024]{1,0:T(8,128)S(1)}, f32[8,1024]{1,0:T(8,128)S(1)}, u32[]{:S(2)}, u32[]{:S(2)}) %collective-permute-start.17) | collective-permute-done | bytes 32800 | tf_op jit(solution)/shard_map/ppermute | solution.py:637
  125.4 25.8 %hidden_grad.1 = (f32[2,1536,512]{2,1,0:T(8,128)}, f32[2,512,512]{2,1,0:T(8,128)S(1)}, bf16[2,512,512]{2,1,0:T(8,128)(2,1)S(1)}) custom-call(s32[5]{0:T(128)S(1)} %copy-done.3, bf16[2,1600,1024]{2,1,0:T(8,128)(2,1)} %get-tuple-element.112.refs_1_, bf16[2,1536,384]{2,1,0:T(8,128)(2,1)} %get-tuple-element.101.refs_2_, ...), custom_call_target="tpu_custom_call" | custom-call | flops 27000000512 | bytes 4096 | tf_op jit(solution)/shard_map/hidden_grad/pallas_call | solution.py:68
  152.0 2.7 %collective-permute-start.22 = (f32[8,1024]{1,0:T(8,128)S(1)}, f32[8,1024]{1,0:T(8,128)S(1)}, u32[]{:S(2)}, u32[]{:S(2)}) collective-permute-start(f32[8,1024]{1,0:T(8,128)S(1)} %add.160), channel_id=1, source_target_pairs={{0,16},{2,18},{4,20},{6,22},{8,24},{10,26},{12,28},{14,30},{16,0},... | collective-permute-start | bytes 98312 | tf_op jit(solution)/shard_map/ppermute | solution.py:637
  162.5 3.3 %collective-permute-done.26 = bf16[2,1,1,128,512]{4,3,0,2,1:T(8,128)(2,1)S(1)} collective-permute-done((bf16[2,1,1,128,512]{4,3,0,2,1:T(8,128)(2,1)S(1)}, bf16[2,1,1,128,512]{4,3,0,2,1:T(8,128)(2,1)S(1)}, u32[]{:S(2)}, u32[]{:S(2)}) %collective-permute-start.26) | collective-permute-done | bytes 262176 | tf_op jit(solution)/shard_map/ppermute | solution.py:637
  167.0 4.2 %collective-permute-done.28 = bf16[1,2,1,128,512]{4,3,0,2,1:T(8,128)(2,1)S(1)} collective-permute-done((bf16[1,2,1,128,512]{4,3,0,2,1:T(8,128)(2,1)S(1)}, bf16[1,2,1,128,512]{4,3,0,2,1:T(8,128)(2,1)S(1)}, u32[]{:S(2)}, u32[]{:S(2)}) %collective-permute-start.28) | collective-permute-done | bytes 262176 | tf_op jit(solution)/shard_map/ppermute | solution.py:637
  173.8 2.6 %collective-permute-done.29 = bf16[1,1,1,128,512]{4,3,0,2,1:T(8,128)(2,1)S(1)} collective-permute-done((bf16[1,1,1,128,512]{4,3,0,2,1:T(8,128)(2,1)S(1)}, bf16[1,1,1,128,512]{4,3,0,2,1:T(8,128)(2,1)S(1)}, u32[]{:S(2)}, u32[]{:S(2)}) %collective-permute-start.29) | collective-permute-done | bytes 131104 | tf_op jit(solution)/shard_map/ppermute | solution.py:637
  178.3 2.0 collective-permute-start.32
  180.3 3.6 %collective-permute-done.30 = bf16[2,64,512]{2,1,0:T(8,128)(2,1)S(1)} collective-permute-done((bf16[2,64,512]{2,1,0:T(8,128)(2,1)S(1)}, bf16[2,64,512]{2,1,0:T(8,128)(2,1)S(1)}, u32[]{:S(2)}, u32[]{:S(2)}) %collective-permute-start.30) | collective-permute-done | bytes 131104 | tf_op jit(solution)/shard_map/ppermute | solution.py:637
  185.8 6.8 %attention_grad.1 = (f32[2,16,512]{2,1,0:T(8,128)}, f32[512,512]{1,0:T(8,128)}, f32[72,512]{1,0:T(8,128)}) custom-call(s32[5]{0:T(128)S(1)} %copy-done.3, f32[8,1024]{1,0:T(8,128)} %add.177.refs_1_, bf16[2,256,512]{2,1,0:T(8,128)(2,1)} %get-tuple-element.141.refs_2_, f32[2,256,256]{2,1,0:T(8,128)} %get-tuple-element.142.refs_3_, ...), custom_call_target="tpu_custom_call" | custom-call | flops 7000000000 | bytes 4096 | tf_op jit(solution)/shard_map/attention_grad/pallas_call | solution.py:68
  192.6 2.6 %collective-permute-done.32 = bf16[4,64,512]{2,1,0:T(8,128)(2,1)S(1)} collective-permute-done((bf16[4,64,512]{2,1,0:T(8,128)(2,1)S(1)}, bf16[4,64,512]{2,1,0:T(8,128)(2,1)S(1)}, u32[]{:S(2)}, u32[]{:S(2)}) %collective-permute-start.32) | collective-permute-done | bytes 262176 | tf_op jit(solution)/shard_map/ppermute | solution.py:637
  197.1 2.4 %collective-permute-start.39 = (bf16[4,64,512]{2,1,0:T(8,128)(2,1)S(1)}, bf16[4,64,512]{2,1,0:T(8,128)(2,1)S(1)}, u32[]{:S(2)}, u32[]{:S(2)}) collective-permute-start(bf16[4,64,512]{2,1,0:T(8,128)(2,1)S(1)} %reduce-precision_convert_fusion.1), channel_id=1, source_target_pairs={{0,8},{2,10},{4,12},{6,14},{8,0},{10,2},{12,4},{14,6},{16,24},{18,... | collective-permute-start | bytes 786440 | tf_op jit(solution)/shard_map/ppermute | solution.py:637
  202.8 3.5 %small_grads.1 = (f32[16,512]{1,0:T(8,128)}, f32[256,512]{1,0:T(8,128)}, f32[256,512]{1,0:T(8,128)}, f32[256,1024]{1,0:T(8,128)}) custom-call(s32[5]{0:T(128)S(1)} %copy-done.3, f32[2,72,512]{2,1,0:T(8,128)} %pad_maximum_fusion.3.refs_1_, bf16[32,512]{1,0:T(8,128)(2,1)} %copy-done.1, bf16[512,512]{1,0:T(8,128)(2,1)} %get-tuple-element.156.refs_3_), custom_call_target="tpu_custom_call" | custom-call | flops 3300000000 | bytes 4096 | tf_op jit(solution)/shard_map/small_grads/pallas_call | solution.py:68
  210.9 1.7 collective-permute-done.37
  214.4 2.0 select_convert_fusion
  216.4 2.0 join_cond_step.1
  218.4 2.8 %join_conv_proj.1 = (f32[3,256,1024]{2,1,0:T(8,128)}, f32[256,1024]{1,0:T(8,128)}) custom-call(s32[5]{0:T(128)S(1)} %copy-done.3, bf16[4,256,512]{2,1,0:T(8,128)(2,1)S(1)} %pad_maximum_fusion.1.refs_1_, bf16[4,256,512]{2,1,0:T(8,128)(2,1)S(1)} %collective-permute-done.42.refs_2_), custom_call_target="tpu_custom_call" | custom-call | flops 3000000000 | bytes 4096 | tf_op jit(solution)/shard_map/join_conv_proj/pallas_call | solution.py:68
  (169 shorter events, 49.1 us)
Async XLA Ops:
  2.5 23.2 %collective-permute-start.2 = (bf16[1,128,1024]{2,1,0:T(8,128)(2,1)S(1)}, bf16[1,128,1024]{2,1,0:T(8,128)(2,1)S(1)}, u32[]{:S(2)}, u32[]{:S(2)}) collective-permute-start(bf16[1,128,1024]{2,1,0:T(8,128)(2,1)S(1)} %bitcast.57), channel_id=1, source_target_pairs={{0,1},{1,0},{2,3},{3,2},{4,5},{5,4},{6,7},{7,6},{8,9},{9,8},{10,11... | collective-permute-start | bytes 786440 | tf_op jit(solution)/shard_map/ppermute | solution.py:637
  6.7 31.5 %collective-permute-start.1 = (bf16[4,2,32,512]{3,2,1,0:T(8,128)(2,1)S(1)}, bf16[4,2,32,512]{3,2,1,0:T(8,128)(2,1)S(1)}, u32[]{:S(2)}, u32[]{:S(2)}) collective-permute-start(bf16[4,2,32,512]{3,2,1,0:T(8,128)(2,1)S(1)} %get-tuple-element.92), channel_id=1, source_target_pairs={{2,0},{4,2},{6,4},{8,6},{10,8},{12,10},{14,12},{16,14},{18,16},{20... | collective-permute-start | bytes 786440 | tf_op jit(solution)/shard_map/ppermute | solution.py:824
  10.3 25.7 %collective-permute-start.6 = (bf16[16,512]{1,0:T(8,128)(2,1)S(1)}, bf16[16,512]{1,0:T(8,128)(2,1)S(1)}, u32[]{:S(2)}, u32[]{:S(2)}) collective-permute-start(bf16[16,512]{1,0:T(8,128)(2,1)S(1)} %convert_element_type.138), channel_id=1, source_target_pairs={{0,1},{1,0},{2,3},{3,2},{4,5},{5,4},{6,7},{7,6},{8,9},{9,8},{10,11... | collective-permute-start | bytes 49160 | tf_op jit(solution)/shard_map/ppermute | solution.py:637
  10.4 18.1 %collective-permute-start.7 = (bf16[1,192,1024]{2,1,0:T(8,128)(2,1)S(1)}, bf16[1,192,1024]{2,1,0:T(8,128)(2,1)S(1)}, u32[]{:S(2)}, u32[]{:S(2)}) collective-permute-start(bf16[1,192,1024]{2,1,0:T(8,128)(2,1)S(1)} %bitcast.59), channel_id=1, source_target_pairs={{0,1},{1,0},{2,3},{3,2},{4,5},{5,4},{6,7},{7,6},{8,9},{9,8},{10,11... | collective-permute-start | bytes 1179656 | tf_op jit(solution)/shard_map/ppermute | solution.py:637
  13.2 42.5 %all-to-all-start = ((bf16[16,2,16,512]{3,2,1,0:T(8,128)(2,1)}), bf16[16,2,16,512]{3,2,1,0:T(8,128)(2,1)}, u32[]{:S(2)}, u32[]{:S(2)}) async-start(bf16[16,2,16,512]{3,2,1,0:T(8,128)(2,1)} %broadcast_in_dim.35), calls=%async_computation | async-start | bytes 1048576 | tf_op jit(solution)/shard_map/all_to_all | solution.py:847
  19.8 18.1 %collective-permute-start.11 = (bf16[1,256,1024]{2,1,0:T(8,128)(2,1)S(1)}, bf16[1,256,1024]{2,1,0:T(8,128)(2,1)S(1)}, u32[]{:S(2)}, u32[]{:S(2)}) collective-permute-start(bf16[1,256,1024]{2,1,0:T(8,128)(2,1)S(1)} %bitcast.58), channel_id=1, source_target_pairs={{0,1},{1,0},{2,3},{3,2},{4,5},{5,4},{6,7},{7,6},{8,9},{9,8},{10,11... | collective-permute-start | bytes 1572872 | tf_op jit(solution)/shard_map/ppermute | solution.py:637
  25.7 10.3 %collective-permute-start.3 = (bf16[1,128,1024]{2,1,0:T(8,128)(2,1)S(1)}, bf16[1,128,1024]{2,1,0:T(8,128)(2,1)S(1)}, u32[]{:S(2)}, u32[]{:S(2)}) collective-permute-start(bf16[1,128,1024]{2,1,0:T(8,128)(2,1)S(1)} %collective-permute-done.2.refs_10_), channel_id=1, source_target_pairs={{0,4},{2,6},{4,0},{6,2},{8,12},{10,14},{12,8},{14,10},{16,20},{18,... | collective-permute-start | bytes 786440 | tf_op jit(solution)/shard_map/ppermute | solution.py:637
  28.4 12.9 %collective-permute-start = (bf16[4,2,32,512]{3,2,1,0:T(8,128)(2,1)S(1)}, bf16[4,2,32,512]{3,2,1,0:T(8,128)(2,1)S(1)}, u32[]{:S(2)}, u32[]{:S(2)}) collective-permute-start(bf16[4,2,32,512]{3,2,1,0:T(8,128)(2,1)S(1)} %get-tuple-element.91.refs_10_), channel_id=1, source_target_pairs={{0,2},{2,4},{4,6},{6,8},{8,10},{10,12},{12,14},{14,16},{16,18},{18... | collective-permute-start | bytes 786440 | tf_op jit(solution)/shard_map/ppermute | solution.py:823
  36.0 18.5 %collective-permute-start.8 = (bf16[1,192,1024]{2,1,0:T(8,128)(2,1)S(1)}, bf16[1,192,1024]{2,1,0:T(8,128)(2,1)S(1)}, u32[]{:S(2)}, u32[]{:S(2)}) collective-permute-start(bf16[1,192,1024]{2,1,0:T(8,128)(2,1)S(1)} %collective-permute-done.7.refs_8_), channel_id=1, source_target_pairs={{0,4},{2,6},{4,0},{6,2},{8,12},{10,14},{12,8},{14,10},{16,20},{18,... | collective-permute-start | bytes 1179656 | tf_op jit(solution)/shard_map/ppermute | solution.py:637
  38.2 16.8 %collective-permute-start.12 = (bf16[1,256,1024]{2,1,0:T(8,128)(2,1)S(1)}, bf16[1,256,1024]{2,1,0:T(8,128)(2,1)S(1)}, u32[]{:S(2)}, u32[]{:S(2)}) collective-permute-start(bf16[1,256,1024]{2,1,0:T(8,128)(2,1)S(1)} %collective-permute-done.11.refs_12_), channel_id=1, source_target_pairs={{0,8},{2,10},{4,12},{6,14},{8,0},{10,2},{12,4},{14,6},{16,24},{18,... | collective-permute-start | bytes 1572872 | tf_op jit(solution)/shard_map/ppermute | solution.py:637
  41.4 13.7 %collective-permute-start.9 = (bf16[1,192,1024]{2,1,0:T(8,128)(2,1)S(1)}, bf16[1,192,1024]{2,1,0:T(8,128)(2,1)S(1)}, u32[]{:S(2)}, u32[]{:S(2)}) collective-permute-start(bf16[1,192,1024]{2,1,0:T(8,128)(2,1)S(1)} %collective-permute-done.7.refs_8_), channel_id=1, source_target_pairs={{0,2},{2,0},{4,6},{6,4},{8,10},{10,8},{12,14},{14,12},{16,18},{18,... | collective-permute-start | bytes 1179656 | tf_op jit(solution)/shard_map/ppermute | solution.py:637
  54.5 9.2 %collective-permute-start.13 = (bf16[1,256,1024]{2,1,0:T(8,128)(2,1)S(1)}, bf16[1,256,1024]{2,1,0:T(8,128)(2,1)S(1)}, u32[]{:S(2)}, u32[]{:S(2)}) collective-permute-start(bf16[1,256,1024]{2,1,0:T(8,128)(2,1)S(1)} %collective-permute-done.11.refs_12_), channel_id=1, source_target_pairs={{0,2},{2,0},{4,6},{6,4},{8,10},{10,8},{12,14},{14,12},{16,18},{18,... | collective-permute-start | bytes 1572872 | tf_op jit(solution)/shard_map/ppermute | solution.py:637
  55.0 8.7 %collective-permute-start.14 = (bf16[1,256,1024]{2,1,0:T(8,128)(2,1)S(1)}, bf16[1,256,1024]{2,1,0:T(8,128)(2,1)S(1)}, u32[]{:S(2)}, u32[]{:S(2)}) collective-permute-start(bf16[1,256,1024]{2,1,0:T(8,128)(2,1)S(1)} %collective-permute-done.12.refs_13_), channel_id=1, source_target_pairs={{0,2},{2,0},{4,6},{6,4},{8,10},{10,8},{12,14},{14,12},{16,18},{18,... | collective-permute-start | bytes 1572872 | tf_op jit(solution)/shard_map/ppermute | solution.py:637
  112.7 6.7 %collective-permute-start.15 = (bf16[3,512,512]{2,1,0:T(8,128)(2,1)}, bf16[3,512,512]{2,1,0:T(8,128)(2,1)}, u32[]{:S(2)}, u32[]{:S(2)}) collective-permute-start(bf16[3,512,512]{2,1,0:T(8,128)(2,1)} %get-tuple-element.117), channel_id=1, source_target_pairs={{0,2},{2,0},{4,6},{6,4},{8,10},{10,8},{12,14},{14,12},{16,18},{18,... | collective-permute-start | bytes 4718600 | tf_op jit(solution)/shard_map/ppermute | solution.py:637
  116.2 9.0 %collective-permute-start.18 = (f32[8,1024]{1,0:T(8,128)S(1)}, f32[8,1024]{1,0:T(8,128)S(1)}, u32[]{:S(2)}, u32[]{:S(2)}) collective-permute-start(f32[8,1024]{1,0:T(8,128)S(1)} %add.158), channel_id=1, source_target_pairs={{0,4},{2,6},{4,0},{6,2},{8,12},{10,14},{12,8},{14,10},{16,20},{18,... | collective-permute-start | bytes 98312 | tf_op jit(solution)/shard_map/ppermute | solution.py:637
  121.1 30.0 %collective-permute-start.20 = (bf16[2,1,2,128,512]{4,3,0,2,1:T(8,128)(2,1)S(1)}, bf16[2,1,2,128,512]{4,3,0,2,1:T(8,128)(2,1)S(1)}, u32[]{:S(2)}, u32[]{:S(2)}) collective-permute-start(bf16[2,1,2,128,512]{4,3,0,2,1:T(8,128)(2,1)S(1)} %copy.56), channel_id=1, source_target_pairs={{0,1},{1,0},{2,3},{3,2},{4,5},{5,4},{6,7},{7,6},{8,9},{9,8},{10,11... | collective-permute-start | bytes 1572872 | tf_op jit(solution)/shard_map/ppermute | solution.py:637
  124.2 27.0 %collective-permute-start.21 = (bf16[2,2,1,128,512]{4,3,0,2,1:T(8,128)(2,1)S(1)}, bf16[2,2,1,128,512]{4,3,0,2,1:T(8,128)(2,1)}, u32[]{:S(2)}, u32[]{:S(2)}) collective-permute-start(bf16[2,2,1,128,512]{4,3,0,2,1:T(8,128)(2,1)S(1)} %copy.55), channel_id=1, source_target_pairs={{0,4},{2,6},{4,0},{6,2},{8,12},{10,14},{12,8},{14,10},{16,20},{18,... | collective-permute-start | bytes 1572872 | tf_op jit(solution)/shard_map/ppermute | solution.py:637
  125.3 25.9 %collective-permute-start.19 = (f32[8,1024]{1,0:T(8,128)S(1)}, f32[8,1024]{1,0:T(8,128)S(1)}, u32[]{:S(2)}, u32[]{:S(2)}) collective-permute-start(f32[8,1024]{1,0:T(8,128)S(1)} %add.159.refs_13_), channel_id=1, source_target_pairs={{0,8},{2,10},{4,12},{6,14},{8,0},{10,2},{12,4},{14,6},{16,24},{18,... | collective-permute-start | bytes 98312 | tf_op jit(solution)/shard_map/ppermute | solution.py:637
  152.0 6.5 %collective-permute-start.23 = (bf16[2,512,512]{2,1,0:T(8,128)(2,1)S(1)}, bf16[2,512,512]{2,1,0:T(8,128)(2,1)}, u32[]{:S(2)}, u32[]{:S(2)}) collective-permute-start(bf16[2,512,512]{2,1,0:T(8,128)(2,1)S(1)} %get-tuple-element.127), channel_id=1, source_target_pairs={{0,2},{2,0},{4,6},{6,4},{8,10},{10,8},{12,14},{14,12},{16,18},{18,... | collective-permute-start | bytes 3145736 | tf_op jit(solution)/shard_map/ppermute | solution.py:637
  152.0 14.7 %collective-permute-start.22 = (f32[8,1024]{1,0:T(8,128)S(1)}, f32[8,1024]{1,0:T(8,128)S(1)}, u32[]{:S(2)}, u32[]{:S(2)}) collective-permute-start(f32[8,1024]{1,0:T(8,128)S(1)} %add.160), channel_id=1, source_target_pairs={{0,16},{2,18},{4,20},{6,22},{8,24},{10,26},{12,28},{14,30},{16,0},... | collective-permute-start | bytes 98312 | tf_op jit(solution)/shard_map/ppermute | solution.py:637
  156.6 9.2 %collective-permute-start.26 = (bf16[2,1,1,128,512]{4,3,0,2,1:T(8,128)(2,1)S(1)}, bf16[2,1,1,128,512]{4,3,0,2,1:T(8,128)(2,1)S(1)}, u32[]{:S(2)}, u32[]{:S(2)}) collective-permute-start(bf16[2,1,1,128,512]{4,3,0,2,1:T(8,128)(2,1)S(1)} %get-tuple-element.212), channel_id=1, source_target_pairs={{0,1},{1,0},{2,3},{3,2},{4,5},{5,4},{6,7},{7,6},{8,9},{9,8},{10,11... | collective-permute-start | bytes 786440 | tf_op jit(solution)/shard_map/ppermute | solution.py:637
  157.5 9.2 %collective-permute-start.25 = (bf16[2,1,1,128,512]{4,3,0,2,1:T(8,128)(2,1)S(1)}, bf16[2,1,1,128,512]{4,3,0,2,1:T(8,128)(2,1)S(1)}, u32[]{:S(2)}, u32[]{:S(2)}) collective-permute-start(bf16[2,1,1,128,512]{4,3,0,2,1:T(8,128)(2,1)S(1)} %get-tuple-element.213), channel_id=1, source_target_pairs={{0,4},{2,6},{4,0},{6,2},{8,12},{10,14},{12,8},{14,10},{16,20},{18,... | collective-permute-start | bytes 786440 | tf_op jit(solution)/shard_map/ppermute | solution.py:637
  160.1 11.1 %collective-permute-start.28 = (bf16[1,2,1,128,512]{4,3,0,2,1:T(8,128)(2,1)S(1)}, bf16[1,2,1,128,512]{4,3,0,2,1:T(8,128)(2,1)S(1)}, u32[]{:S(2)}, u32[]{:S(2)}) collective-permute-start(bf16[1,2,1,128,512]{4,3,0,2,1:T(8,128)(2,1)S(1)} %dynamic-slice_convert_fusion.1), channel_id=1, source_target_pairs={{0,4},{2,6},{4,0},{6,2},{8,12},{10,14},{12,8},{14,10},{16,20},{18,... | collective-permute-start | bytes 786440 | tf_op jit(solution)/shard_map/ppermute | solution.py:637
  161.2 11.4 %collective-permute-start.24 = (bf16[1,1,2,128,512]{4,3,0,2,1:T(8,128)(2,1)S(1)}, bf16[1,1,2,128,512]{4,3,0,2,1:T(8,128)(2,1)S(1)}, u32[]{:S(2)}, u32[]{:S(2)}) collective-permute-start(bf16[1,1,2,128,512]{4,3,0,2,1:T(8,128)(2,1)S(1)} %dynamic-slice_convert_fusion.2), channel_id=1, source_target_pairs={{0,1},{1,0},{2,3},{3,2},{4,5},{5,4},{6,7},{7,6},{8,9},{9,8},{10,11... | collective-permute-start | bytes 786440 | tf_op jit(solution)/shard_map/ppermute | solution.py:637
  166.8 11.4 %collective-permute-start.31 = (bf16[4,64,512]{2,1,0:T(8,128)(2,1)S(1)}, bf16[4,64,512]{2,1,0:T(8,128)(2,1)S(1)}, u32[]{:S(2)}, u32[]{:S(2)}) collective-permute-start(bf16[4,64,512]{2,1,0:T(8,128)(2,1)S(1)} %fusion.6), channel_id=1, source_target_pairs={{0,8},{2,10},{4,12},{6,14},{8,0},{10,2},{12,4},{14,6},{16,24},{18,... | collective-permute-start | bytes 786440 | tf_op jit(solution)/shard_map/ppermute | solution.py:637
  178.3 16.9 %collective-permute-start.32 = (bf16[4,64,512]{2,1,0:T(8,128)(2,1)S(1)}, bf16[4,64,512]{2,1,0:T(8,128)(2,1)S(1)}, u32[]{:S(2)}, u32[]{:S(2)}) collective-permute-start(bf16[4,64,512]{2,1,0:T(8,128)(2,1)S(1)} %fusion.17), channel_id=1, source_target_pairs={{0,16},{2,18},{4,20},{6,22},{8,24},{10,26},{12,28},{14,30},{16,0},... | collective-permute-start | bytes 786440 | tf_op jit(solution)/shard_map/ppermute | solution.py:637
  184.0 22.2 %collective-permute-start.34 = (bf16[2,64,512]{2,1,0:T(8,128)(2,1)S(1)}, bf16[2,64,512]{2,1,0:T(8,128)(2,1)S(1)}, u32[]{:S(2)}, u32[]{:S(2)}) collective-permute-start(bf16[2,64,512]{2,1,0:T(8,128)(2,1)S(1)} %fusion.16), channel_id=1, source_target_pairs={{0,16},{2,18},{4,20},{6,22},{8,24},{10,26},{12,28},{14,30},{16,0},... | collective-permute-start | bytes 393224 | tf_op jit(solution)/shard_map/ppermute | solution.py:637
  195.2 6.6 %collective-permute-start.33 = (f32[1,72,512]{2,1,0:T(8,128)}, f32[1,72,512]{2,1,0:T(8,128)S(1)}, u32[]{:S(2)}, u32[]{:S(2)}) collective-permute-start(f32[1,72,512]{2,1,0:T(8,128)} %bitcast.81), channel_id=1, source_target_pairs={{0,1},{1,0},{2,3},{3,2},{4,5},{5,4},{6,7},{7,6},{8,9},{9,8},{10,11... | collective-permute-start | bytes 442376 | tf_op jit(solution)/shard_map/ppermute | solution.py:637
  196.0 13.2 %collective-permute-start.41 = (bf16[4,64,512]{2,1,0:T(8,128)(2,1)S(1)}, bf16[4,64,512]{2,1,0:T(8,128)(2,1)S(1)}, u32[]{:S(2)}, u32[]{:S(2)}) collective-permute-start(bf16[4,64,512]{2,1,0:T(8,128)(2,1)S(1)} %reduce-precision_convert_fusion.1), channel_id=1, source_target_pairs={{0,12},{2,14},{4,8},{6,10},{8,4},{10,6},{12,0},{14,2},{16,28},{18,... | collective-permute-start | bytes 786440 | tf_op jit(solution)/shard_map/ppermute | solution.py:637
  196.0 14.0 %collective-permute-start.40 = (bf16[4,64,512]{2,1,0:T(8,128)(2,1)S(1)}, bf16[4,64,512]{2,1,0:T(8,128)(2,1)S(1)}, u32[]{:S(2)}, u32[]{:S(2)}) collective-permute-start(bf16[4,64,512]{2,1,0:T(8,128)(2,1)S(1)} %reduce-precision_convert_fusion.1), channel_id=1, source_target_pairs={{0,4},{2,6},{4,0},{6,2},{8,12},{10,14},{12,8},{14,10},{16,20},{18,... | collective-permute-start | bytes 786440 | tf_op jit(solution)/shard_map/ppermute | solution.py:637
  197.1 13.5 %collective-permute-start.39 = (bf16[4,64,512]{2,1,0:T(8,128)(2,1)S(1)}, bf16[4,64,512]{2,1,0:T(8,128)(2,1)S(1)}, u32[]{:S(2)}, u32[]{:S(2)}) collective-permute-start(bf16[4,64,512]{2,1,0:T(8,128)(2,1)S(1)} %reduce-precision_convert_fusion.1), channel_id=1, source_target_pairs={{0,8},{2,10},{4,12},{6,14},{8,0},{10,2},{12,4},{14,6},{16,24},{18,... | collective-permute-start | bytes 786440 | tf_op jit(solution)/shard_map/ppermute | solution.py:637
  210.8 7.6 %collective-permute-start.42 = (bf16[4,256,512]{2,1,0:T(8,128)(2,1)S(1)}, bf16[4,256,512]{2,1,0:T(8,128)(2,1)S(1)}, u32[]{:S(2)}, u32[]{:S(2)}) collective-permute-start(bf16[4,256,512]{2,1,0:T(8,128)(2,1)S(1)} %pad_maximum_fusion.1.refs_1_), channel_id=1, source_target_pairs={{0,2},{2,0},{4,6},{6,4},{8,10},{10,8},{12,14},{14,12},{16,18},{18,... | collective-permute-start | bytes 3145736 | tf_op jit(solution)/shard_map/ppermute | solution.py:637
  (36 other events, 219.0 us)

commit v4 on v3

--- a/solution.py
+++ b/solution.py
@@ -748,18 +748,14 @@
         return own, swapped(own, "tm", 1)
 
 
-def join_kernel(place, own, other, *outs):
+def join_kernel(place, own_first, other_first, own, other, out_first, out_second, out_taps, out_last):
     width = own.shape[2]
     mine, theirs = halves_of(place[0], width)
-    first = 0
-    for out in outs:
-        for source, columns in ((own, mine), (other, theirs)):
-            if len(out.shape) == 2:
-                out[:, pl.ds(columns, width)] = source[first].astype(f32)
-            else:
-                count = out.shape[0]
-                out[:, :, pl.ds(columns, width)] = source[first : first + count].astype(f32)
-        first += 1 if len(out.shape) == 2 else out.shape[0]
+    for first, rest, columns in ((own_first, own, mine), (other_first, other, theirs)):
+        out_first[:, pl.ds(columns, width)] = first[0].astype(f32)
+        out_second[:, pl.ds(columns, width)] = first[1].astype(f32)
+        out_taps[:, :, pl.ds(columns, width)] = rest[0:3].astype(f32)
+        out_last[:, pl.ds(columns, width)] = rest[3].astype(f32)
 
 
 def step_embedding(pack_steps, width):
@@ -1039,6 +1035,17 @@
     packs = small[None]
     for bit in bits_of("fsdp"):
         packs = jnp.concatenate([packs, swapped(packs, "fsdp", bit)], axis=0)
+
+    flat, tall = (shard_rows, wide), (3, shard_rows, wide)
+    for bit in more_bits:
+        conv_proj.fold(cond_step.away)
+        conv_proj.start_double(bit)
+        cond_step.fold(conv_proj.away)
+        cond_step.start_double(bit)
+    conv_proj.fold()
+    conv_proj.start_gather()
+    cond_step.fold(conv_proj.away, packs, pair)
+    cond_step.start_gather()
     grad_queries, grad_query, grad_out, grad_film = call(
         small_grad_kernel,
         (1,),
@@ -1052,32 +1059,21 @@
         "small_grads",
         3.3,
         scratch=[pltpu.VMEM((width, wide), f32), pltpu.VMEM((QUERIES, width), f32)],
-    )
-
-    def join(halves, shapes, name):
-        return call(
-            join_kernel,
-            (1,),
-            [scalars(place)] + [fixed(a) for a in halves],
-            [new(shape) for shape in shapes],
-            name,
-            3,
-        )
-
-    flat, tall = (shard_rows, wide), (3, shard_rows, wide)
-    for bit in more_bits:
-        conv_proj.fold(cond_step.away)
-        conv_proj.start_double(bit)
-        cond_step.fold(conv_proj.away)
-        cond_step.start_double(bit)
-    conv_proj.fold()
-    conv_proj.start_gather()
-    cond_step.fold(conv_proj.away, grad_queries)
-    cond_step.start_gather()
+        after=[cond_step.away],
+    )
+    grad_queries, grad_key, *cond_step.raw = lax.optimization_barrier(
+        (grad_queries, grad_key, *cond_step.raw)
+    )
     conv_proj = conv_proj.gather()
     cond_step = cond_step.gather()
-    grad_cond, grad_step = join(cond_step, [flat, flat], "join_cond_step")
-    grad_conv, grad_proj = join(conv_proj, [tall, flat], "join_conv_proj")
+    grad_cond, grad_step, grad_conv, grad_proj = call(
+        join_kernel,
+        (1,),
+        [scalars(place)] + [fixed(a) for a in (*cond_step, *conv_proj)],
+        [new(shape) for shape in (flat, flat, tall, flat)],
+        "join",
+        4,
+    )
     return (
         res_out[:, None],
         skip_out[:, None],

time: 222 us -> 223 us (level)
  waiting for transfers between devices: 35.1 us -> 39.3 us
    ppermute x43, waiting for transfers between devices: 35.1 us -> 39.3 us  [swapped(): return lax.ppermute(array, axis, [(i, i ^ bit) for i in range(count)])]
    pallas_call x13 -> x12, Pallas kernels: 114 us -> 112 us  [call(): pl.pallas_call(body, grid=grid, in_specs=[spec for _, spec in ins] + [ANY...]
  transfers between devices with their start and end apart: 46 -> 46, of which waited for: 16 -> 16; matrix products, arithmetic and copies ran while one was open for 7% -> 7% of each run, Pallas kernels for 29% -> 27%
where the time goes in v4:
time: 223 us
  Pallas kernels  112 us (50%)
  starting transfers between devices  47 us (21%)
  waiting for transfers between devices  39.3 us (18%)
  other arithmetic  12.2 us (5%)
  local copies, waits for them, and re-layouts  10.4 us (5%)
    pallas_call x12, Pallas kernels, call(): pl.pallas_call(body, grid=grid, in_specs=[spec for _, spec in ins] + [ANY...  112 us
    ppermute x43, waiting for transfers between devices, swapped(): return lax.ppermute(array, axis, [(i, i ^ bit) for i in range(count)])  39.3 us
    ppermute x43, starting transfers between devices, swapped(): return lax.ppermute(array, axis, [(i, i ^ bit) for i in range(count)])  37.7 us
    unnamed x46, local copies, waits for them, and re-layouts  7.87 us
    all_to_all x1, starting transfers between devices, per_device(): every_prompt = lax.all_to_all(every_prompt, 'tm', 0, 0)  6.59 us
    add x4, other arithmetic, __init__(): k + r.astype(f32)  5.83 us
  transfers between devices with their start and end apart: 46, of which 16 were waited for; matrix products, arithmetic and copies ran while one was open for 7% of the time, Pallas kernels for 27%

profile of v4, /device:TPU:0, one launch (start us, length us, event | category | flops | bytes accessed | tf_op | source)
XLA Modules:
  0.0 222.6 jit_solution(13199149195660433263)
XLA Ops:
  0.8 1.7 pack_first.1.refs_4_
  2.5 3.0 %collective-permute-start.2 = (bf16[1,128,1024]{2,1,0:T(8,128)(2,1)S(1)}, bf16[1,128,1024]{2,1,0:T(8,128)(2,1)S(1)}, u32[]{:S(2)}, u32[]{:S(2)}) collective-permute-start(bf16[1,128,1024]{2,1,0:T(8,128)(2,1)S(1)} %bitcast.57), channel_id=1, source_target_pairs={{0,1},{1,0},{2,3},{3,2},{4,5},{5,4},{6,7},{7,6},{8,9},{9,8},{10,11... | collective-permute-start | bytes 786440 | tf_op jit(solution)/shard_map/ppermute | solution.py:637
  8.0 2.3 %pack_rest.1 = (bf16[192,1024]{1,0:T(8,128)(2,1)S(1)}, bf16[256,1024]{1,0:T(8,128)(2,1)S(1)}) custom-call(s32[5]{0:T(128)S(1)} %stack.23.refs_0_, f32[256,512]{1,0:T(8,128)} %refs_3_.3, f32[256,512]{1,0:T(8,128)} %refs_4_.3, f32[256,512]{1,0:T(8,128)} %refs_5_.3, f32[256,512]{1,0:T(8,128)} %refs_6_.3, f32[256,1024]{1,0:T(8,128)} %refs_7_.3, ...), custom_call_target="tpu_custom_call" | custom-call | flops 2000000000 | bytes 4096 | tf_op jit(solution)/shard_map/pack_rest/pallas_call | solution.py:68
  10.4 2.0 collective-permute-start.7
  13.2 6.6 %all-to-all-start = ((bf16[16,2,16,512]{3,2,1,0:T(8,128)(2,1)}), bf16[16,2,16,512]{3,2,1,0:T(8,128)(2,1)}, u32[]{:S(2)}, u32[]{:S(2)}) async-start(bf16[16,2,16,512]{3,2,1,0:T(8,128)(2,1)} %broadcast_in_dim.35), calls=%async_computation | async-start | bytes 1048576 | tf_op jit(solution)/shard_map/all_to_all | solution.py:843
  20.4 5.1 %masks.1 = (bf16[2,1536,384]{2,1,0:T(8,128)(2,1)}, bf16[2,1536,128]{2,1,0:T(8,128)(2,1)}, bf16[2,64,384]{2,1,0:T(8,128)(2,1)}, bf16[2,64,128]{2,1,0:T(8,128)(2,1)}) custom-call(s32[5]{0:T(128)S(1)} %stack.23.refs_0_, s32[2,30]{1,0:T(2,128)S(1)} %bitcast.60, bf16[192,1024]{1,0:T(8,128)(2,1)S(1)} %get-tuple-element.98.refs_2_), custom_call_target="tpu_custom_call" | custom-call | flops 5000000000 | bytes 4096 | tf_op jit(solution)/shard_map/masks/pallas_call | solution.py:68
  25.7 1.8 collective-permute-start.3
  29.9 6.1 %collective-permute-done.3.refs_11_ = bf16[1,128,1024]{2,1,0:T(8,128)(2,1)S(1)} collective-permute-done((bf16[1,128,1024]{2,1,0:T(8,128)(2,1)S(1)}, bf16[1,128,1024]{2,1,0:T(8,128)(2,1)S(1)}, u32[]{:S(2)}, u32[]{:S(2)}) %collective-permute-start.3) | collective-permute-done | bytes 262176 | tf_op jit(solution)/shard_map/ppermute | solution.py:637
  36.0 1.9 collective-permute-start.8
  38.2 3.1 %collective-permute-start.12 = (bf16[1,256,1024]{2,1,0:T(8,128)(2,1)S(1)}, bf16[1,256,1024]{2,1,0:T(8,128)(2,1)S(1)}, u32[]{:S(2)}, u32[]{:S(2)}) collective-permute-start(bf16[1,256,1024]{2,1,0:T(8,128)(2,1)S(1)} %collective-permute-done.11.refs_12_), channel_id=1, source_target_pairs={{0,8},{2,10},{4,12},{6,14},{8,0},{10,2},{12,4},{14,6},{16,24},{18,... | collective-permute-start | bytes 1572872 | tf_op jit(solution)/shard_map/ppermute | solution.py:637
  42.1 10.7 %film.1 = (bf16[2,1632,512]{2,1,0:T(8,128)(2,1)S(1)}, bf16[512,512]{1,0:T(8,128)(2,1)}, bf16[128,512]{1,0:T(8,128)(2,1)}) custom-call(s32[5]{0:T(128)S(1)} %stack.23.refs_0_, bf16[2,1536,512]{2,1,0:T(8,128)(2,1)} %bitcast.62, bf16[2,1536,512]{2,1,0:T(8,128)(2,1)} %bitcast.66, bf16[4,2,32,512]{3,2,1,0:T(8,128)(2,1)} %copy-done.16, ...), custom_call_target="tpu_custom_call" | custom-call | flops 1000000000 | bytes 4096 | tf_op jit(solution)/shard_map/film/pallas_call | solution.py:68
  52.8 1.7 copy-done.4
  57.9 5.8 %attention.1 = (f32[2,8,1024]{2,1,0:T(8,128)}, bf16[2,256,512]{2,1,0:T(8,128)(2,1)}, f32[2,256,256]{2,1,0:T(8,128)}, bf16[2,256,512]{2,1,0:T(8,128)(2,1)}, bf16[...) custom-call(s32[5]{0:T(128)S(1)} %stack.23.refs_0_, ...), custom_call_target="tpu_custom_call" | custom-call | flops 5000000000 | bytes 4096 | tf_op jit(solution)/shard_map/attention/pallas_call | solution.py:68
  63.7 1.9 copy-done.5
  65.7 32.8 %conv.1 = (bf16[2,1600,1024]{2,1,0:T(8,128)(2,1)S(1)}, bf16[2,1600,1024]{2,1,0:T(8,128)(2,1)}, bf16[1536,1024]{1,0:T(8,128)(2,1)}, f32[8,1024]{1,0:T(8,128)}, f3...) custom-call(s32[5]{0:T(128)S(1)} %stack.23.refs_0_, ...), custom_call_target="tpu_custom_call" | custom-call | flops 32000000000 | bytes 4096 | tf_op jit(solution)/shard_map/conv/pallas_call | solution.py:68
  99.5 13.2 %conv_grad.1 = (f32[3,512,512]{2,1,0:T(8,128)S(1)}, bf16[3,512,512]{2,1,0:T(8,128)(2,1)}) custom-call(s32[5]{0:T(128)} %copy-done.2, bf16[2,1632,512]{2,1,0:T(8,128)(2,1)S(1)} %copy-done.5, bf16[2,1536,384]{2,1,0:T(8,128)(2,1)} %get-tuple-element.106.refs_2_, bf16[2,1600,1024]{2,1,0:T(8,128)(2,1)S(1)} %get-tuple-element.120.refs_3_), custom_call_target="tpu_custom_call" | custom-call | flops 13500000256 | bytes 4096 | tf_op jit(solution)/shard_map/conv_grad/pallas_call | solution.py:68
  113.4 2.9 %collective-permute-done.17 = f32[8,1024]{1,0:T(8,128)S(1)} collective-permute-done((f32[8,1024]{1,0:T(8,128)S(1)}, f32[8,1024]{1,0:T(8,128)S(1)}, u32[]{:S(2)}, u32[]{:S(2)}) %collective-permute-start.17) | collective-permute-done | bytes 32800 | tf_op jit(solution)/shard_map/ppermute | solution.py:637
  116.3 1.7 collective-permute-start.18
  125.4 25.8 %hidden_grad.1 = (f32[2,1536,512]{2,1,0:T(8,128)}, f32[2,512,512]{2,1,0:T(8,128)S(1)}, bf16[2,512,512]{2,1,0:T(8,128)(2,1)S(1)}) custom-call(s32[5]{0:T(128)S(1)} %copy-done.3, bf16[2,1600,1024]{2,1,0:T(8,128)(2,1)} %get-tuple-element.117.refs_1_, bf16[2,1536,384]{2,1,0:T(8,128)(2,1)} %get-tuple-element.106.refs_2_, ...), custom_call_target="tpu_custom_call" | custom-call | flops 27000000512 | bytes 4096 | tf_op jit(solution)/shard_map/hidden_grad/pallas_call | solution.py:68
  152.0 2.7 %collective-permute-start.22 = (f32[8,1024]{1,0:T(8,128)S(1)}, f32[8,1024]{1,0:T(8,128)S(1)}, u32[]{:S(2)}, u32[]{:S(2)}) collective-permute-start(f32[8,1024]{1,0:T(8,128)S(1)} %add.160), channel_id=1, source_target_pairs={{0,16},{2,18},{4,20},{6,22},{8,24},{10,26},{12,28},{14,30},{16,0},... | collective-permute-start | bytes 98312 | tf_op jit(solution)/shard_map/ppermute | solution.py:637
  158.5 1.6 convert_add_fusion.1
  162.5 3.3 %collective-permute-done.26 = bf16[2,1,1,128,512]{4,3,0,2,1:T(8,128)(2,1)S(1)} collective-permute-done((bf16[2,1,1,128,512]{4,3,0,2,1:T(8,128)(2,1)S(1)}, bf16[2,1,1,128,512]{4,3,0,2,1:T(8,128)(2,1)S(1)}, u32[]{:S(2)}, u32[]{:S(2)}) %collective-permute-start.26) | collective-permute-done | bytes 262176 | tf_op jit(solution)/shard_map/ppermute | solution.py:637
  167.0 4.2 %collective-permute-done.28 = bf16[1,2,1,128,512]{4,3,0,2,1:T(8,128)(2,1)S(1)} collective-permute-done((bf16[1,2,1,128,512]{4,3,0,2,1:T(8,128)(2,1)S(1)}, bf16[1,2,1,128,512]{4,3,0,2,1:T(8,128)(2,1)S(1)}, u32[]{:S(2)}, u32[]{:S(2)}) %collective-permute-start.28) | collective-permute-done | bytes 262176 | tf_op jit(solution)/shard_map/ppermute | solution.py:637
  173.8 2.6 %collective-permute-done.29 = bf16[1,1,1,128,512]{4,3,0,2,1:T(8,128)(2,1)S(1)} collective-permute-done((bf16[1,1,1,128,512]{4,3,0,2,1:T(8,128)(2,1)S(1)}, bf16[1,1,1,128,512]{4,3,0,2,1:T(8,128)(2,1)S(1)}, u32[]{:S(2)}, u32[]{:S(2)}) %collective-permute-start.29) | collective-permute-done | bytes 131104 | tf_op jit(solution)/shard_map/ppermute | solution.py:637
  178.3 2.0 collective-permute-start.32
  180.3 3.6 %collective-permute-done.30 = bf16[2,64,512]{2,1,0:T(8,128)(2,1)S(1)} collective-permute-done((bf16[2,64,512]{2,1,0:T(8,128)(2,1)S(1)}, bf16[2,64,512]{2,1,0:T(8,128)(2,1)S(1)}, u32[]{:S(2)}, u32[]{:S(2)}) %collective-permute-start.30) | collective-permute-done | bytes 131104 | tf_op jit(solution)/shard_map/ppermute | solution.py:637
  185.8 6.8 %attention_grad.1 = (f32[2,16,512]{2,1,0:T(8,128)}, f32[512,512]{1,0:T(8,128)}, f32[72,512]{1,0:T(8,128)}) custom-call(s32[5]{0:T(128)S(1)} %copy-done.3, f32[8,1024]{1,0:T(8,128)} %add.177.refs_1_, bf16[2,256,512]{2,1,0:T(8,128)(2,1)} %get-tuple-element.146.refs_2_, f32[2,256,256]{2,1,0:T(8,128)} %get-tuple-element.147.refs_3_, ...), custom_call_target="tpu_custom_call" | custom-call | flops 7000000000 | bytes 4096 | tf_op jit(solution)/shard_map/attention_grad/pallas_call | solution.py:68
  192.6 2.5 %collective-permute-done.32 = bf16[4,64,512]{2,1,0:T(8,128)(2,1)S(1)} collective-permute-done((bf16[4,64,512]{2,1,0:T(8,128)(2,1)S(1)}, bf16[4,64,512]{2,1,0:T(8,128)(2,1)S(1)}, u32[]{:S(2)}, u32[]{:S(2)}) %collective-permute-start.32) | collective-permute-done | bytes 262176 | tf_op jit(solution)/shard_map/ppermute | solution.py:637
  205.5 3.2 %collective-permute-done.43 = bf16[4,64,512]{2,1,0:T(8,128)(2,1)S(1)} collective-permute-done((bf16[4,64,512]{2,1,0:T(8,128)(2,1)S(1)}, bf16[4,64,512]{2,1,0:T(8,128)(2,1)S(1)}, u32[]{:S(2)}, u32[]{:S(2)}) %collective-permute-start.43) | collective-permute-done | bytes 262176 | tf_op jit(solution)/shard_map/ppermute | solution.py:637
  208.7 3.0 %collective-permute-done.42 = bf16[4,64,512]{2,1,0:T(8,128)(2,1)S(1)} collective-permute-done((bf16[4,64,512]{2,1,0:T(8,128)(2,1)S(1)}, bf16[4,64,512]{2,1,0:T(8,128)(2,1)S(1)}, u32[]{:S(2)}, u32[]{:S(2)}) %collective-permute-start.42) | collective-permute-done | bytes 262176 | tf_op jit(solution)/shard_map/ppermute | solution.py:637
  212.5 3.4 %small_grads.1 = (f32[16,512]{1,0:T(8,128)}, f32[256,512]{1,0:T(8,128)}, f32[256,512]{1,0:T(8,128)}, f32[256,1024]{1,0:T(8,128)}) custom-call(s32[5]{0:T(128)S(1)} %copy-done.3, f32[2,72,512]{2,1,0:T(8,128)} %pad_maximum_fusion.3.refs_1_, bf16[32,512]{1,0:T(8,128)(2,1)} %copy-done.1, bf16[512,512]{1,0:T(8,128)(2,1)} %get-tuple-element.161.refs_3_, ...), custom_call_target="tpu_custom_call" | custom-call | flops 3300000000 | bytes 4096 | tf_op jit(solution)/shard_map/small_grads/pallas_call | solution.py:68
  219.1 3.5 %join.1 = (f32[256,1024]{1,0:T(8,128)}, f32[256,1024]{1,0:T(8,128)}, f32[3,256,1024]{2,1,0:T(8,128)}, f32[256,1024]{1,0:T(8,128)}) custom-call(s32[5]{0:T(128)S(1)} %copy-done.3, bf16[2,256,512]{2,1,0:T(8,128)(2,1)S(1)} %pad_maximum_fusion.2.refs_1_, bf16[2,256,512]{2,1,0:T(8,128)(2,1)S(1)} %collective-permute-done.40.refs_2_, ...), custom_call_target="tpu_custom_call" | custom-call | flops 4000000000 | bytes 4096 | tf_op jit(solution)/shard_map/join/pallas_call | solution.py:68
  (168 shorter events, 48.4 us)
Async XLA Ops:
  2.5 23.2 %collective-permute-start.2 = (bf16[1,128,1024]{2,1,0:T(8,128)(2,1)S(1)}, bf16[1,128,1024]{2,1,0:T(8,128)(2,1)S(1)}, u32[]{:S(2)}, u32[]{:S(2)}) collective-permute-start(bf16[1,128,1024]{2,1,0:T(8,128)(2,1)S(1)} %bitcast.57), channel_id=1, source_target_pairs={{0,1},{1,0},{2,3},{3,2},{4,5},{5,4},{6,7},{7,6},{8,9},{9,8},{10,11... | collective-permute-start | bytes 786440 | tf_op jit(solution)/shard_map/ppermute | solution.py:637
  6.7 31.5 %collective-permute-start.1 = (bf16[4,2,32,512]{3,2,1,0:T(8,128)(2,1)S(1)}, bf16[4,2,32,512]{3,2,1,0:T(8,128)(2,1)S(1)}, u32[]{:S(2)}, u32[]{:S(2)}) collective-permute-start(bf16[4,2,32,512]{3,2,1,0:T(8,128)(2,1)S(1)} %get-tuple-element.97), channel_id=1, source_target_pairs={{2,0},{4,2},{6,4},{8,6},{10,8},{12,10},{14,12},{16,14},{18,16},{20... | collective-permute-start | bytes 786440 | tf_op jit(solution)/shard_map/ppermute | solution.py:820
  10.3 25.7 %collective-permute-start.6 = (bf16[16,512]{1,0:T(8,128)(2,1)S(1)}, bf16[16,512]{1,0:T(8,128)(2,1)S(1)}, u32[]{:S(2)}, u32[]{:S(2)}) collective-permute-start(bf16[16,512]{1,0:T(8,128)(2,1)S(1)} %convert_element_type.138), channel_id=1, source_target_pairs={{0,1},{1,0},{2,3},{3,2},{4,5},{5,4},{6,7},{7,6},{8,9},{9,8},{10,11... | collective-permute-start | bytes 49160 | tf_op jit(solution)/shard_map/ppermute | solution.py:637
  10.4 18.1 %collective-permute-start.7 = (bf16[1,192,1024]{2,1,0:T(8,128)(2,1)S(1)}, bf16[1,192,1024]{2,1,0:T(8,128)(2,1)S(1)}, u32[]{:S(2)}, u32[]{:S(2)}) collective-permute-start(bf16[1,192,1024]{2,1,0:T(8,128)(2,1)S(1)} %bitcast.59), channel_id=1, source_target_pairs={{0,1},{1,0},{2,3},{3,2},{4,5},{5,4},{6,7},{7,6},{8,9},{9,8},{10,11... | collective-permute-start | bytes 1179656 | tf_op jit(solution)/shard_map/ppermute | solution.py:637
  13.2 42.5 %all-to-all-start = ((bf16[16,2,16,512]{3,2,1,0:T(8,128)(2,1)}), bf16[16,2,16,512]{3,2,1,0:T(8,128)(2,1)}, u32[]{:S(2)}, u32[]{:S(2)}) async-start(bf16[16,2,16,512]{3,2,1,0:T(8,128)(2,1)} %broadcast_in_dim.35), calls=%async_computation | async-start | bytes 1048576 | tf_op jit(solution)/shard_map/all_to_all | solution.py:843
  19.8 18.1 %collective-permute-start.11 = (bf16[1,256,1024]{2,1,0:T(8,128)(2,1)S(1)}, bf16[1,256,1024]{2,1,0:T(8,128)(2,1)S(1)}, u32[]{:S(2)}, u32[]{:S(2)}) collective-permute-start(bf16[1,256,1024]{2,1,0:T(8,128)(2,1)S(1)} %bitcast.58), channel_id=1, source_target_pairs={{0,1},{1,0},{2,3},{3,2},{4,5},{5,4},{6,7},{7,6},{8,9},{9,8},{10,11... | collective-permute-start | bytes 1572872 | tf_op jit(solution)/shard_map/ppermute | solution.py:637
  25.7 10.3 %collective-permute-start.3 = (bf16[1,128,1024]{2,1,0:T(8,128)(2,1)S(1)}, bf16[1,128,1024]{2,1,0:T(8,128)(2,1)S(1)}, u32[]{:S(2)}, u32[]{:S(2)}) collective-permute-start(bf16[1,128,1024]{2,1,0:T(8,128)(2,1)S(1)} %collective-permute-done.2.refs_10_), channel_id=1, source_target_pairs={{0,4},{2,6},{4,0},{6,2},{8,12},{10,14},{12,8},{14,10},{16,20},{18,... | collective-permute-start | bytes 786440 | tf_op jit(solution)/shard_map/ppermute | solution.py:637
  28.4 12.9 %collective-permute-start = (bf16[4,2,32,512]{3,2,1,0:T(8,128)(2,1)S(1)}, bf16[4,2,32,512]{3,2,1,0:T(8,128)(2,1)S(1)}, u32[]{:S(2)}, u32[]{:S(2)}) collective-permute-start(bf16[4,2,32,512]{3,2,1,0:T(8,128)(2,1)S(1)} %get-tuple-element.96.refs_10_), channel_id=1, source_target_pairs={{0,2},{2,4},{4,6},{6,8},{8,10},{10,12},{12,14},{14,16},{16,18},{18... | collective-permute-start | bytes 786440 | tf_op jit(solution)/shard_map/ppermute | solution.py:819
  36.0 18.5 %collective-permute-start.8 = (bf16[1,192,1024]{2,1,0:T(8,128)(2,1)S(1)}, bf16[1,192,1024]{2,1,0:T(8,128)(2,1)S(1)}, u32[]{:S(2)}, u32[]{:S(2)}) collective-permute-start(bf16[1,192,1024]{2,1,0:T(8,128)(2,1)S(1)} %collective-permute-done.7.refs_8_), channel_id=1, source_target_pairs={{0,4},{2,6},{4,0},{6,2},{8,12},{10,14},{12,8},{14,10},{16,20},{18,... | collective-permute-start | bytes 1179656 | tf_op jit(solution)/shard_map/ppermute | solution.py:637
  38.2 16.8 %collective-permute-start.12 = (bf16[1,256,1024]{2,1,0:T(8,128)(2,1)S(1)}, bf16[1,256,1024]{2,1,0:T(8,128)(2,1)S(1)}, u32[]{:S(2)}, u32[]{:S(2)}) collective-permute-start(bf16[1,256,1024]{2,1,0:T(8,128)(2,1)S(1)} %collective-permute-done.11.refs_12_), channel_id=1, source_target_pairs={{0,8},{2,10},{4,12},{6,14},{8,0},{10,2},{12,4},{14,6},{16,24},{18,... | collective-permute-start | bytes 1572872 | tf_op jit(solution)/shard_map/ppermute | solution.py:637
  41.4 13.7 %collective-permute-start.9 = (bf16[1,192,1024]{2,1,0:T(8,128)(2,1)S(1)}, bf16[1,192,1024]{2,1,0:T(8,128)(2,1)S(1)}, u32[]{:S(2)}, u32[]{:S(2)}) collective-permute-start(bf16[1,192,1024]{2,1,0:T(8,128)(2,1)S(1)} %collective-permute-done.7.refs_8_), channel_id=1, source_target_pairs={{0,2},{2,0},{4,6},{6,4},{8,10},{10,8},{12,14},{14,12},{16,18},{18,... | collective-permute-start | bytes 1179656 | tf_op jit(solution)/shard_map/ppermute | solution.py:637
  54.5 9.2 %collective-permute-start.13 = (bf16[1,256,1024]{2,1,0:T(8,128)(2,1)S(1)}, bf16[1,256,1024]{2,1,0:T(8,128)(2,1)S(1)}, u32[]{:S(2)}, u32[]{:S(2)}) collective-permute-start(bf16[1,256,1024]{2,1,0:T(8,128)(2,1)S(1)} %collective-permute-done.11.refs_12_), channel_id=1, source_target_pairs={{0,2},{2,0},{4,6},{6,4},{8,10},{10,8},{12,14},{14,12},{16,18},{18,... | collective-permute-start | bytes 1572872 | tf_op jit(solution)/shard_map/ppermute | solution.py:637
  55.0 8.7 %collective-permute-start.14 = (bf16[1,256,1024]{2,1,0:T(8,128)(2,1)S(1)}, bf16[1,256,1024]{2,1,0:T(8,128)(2,1)S(1)}, u32[]{:S(2)}, u32[]{:S(2)}) collective-permute-start(bf16[1,256,1024]{2,1,0:T(8,128)(2,1)S(1)} %collective-permute-done.12.refs_13_), channel_id=1, source_target_pairs={{0,2},{2,0},{4,6},{6,4},{8,10},{10,8},{12,14},{14,12},{16,18},{18,... | collective-permute-start | bytes 1572872 | tf_op jit(solution)/shard_map/ppermute | solution.py:637
  116.3 9.0 %collective-permute-start.18 = (f32[8,1024]{1,0:T(8,128)S(1)}, f32[8,1024]{1,0:T(8,128)S(1)}, u32[]{:S(2)}, u32[]{:S(2)}) collective-permute-start(f32[8,1024]{1,0:T(8,128)S(1)} %add.158), channel_id=1, source_target_pairs={{0,4},{2,6},{4,0},{6,2},{8,12},{10,14},{12,8},{14,10},{16,20},{18,... | collective-permute-start | bytes 98312 | tf_op jit(solution)/shard_map/ppermute | solution.py:637
  121.2 30.0 %collective-permute-start.20 = (bf16[2,1,2,128,512]{4,3,0,2,1:T(8,128)(2,1)S(1)}, bf16[2,1,2,128,512]{4,3,0,2,1:T(8,128)(2,1)S(1)}, u32[]{:S(2)}, u32[]{:S(2)}) collective-permute-start(bf16[2,1,2,128,512]{4,3,0,2,1:T(8,128)(2,1)S(1)} %copy.56), channel_id=1, source_target_pairs={{0,1},{1,0},{2,3},{3,2},{4,5},{5,4},{6,7},{7,6},{8,9},{9,8},{10,11... | collective-permute-start | bytes 1572872 | tf_op jit(solution)/shard_map/ppermute | solution.py:637
  124.2 27.0 %collective-permute-start.21 = (bf16[2,2,1,128,512]{4,3,0,2,1:T(8,128)(2,1)S(1)}, bf16[2,2,1,128,512]{4,3,0,2,1:T(8,128)(2,1)}, u32[]{:S(2)}, u32[]{:S(2)}) collective-permute-start(bf16[2,2,1,128,512]{4,3,0,2,1:T(8,128)(2,1)S(1)} %copy.55), channel_id=1, source_target_pairs={{0,4},{2,6},{4,0},{6,2},{8,12},{10,14},{12,8},{14,10},{16,20},{18,... | collective-permute-start | bytes 1572872 | tf_op jit(solution)/shard_map/ppermute | solution.py:637
  125.3 25.9 %collective-permute-start.19 = (f32[8,1024]{1,0:T(8,128)S(1)}, f32[8,1024]{1,0:T(8,128)S(1)}, u32[]{:S(2)}, u32[]{:S(2)}) collective-permute-start(f32[8,1024]{1,0:T(8,128)S(1)} %add.159.refs_13_), channel_id=1, source_target_pairs={{0,8},{2,10},{4,12},{6,14},{8,0},{10,2},{12,4},{14,6},{16,24},{18,... | collective-permute-start | bytes 98312 | tf_op jit(solution)/shard_map/ppermute | solution.py:637
  152.0 14.7 %collective-permute-start.22 = (f32[8,1024]{1,0:T(8,128)S(1)}, f32[8,1024]{1,0:T(8,128)S(1)}, u32[]{:S(2)}, u32[]{:S(2)}) collective-permute-start(f32[8,1024]{1,0:T(8,128)S(1)} %add.160), channel_id=1, source_target_pairs={{0,16},{2,18},{4,20},{6,22},{8,24},{10,26},{12,28},{14,30},{16,0},... | collective-permute-start | bytes 98312 | tf_op jit(solution)/shard_map/ppermute | solution.py:637
  156.6 9.2 %collective-permute-start.26 = (bf16[2,1,1,128,512]{4,3,0,2,1:T(8,128)(2,1)S(1)}, bf16[2,1,1,128,512]{4,3,0,2,1:T(8,128)(2,1)S(1)}, u32[]{:S(2)}, u32[]{:S(2)}) collective-permute-start(bf16[2,1,1,128,512]{4,3,0,2,1:T(8,128)(2,1)S(1)} %get-tuple-element.222), channel_id=1, source_target_pairs={{0,1},{1,0},{2,3},{3,2},{4,5},{5,4},{6,7},{7,6},{8,9},{9,8},{10,11... | collective-permute-start | bytes 786440 | tf_op jit(solution)/shard_map/ppermute | solution.py:637
  157.5 9.2 %collective-permute-start.25 = (bf16[2,1,1,128,512]{4,3,0,2,1:T(8,128)(2,1)S(1)}, bf16[2,1,1,128,512]{4,3,0,2,1:T(8,128)(2,1)S(1)}, u32[]{:S(2)}, u32[]{:S(2)}) collective-permute-start(bf16[2,1,1,128,512]{4,3,0,2,1:T(8,128)(2,1)S(1)} %get-tuple-element.223), channel_id=1, source_target_pairs={{0,4},{2,6},{4,0},{6,2},{8,12},{10,14},{12,8},{14,10},{16,20},{18,... | collective-permute-start | bytes 786440 | tf_op jit(solution)/shard_map/ppermute | solution.py:637
  160.2 11.1 %collective-permute-start.28 = (bf16[1,2,1,128,512]{4,3,0,2,1:T(8,128)(2,1)S(1)}, bf16[1,2,1,128,512]{4,3,0,2,1:T(8,128)(2,1)S(1)}, u32[]{:S(2)}, u32[]{:S(2)}) collective-permute-start(bf16[1,2,1,128,512]{4,3,0,2,1:T(8,128)(2,1)S(1)} %dynamic-slice_convert_fusion.1), channel_id=1, source_target_pairs={{0,4},{2,6},{4,0},{6,2},{8,12},{10,14},{12,8},{14,10},{16,20},{18,... | collective-permute-start | bytes 786440 | tf_op jit(solution)/shard_map/ppermute | solution.py:637
  161.3 11.4 %collective-permute-start.24 = (bf16[1,1,2,128,512]{4,3,0,2,1:T(8,128)(2,1)S(1)}, bf16[1,1,2,128,512]{4,3,0,2,1:T(8,128)(2,1)S(1)}, u32[]{:S(2)}, u32[]{:S(2)}) collective-permute-start(bf16[1,1,2,128,512]{4,3,0,2,1:T(8,128)(2,1)S(1)} %dynamic-slice_convert_fusion.2), channel_id=1, source_target_pairs={{0,1},{1,0},{2,3},{3,2},{4,5},{5,4},{6,7},{7,6},{8,9},{9,8},{10,11... | collective-permute-start | bytes 786440 | tf_op jit(solution)/shard_map/ppermute | solution.py:637
  166.8 11.4 %collective-permute-start.31 = (bf16[4,64,512]{2,1,0:T(8,128)(2,1)S(1)}, bf16[4,64,512]{2,1,0:T(8,128)(2,1)S(1)}, u32[]{:S(2)}, u32[]{:S(2)}) collective-permute-start(bf16[4,64,512]{2,1,0:T(8,128)(2,1)S(1)} %fusion.6), channel_id=1, source_target_pairs={{0,8},{2,10},{4,12},{6,14},{8,0},{10,2},{12,4},{14,6},{16,24},{18,... | collective-permute-start | bytes 786440 | tf_op jit(solution)/shard_map/ppermute | solution.py:637
  178.3 16.9 %collective-permute-start.32 = (bf16[4,64,512]{2,1,0:T(8,128)(2,1)S(1)}, bf16[4,64,512]{2,1,0:T(8,128)(2,1)S(1)}, u32[]{:S(2)}, u32[]{:S(2)}) collective-permute-start(bf16[4,64,512]{2,1,0:T(8,128)(2,1)S(1)} %fusion.17), channel_id=1, source_target_pairs={{0,16},{2,18},{4,20},{6,22},{8,24},{10,26},{12,28},{14,30},{16,0},... | collective-permute-start | bytes 786440 | tf_op jit(solution)/shard_map/ppermute | solution.py:637
  184.0 19.9 %collective-permute-start.34 = (bf16[2,64,512]{2,1,0:T(8,128)(2,1)S(1)}, bf16[2,64,512]{2,1,0:T(8,128)(2,1)S(1)}, u32[]{:S(2)}, u32[]{:S(2)}) collective-permute-start(bf16[2,64,512]{2,1,0:T(8,128)(2,1)S(1)} %fusion.16), channel_id=1, source_target_pairs={{0,16},{2,18},{4,20},{6,22},{8,24},{10,26},{12,28},{14,30},{16,0},... | collective-permute-start | bytes 393224 | tf_op jit(solution)/shard_map/ppermute | solution.py:637
  196.9 6.9 %collective-permute-start.35 = (bf16[256,512]{1,0:T(8,128)(2,1)S(1)}, bf16[256,512]{1,0:T(8,128)(2,1)S(1)}, u32[]{:S(2)}, u32[]{:S(2)}) collective-permute-start(bf16[256,512]{1,0:T(8,128)(2,1)S(1)} %dynamic-slice_convert_fusion), channel_id=1, source_target_pairs={{0,1},{1,0},{2,3},{3,2},{4,5},{5,4},{6,7},{7,6},{8,9},{9,8},{10,11... | collective-permute-start | bytes 786440 | tf_op jit(solution)/shard_map/ppermute | solution.py:637
  198.5 10.3 %collective-permute-start.43 = (bf16[4,64,512]{2,1,0:T(8,128)(2,1)S(1)}, bf16[4,64,512]{2,1,0:T(8,128)(2,1)S(1)}, u32[]{:S(2)}, u32[]{:S(2)}) collective-permute-start(bf16[4,64,512]{2,1,0:T(8,128)(2,1)S(1)} %reduce-precision_convert_fusion.1), channel_id=1, source_target_pairs={{0,12},{2,14},{4,8},{6,10},{8,4},{10,6},{12,0},{14,2},{16,28},{18,... | collective-permute-start | bytes 786440 | tf_op jit(solution)/shard_map/ppermute | solution.py:637
  198.5 13.2 %collective-permute-start.42 = (bf16[4,64,512]{2,1,0:T(8,128)(2,1)S(1)}, bf16[4,64,512]{2,1,0:T(8,128)(2,1)S(1)}, u32[]{:S(2)}, u32[]{:S(2)}) collective-permute-start(bf16[4,64,512]{2,1,0:T(8,128)(2,1)S(1)} %reduce-precision_convert_fusion.1), channel_id=1, source_target_pairs={{0,4},{2,6},{4,0},{6,2},{8,12},{10,14},{12,8},{14,10},{16,20},{18,... | collective-permute-start | bytes 786440 | tf_op jit(solution)/shard_map/ppermute | solution.py:637
  201.0 11.2 %collective-permute-start.41 = (bf16[4,64,512]{2,1,0:T(8,128)(2,1)S(1)}, bf16[4,64,512]{2,1,0:T(8,128)(2,1)S(1)}, u32[]{:S(2)}, u32[]{:S(2)}) collective-permute-start(bf16[4,64,512]{2,1,0:T(8,128)(2,1)S(1)} %reduce-precision_convert_fusion.1), channel_id=1, source_target_pairs={{0,8},{2,10},{4,12},{6,14},{8,0},{10,2},{12,4},{14,6},{16,24},{18,... | collective-permute-start | bytes 786440 | tf_op jit(solution)/shard_map/ppermute | solution.py:637
  204.0 12.9 %collective-permute-start.39 = (bf16[2,64,512]{2,1,0:T(8,128)(2,1)S(1)}, bf16[2,64,512]{2,1,0:T(8,128)(2,1)S(1)}, u32[]{:S(2)}, u32[]{:S(2)}) collective-permute-start(bf16[2,64,512]{2,1,0:T(8,128)(2,1)S(1)} %reduce-precision_convert_fusion.2.refs_4_), channel_id=1, source_target_pairs={{0,12},{2,14},{4,8},{6,10},{8,4},{10,6},{12,0},{14,2},{16,28},{18,... | collective-permute-start | bytes 393224 | tf_op jit(solution)/shard_map/ppermute | solution.py:637
  204.4 12.5 %collective-permute-start.38 = (bf16[2,64,512]{2,1,0:T(8,128)(2,1)S(1)}, bf16[2,64,512]{2,1,0:T(8,128)(2,1)S(1)}, u32[]{:S(2)}, u32[]{:S(2)}) collective-permute-start(bf16[2,64,512]{2,1,0:T(8,128)(2,1)S(1)} %reduce-precision_convert_fusion.2.refs_4_), channel_id=1, source_target_pairs={{0,4},{2,6},{4,0},{6,2},{8,12},{10,14},{12,8},{14,10},{16,20},{18,... | collective-permute-start | bytes 393224 | tf_op jit(solution)/shard_map/ppermute | solution.py:637
  208.7 8.2 %collective-permute-start.37 = (bf16[2,64,512]{2,1,0:T(8,128)(2,1)S(1)}, bf16[2,64,512]{2,1,0:T(8,128)(2,1)S(1)}, u32[]{:S(2)}, u32[]{:S(2)}) collective-permute-start(bf16[2,64,512]{2,1,0:T(8,128)(2,1)S(1)} %reduce-precision_convert_fusion.2.refs_4_), channel_id=1, source_target_pairs={{0,8},{2,10},{4,12},{6,14},{8,0},{10,2},{12,4},{14,6},{16,24},{18,... | collective-permute-start | bytes 393224 | tf_op jit(solution)/shard_map/ppermute | solution.py:637
  (36 other events, 225.7 us)

commit v5 on v4

--- a/solution.py
+++ b/solution.py
@@ -839,7 +839,7 @@
         after=[second],
     )
     first_quarters = gathered(first, members, early=[second], late=[mask_ends])
-    every_prompt = jnp.broadcast_to(behind(prompt, second)[None, :, 0], (tm_count, MICRO, *prompt.shape[2:]))
+    every_prompt = jnp.broadcast_to(behind(prompt, mask_ends)[None, :, 0], (tm_count, MICRO, *prompt.shape[2:]))
     every_prompt = lax.all_to_all(every_prompt, "tm", 0, 0)
     full_queries = behind(queries, second).astype(bf16)
     for bit in bits_of("fsdp"):

time: 223 us -> 228 us (1.022)
  starting transfers between devices: 47 us -> 49.7 us
  transfers between devices with their start and end apart: 46 -> 46, of which waited for: 16 -> 16; matrix products, arithmetic and copies ran while one was open for 7% -> 6% of each run, Pallas kernels for 27% -> 27%
where the time goes in v5:
time: 228 us; the launch traced here: 227 us
  Pallas kernels  112 us (49%)
  starting transfers between devices  49.7 us (22%)
  waiting for transfers between devices  41.4 us (18%)
  other arithmetic  12.2 us (5%)
  local copies, waits for them, and re-layouts  10.4 us (5%)
    pallas_call x12, Pallas kernels, call(): pl.pallas_call(body, grid=grid, in_specs=[spec for _, spec in ins] + [ANY...  112 us
    ppermute x43, waiting for transfers between devices, swapped(): return lax.ppermute(array, axis, [(i, i ^ bit) for i in range(count)])  41.4 us
    ppermute x43, starting transfers between devices, swapped(): return lax.ppermute(array, axis, [(i, i ^ bit) for i in range(count)])  39.6 us
    unnamed x46, local copies, waits for them, and re-layouts  7.86 us
    all_to_all x1, starting transfers between devices, per_device(): every_prompt = lax.all_to_all(every_prompt, 'tm', 0, 0)  7.02 us
    add x4, other arithmetic, __init__(): k + r.astype(f32)  5.83 us
  transfers between devices with their start and end apart: 46, of which 16 were waited for; matrix products, arithmetic and copies ran while one was open for 6% of the time, Pallas kernels for 27%

profile of v5, /device:TPU:0, one launch (start us, length us, event | category | flops | bytes accessed | tf_op | source)
XLA Modules:
  0.0 227.3 jit_solution(9398169787170807776)
XLA Ops:
  0.8 1.7 pack_first.1.refs_4_
  2.5 3.0 %collective-permute-start.2 = (bf16[1,128,1024]{2,1,0:T(8,128)(2,1)S(1)}, bf16[1,128,1024]{2,1,0:T(8,128)(2,1)S(1)}, u32[]{:S(2)}, u32[]{:S(2)}) collective-permute-start(bf16[1,128,1024]{2,1,0:T(8,128)(2,1)S(1)} %bitcast.57), channel_id=1, source_target_pairs={{0,1},{1,0},{2,3},{3,2},{4,5},{5,4},{6,7},{7,6},{8,9},{9,8},{10,11... | collective-permute-start | bytes 786440 | tf_op jit(solution)/shard_map/ppermute | solution.py:637
  8.0 2.3 pack_rest.1
  10.4 2.0 collective-permute-start.7
  12.4 5.1 %masks.1 = (bf16[2,1536,384]{2,1,0:T(8,128)(2,1)}, bf16[2,1536,128]{2,1,0:T(8,128)(2,1)}, bf16[2,64,384]{2,1,0:T(8,128)(2,1)}, bf16[2,64,128]{2,1,0:T(8,128)(2,1)}) custom-call(s32[5]{0:T(128)S(1)} %stack.23.refs_0_, s32[2,30]{1,0:T(2,128)S(1)} %bitcast.60, bf16[192,1024]{1,0:T(8,128)(2,1)S(1)} %get-tuple-element.98.refs_2_), custom_call_target="tpu_custom_call" | custom-call | flops 5000000000 | bytes 4096 | tf_op jit(solution)/shard_map/masks/pallas_call | solution.py:68
  18.4 7.0 %all-to-all-start = ((bf16[16,2,16,512]{3,2,1,0:T(8,128)(2,1)}), bf16[16,2,16,512]{3,2,1,0:T(8,128)(2,1)}, u32[]{:S(2)}, u32[]{:S(2)}) async-start(bf16[16,2,16,512]{3,2,1,0:T(8,128)(2,1)} %broadcast_in_dim.35), calls=%async_computation | async-start | bytes 1048576 | tf_op jit(solution)/shard_map/all_to_all | solution.py:843
  25.6 1.9 collective-permute-start.3
  28.4 1.8 collective-permute-start
  30.2 9.0 %collective-permute-done.3.refs_11_ = bf16[1,128,1024]{2,1,0:T(8,128)(2,1)S(1)} collective-permute-done((bf16[1,128,1024]{2,1,0:T(8,128)(2,1)S(1)}, bf16[1,128,1024]{2,1,0:T(8,128)(2,1)S(1)}, u32[]{:S(2)}, u32[]{:S(2)}) %collective-permute-start.3) | collective-permute-done | bytes 262176 | tf_op jit(solution)/shard_map/ppermute | solution.py:637
  40.2 4.5 %collective-permute-start.12 = (bf16[1,256,1024]{2,1,0:T(8,128)(2,1)S(1)}, bf16[1,256,1024]{2,1,0:T(8,128)(2,1)S(1)}, u32[]{:S(2)}, u32[]{:S(2)}) collective-permute-start(bf16[1,256,1024]{2,1,0:T(8,128)(2,1)S(1)} %collective-permute-done.11.refs_12_), channel_id=1, source_target_pairs={{0,8},{2,10},{4,12},{6,14},{8,0},{10,2},{12,4},{14,6},{16,24},{18,... | collective-permute-start | bytes 1572872 | tf_op jit(solution)/shard_map/ppermute | solution.py:637
  45.5 10.7 %film.1 = (bf16[2,1632,512]{2,1,0:T(8,128)(2,1)S(1)}, bf16[512,512]{1,0:T(8,128)(2,1)}, bf16[128,512]{1,0:T(8,128)(2,1)}) custom-call(s32[5]{0:T(128)S(1)} %stack.23.refs_0_, bf16[2,1536,512]{2,1,0:T(8,128)(2,1)} %bitcast.62, bf16[2,1536,512]{2,1,0:T(8,128)(2,1)} %bitcast.66, bf16[4,2,32,512]{3,2,1,0:T(8,128)(2,1)} %copy-done.16, ...), custom_call_target="tpu_custom_call" | custom-call | flops 1000000000 | bytes 4096 | tf_op jit(solution)/shard_map/film/pallas_call | solution.py:68
  56.2 1.7 copy-done.4
  61.3 5.8 %attention.1 = (f32[2,8,1024]{2,1,0:T(8,128)}, bf16[2,256,512]{2,1,0:T(8,128)(2,1)}, f32[2,256,256]{2,1,0:T(8,128)}, bf16[2,256,512]{2,1,0:T(8,128)(2,1)}, bf16[...) custom-call(s32[5]{0:T(128)S(1)} %stack.23.refs_0_, ...), custom_call_target="tpu_custom_call" | custom-call | flops 5000000000 | bytes 4096 | tf_op jit(solution)/shard_map/attention/pallas_call | solution.py:68
  67.1 1.9 copy-done.5
  69.1 32.8 %conv.1 = (bf16[2,1600,1024]{2,1,0:T(8,128)(2,1)S(1)}, bf16[2,1600,1024]{2,1,0:T(8,128)(2,1)}, bf16[1536,1024]{1,0:T(8,128)(2,1)}, f32[8,1024]{1,0:T(8,128)}, f3...) custom-call(s32[5]{0:T(128)S(1)} %stack.23.refs_0_, ...), custom_call_target="tpu_custom_call" | custom-call | flops 32000000000 | bytes 4096 | tf_op jit(solution)/shard_map/conv/pallas_call | solution.py:68
  102.9 13.2 %conv_grad.1 = (f32[3,512,512]{2,1,0:T(8,128)S(1)}, bf16[3,512,512]{2,1,0:T(8,128)(2,1)}) custom-call(s32[5]{0:T(128)} %copy-done.2, bf16[2,1632,512]{2,1,0:T(8,128)(2,1)S(1)} %copy-done.5, bf16[2,1536,384]{2,1,0:T(8,128)(2,1)} %get-tuple-element.106.refs_2_, bf16[2,1600,1024]{2,1,0:T(8,128)(2,1)S(1)} %get-tuple-element.120.refs_3_), custom_call_target="tpu_custom_call" | custom-call | flops 13500000256 | bytes 4096 | tf_op jit(solution)/shard_map/conv_grad/pallas_call | solution.py:68
  116.8 2.9 %collective-permute-done.17 = f32[8,1024]{1,0:T(8,128)S(1)} collective-permute-done((f32[8,1024]{1,0:T(8,128)S(1)}, f32[8,1024]{1,0:T(8,128)S(1)}, u32[]{:S(2)}, u32[]{:S(2)}) %collective-permute-start.17) | collective-permute-done | bytes 32800 | tf_op jit(solution)/shard_map/ppermute | solution.py:637
  129.0 25.8 %hidden_grad.1 = (f32[2,1536,512]{2,1,0:T(8,128)}, f32[2,512,512]{2,1,0:T(8,128)S(1)}, bf16[2,512,512]{2,1,0:T(8,128)(2,1)S(1)}) custom-call(s32[5]{0:T(128)S(1)} %copy-done.3, bf16[2,1600,1024]{2,1,0:T(8,128)(2,1)} %get-tuple-element.117.refs_1_, bf16[2,1536,384]{2,1,0:T(8,128)(2,1)} %get-tuple-element.106.refs_2_, ...), custom_call_target="tpu_custom_call" | custom-call | flops 27000000512 | bytes 4096 | tf_op jit(solution)/shard_map/hidden_grad/pallas_call | solution.py:68
  155.6 2.4 %collective-permute-start.22 = (f32[8,1024]{1,0:T(8,128)S(1)}, f32[8,1024]{1,0:T(8,128)S(1)}, u32[]{:S(2)}, u32[]{:S(2)}) collective-permute-start(f32[8,1024]{1,0:T(8,128)S(1)} %add.160), channel_id=1, source_target_pairs={{0,16},{2,18},{4,20},{6,22},{8,24},{10,26},{12,28},{14,30},{16,0},... | collective-permute-start | bytes 98312 | tf_op jit(solution)/shard_map/ppermute | solution.py:637
  165.8 3.3 %collective-permute-done.26 = bf16[2,1,1,128,512]{4,3,0,2,1:T(8,128)(2,1)S(1)} collective-permute-done((bf16[2,1,1,128,512]{4,3,0,2,1:T(8,128)(2,1)S(1)}, bf16[2,1,1,128,512]{4,3,0,2,1:T(8,128)(2,1)S(1)}, u32[]{:S(2)}, u32[]{:S(2)}) %collective-permute-start.26) | collective-permute-done | bytes 262176 | tf_op jit(solution)/shard_map/ppermute | solution.py:637
  169.8 2.0 collective-permute-start.31
  171.8 2.4 %collective-permute-done.28 = bf16[1,2,1,128,512]{4,3,0,2,1:T(8,128)(2,1)S(1)} collective-permute-done((bf16[1,2,1,128,512]{4,3,0,2,1:T(8,128)(2,1)S(1)}, bf16[1,2,1,128,512]{4,3,0,2,1:T(8,128)(2,1)S(1)}, u32[]{:S(2)}, u32[]{:S(2)}) %collective-permute-start.28) | collective-permute-done | bytes 262176 | tf_op jit(solution)/shard_map/ppermute | solution.py:637
  177.1 2.3 collective-permute-done.29
  181.2 2.0 collective-permute-start.30
  184.1 3.3 %collective-permute-done.30 = bf16[2,64,512]{2,1,0:T(8,128)(2,1)S(1)} collective-permute-done((bf16[2,64,512]{2,1,0:T(8,128)(2,1)S(1)}, bf16[2,64,512]{2,1,0:T(8,128)(2,1)S(1)}, u32[]{:S(2)}, u32[]{:S(2)}) %collective-permute-start.30) | collective-permute-done | bytes 131104 | tf_op jit(solution)/shard_map/ppermute | solution.py:637
  189.0 6.8 %attention_grad.1 = (f32[2,16,512]{2,1,0:T(8,128)}, f32[512,512]{1,0:T(8,128)}, f32[72,512]{1,0:T(8,128)}) custom-call(s32[5]{0:T(128)S(1)} %copy-done.3, f32[8,1024]{1,0:T(8,128)} %add.177.refs_1_, bf16[2,256,512]{2,1,0:T(8,128)(2,1)} %get-tuple-element.146.refs_2_, f32[2,256,256]{2,1,0:T(8,128)} %get-tuple-element.147.refs_3_, ...), custom_call_target="tpu_custom_call" | custom-call | flops 7000000000 | bytes 4096 | tf_op jit(solution)/shard_map/attention_grad/pallas_call | solution.py:68
  195.9 3.8 %collective-permute-done.32 = bf16[4,64,512]{2,1,0:T(8,128)(2,1)S(1)} collective-permute-done((bf16[4,64,512]{2,1,0:T(8,128)(2,1)S(1)}, bf16[4,64,512]{2,1,0:T(8,128)(2,1)S(1)}, u32[]{:S(2)}, u32[]{:S(2)}) %collective-permute-start.32) | collective-permute-done | bytes 262176 | tf_op jit(solution)/shard_map/ppermute | solution.py:637
  201.0 1.9 collective-permute-start.35
  210.2 3.1 %collective-permute-done.43 = bf16[4,64,512]{2,1,0:T(8,128)(2,1)S(1)} collective-permute-done((bf16[4,64,512]{2,1,0:T(8,128)(2,1)S(1)}, bf16[4,64,512]{2,1,0:T(8,128)(2,1)S(1)}, u32[]{:S(2)}, u32[]{:S(2)}) %collective-permute-start.43) | collective-permute-done | bytes 262176 | tf_op jit(solution)/shard_map/ppermute | solution.py:637
  213.3 3.2 %collective-permute-done.42 = bf16[4,64,512]{2,1,0:T(8,128)(2,1)S(1)} collective-permute-done((bf16[4,64,512]{2,1,0:T(8,128)(2,1)S(1)}, bf16[4,64,512]{2,1,0:T(8,128)(2,1)S(1)}, u32[]{:S(2)}, u32[]{:S(2)}) %collective-permute-start.42) | collective-permute-done | bytes 262176 | tf_op jit(solution)/shard_map/ppermute | solution.py:637
  217.2 3.4 %small_grads.1 = (f32[16,512]{1,0:T(8,128)}, f32[256,512]{1,0:T(8,128)}, f32[256,512]{1,0:T(8,128)}, f32[256,1024]{1,0:T(8,128)}) custom-call(s32[5]{0:T(128)S(1)} %copy-done.3, f32[2,72,512]{2,1,0:T(8,128)} %pad_maximum_fusion.3.refs_1_, bf16[32,512]{1,0:T(8,128)(2,1)} %copy-done.1, bf16[512,512]{1,0:T(8,128)(2,1)} %get-tuple-element.161.refs_3_, ...), custom_call_target="tpu_custom_call" | custom-call | flops 3300000000 | bytes 4096 | tf_op jit(solution)/shard_map/small_grads/pallas_call | solution.py:68
  223.8 3.5 %join.1 = (f32[256,1024]{1,0:T(8,128)}, f32[256,1024]{1,0:T(8,128)}, f32[3,256,1024]{2,1,0:T(8,128)}, f32[256,1024]{1,0:T(8,128)}) custom-call(s32[5]{0:T(128)S(1)} %copy-done.3, bf16[2,256,512]{2,1,0:T(8,128)(2,1)S(1)} %pad_maximum_fusion.2.refs_1_, bf16[2,256,512]{2,1,0:T(8,128)(2,1)S(1)} %collective-permute-done.40.refs_2_, ...), custom_call_target="tpu_custom_call" | custom-call | flops 4000000000 | bytes 4096 | tf_op jit(solution)/shard_map/join/pallas_call | solution.py:68
  (168 shorter events, 49.3 us)
Async XLA Ops:
  2.5 23.1 %collective-permute-start.2 = (bf16[1,128,1024]{2,1,0:T(8,128)(2,1)S(1)}, bf16[1,128,1024]{2,1,0:T(8,128)(2,1)S(1)}, u32[]{:S(2)}, u32[]{:S(2)}) collective-permute-start(bf16[1,128,1024]{2,1,0:T(8,128)(2,1)S(1)} %bitcast.57), channel_id=1, source_target_pairs={{0,1},{1,0},{2,3},{3,2},{4,5},{5,4},{6,7},{7,6},{8,9},{9,8},{10,11... | collective-permute-start | bytes 786440 | tf_op jit(solution)/shard_map/ppermute | solution.py:637
  6.7 33.6 %collective-permute-start.1 = (bf16[4,2,32,512]{3,2,1,0:T(8,128)(2,1)S(1)}, bf16[4,2,32,512]{3,2,1,0:T(8,128)(2,1)S(1)}, u32[]{:S(2)}, u32[]{:S(2)}) collective-permute-start(bf16[4,2,32,512]{3,2,1,0:T(8,128)(2,1)S(1)} %get-tuple-element.97), channel_id=1, source_target_pairs={{2,0},{4,2},{6,4},{8,6},{10,8},{12,10},{14,12},{16,14},{18,16},{20... | collective-permute-start | bytes 786440 | tf_op jit(solution)/shard_map/ppermute | solution.py:820
  10.3 28.9 %collective-permute-start.6 = (bf16[16,512]{1,0:T(8,128)(2,1)S(1)}, bf16[16,512]{1,0:T(8,128)(2,1)S(1)}, u32[]{:S(2)}, u32[]{:S(2)}) collective-permute-start(bf16[16,512]{1,0:T(8,128)(2,1)S(1)} %convert_element_type.138), channel_id=1, source_target_pairs={{0,1},{1,0},{2,3},{3,2},{4,5},{5,4},{6,7},{7,6},{8,9},{9,8},{10,11... | collective-permute-start | bytes 49160 | tf_op jit(solution)/shard_map/ppermute | solution.py:637
  10.4 18.1 %collective-permute-start.7 = (bf16[1,192,1024]{2,1,0:T(8,128)(2,1)S(1)}, bf16[1,192,1024]{2,1,0:T(8,128)(2,1)S(1)}, u32[]{:S(2)}, u32[]{:S(2)}) collective-permute-start(bf16[1,192,1024]{2,1,0:T(8,128)(2,1)S(1)} %bitcast.59), channel_id=1, source_target_pairs={{0,1},{1,0},{2,3},{3,2},{4,5},{5,4},{6,7},{7,6},{8,9},{9,8},{10,11... | collective-permute-start | bytes 1179656 | tf_op jit(solution)/shard_map/ppermute | solution.py:637
  12.4 27.6 %collective-permute-start.11 = (bf16[1,256,1024]{2,1,0:T(8,128)(2,1)S(1)}, bf16[1,256,1024]{2,1,0:T(8,128)(2,1)S(1)}, u32[]{:S(2)}, u32[]{:S(2)}) collective-permute-start(bf16[1,256,1024]{2,1,0:T(8,128)(2,1)S(1)} %bitcast.58), channel_id=1, source_target_pairs={{0,1},{1,0},{2,3},{3,2},{4,5},{5,4},{6,7},{7,6},{8,9},{9,8},{10,11... | collective-permute-start | bytes 1572872 | tf_op jit(solution)/shard_map/ppermute | solution.py:637
  18.4 40.7 %all-to-all-start = ((bf16[16,2,16,512]{3,2,1,0:T(8,128)(2,1)}), bf16[16,2,16,512]{3,2,1,0:T(8,128)(2,1)}, u32[]{:S(2)}, u32[]{:S(2)}) async-start(bf16[16,2,16,512]{3,2,1,0:T(8,128)(2,1)} %broadcast_in_dim.35), calls=%async_computation | async-start | bytes 1048576 | tf_op jit(solution)/shard_map/all_to_all | solution.py:843
  25.6 13.6 %collective-permute-start.3 = (bf16[1,128,1024]{2,1,0:T(8,128)(2,1)S(1)}, bf16[1,128,1024]{2,1,0:T(8,128)(2,1)S(1)}, u32[]{:S(2)}, u32[]{:S(2)}) collective-permute-start(bf16[1,128,1024]{2,1,0:T(8,128)(2,1)S(1)} %collective-permute-done.2.refs_10_), channel_id=1, source_target_pairs={{0,4},{2,6},{4,0},{6,2},{8,12},{10,14},{12,8},{14,10},{16,20},{18,... | collective-permute-start | bytes 786440 | tf_op jit(solution)/shard_map/ppermute | solution.py:637
  28.4 16.3 %collective-permute-start = (bf16[4,2,32,512]{3,2,1,0:T(8,128)(2,1)S(1)}, bf16[4,2,32,512]{3,2,1,0:T(8,128)(2,1)S(1)}, u32[]{:S(2)}, u32[]{:S(2)}) collective-permute-start(bf16[4,2,32,512]{3,2,1,0:T(8,128)(2,1)S(1)} %get-tuple-element.96.refs_10_), channel_id=1, source_target_pairs={{0,2},{2,4},{4,6},{6,8},{8,10},{10,12},{12,14},{14,16},{16,18},{18... | collective-permute-start | bytes 786440 | tf_op jit(solution)/shard_map/ppermute | solution.py:819
  39.2 18.7 %collective-permute-start.8 = (bf16[1,192,1024]{2,1,0:T(8,128)(2,1)S(1)}, bf16[1,192,1024]{2,1,0:T(8,128)(2,1)S(1)}, u32[]{:S(2)}, u32[]{:S(2)}) collective-permute-start(bf16[1,192,1024]{2,1,0:T(8,128)(2,1)S(1)} %collective-permute-done.7.refs_8_), channel_id=1, source_target_pairs={{0,4},{2,6},{4,0},{6,2},{8,12},{10,14},{12,8},{14,10},{16,20},{18,... | collective-permute-start | bytes 1179656 | tf_op jit(solution)/shard_map/ppermute | solution.py:637
  40.2 18.2 %collective-permute-start.12 = (bf16[1,256,1024]{2,1,0:T(8,128)(2,1)S(1)}, bf16[1,256,1024]{2,1,0:T(8,128)(2,1)S(1)}, u32[]{:S(2)}, u32[]{:S(2)}) collective-permute-start(bf16[1,256,1024]{2,1,0:T(8,128)(2,1)S(1)} %collective-permute-done.11.refs_12_), channel_id=1, source_target_pairs={{0,8},{2,10},{4,12},{6,14},{8,0},{10,2},{12,4},{14,6},{16,24},{18,... | collective-permute-start | bytes 1572872 | tf_op jit(solution)/shard_map/ppermute | solution.py:637
  44.8 13.7 %collective-permute-start.9 = (bf16[1,192,1024]{2,1,0:T(8,128)(2,1)S(1)}, bf16[1,192,1024]{2,1,0:T(8,128)(2,1)S(1)}, u32[]{:S(2)}, u32[]{:S(2)}) collective-permute-start(bf16[1,192,1024]{2,1,0:T(8,128)(2,1)S(1)} %collective-permute-done.7.refs_8_), channel_id=1, source_target_pairs={{0,2},{2,0},{4,6},{6,4},{8,10},{10,8},{12,14},{14,12},{16,18},{18,... | collective-permute-start | bytes 1179656 | tf_op jit(solution)/shard_map/ppermute | solution.py:637
  57.9 9.2 %collective-permute-start.13 = (bf16[1,256,1024]{2,1,0:T(8,128)(2,1)S(1)}, bf16[1,256,1024]{2,1,0:T(8,128)(2,1)S(1)}, u32[]{:S(2)}, u32[]{:S(2)}) collective-permute-start(bf16[1,256,1024]{2,1,0:T(8,128)(2,1)S(1)} %collective-permute-done.11.refs_12_), channel_id=1, source_target_pairs={{0,2},{2,0},{4,6},{6,4},{8,10},{10,8},{12,14},{14,12},{16,18},{18,... | collective-permute-start | bytes 1572872 | tf_op jit(solution)/shard_map/ppermute | solution.py:637
  58.4 8.7 %collective-permute-start.14 = (bf16[1,256,1024]{2,1,0:T(8,128)(2,1)S(1)}, bf16[1,256,1024]{2,1,0:T(8,128)(2,1)S(1)}, u32[]{:S(2)}, u32[]{:S(2)}) collective-permute-start(bf16[1,256,1024]{2,1,0:T(8,128)(2,1)S(1)} %collective-permute-done.12.refs_13_), channel_id=1, source_target_pairs={{0,2},{2,0},{4,6},{6,4},{8,10},{10,8},{12,14},{14,12},{16,18},{18,... | collective-permute-start | bytes 1572872 | tf_op jit(solution)/shard_map/ppermute | solution.py:637
  119.6 9.2 %collective-permute-start.18 = (f32[8,1024]{1,0:T(8,128)S(1)}, f32[8,1024]{1,0:T(8,128)S(1)}, u32[]{:S(2)}, u32[]{:S(2)}) collective-permute-start(f32[8,1024]{1,0:T(8,128)S(1)} %add.158), channel_id=1, source_target_pairs={{0,4},{2,6},{4,0},{6,2},{8,12},{10,14},{12,8},{14,10},{16,20},{18,... | collective-permute-start | bytes 98312 | tf_op jit(solution)/shard_map/ppermute | solution.py:637
  124.6 30.2 %collective-permute-start.20 = (bf16[2,1,2,128,512]{4,3,0,2,1:T(8,128)(2,1)S(1)}, bf16[2,1,2,128,512]{4,3,0,2,1:T(8,128)(2,1)S(1)}, u32[]{:S(2)}, u32[]{:S(2)}) collective-permute-start(bf16[2,1,2,128,512]{4,3,0,2,1:T(8,128)(2,1)S(1)} %copy.56), channel_id=1, source_target_pairs={{0,1},{1,0},{2,3},{3,2},{4,5},{5,4},{6,7},{7,6},{8,9},{9,8},{10,11... | collective-permute-start | bytes 1572872 | tf_op jit(solution)/shard_map/ppermute | solution.py:637
  127.8 27.0 %collective-permute-start.21 = (bf16[2,2,1,128,512]{4,3,0,2,1:T(8,128)(2,1)S(1)}, bf16[2,2,1,128,512]{4,3,0,2,1:T(8,128)(2,1)}, u32[]{:S(2)}, u32[]{:S(2)}) collective-permute-start(bf16[2,2,1,128,512]{4,3,0,2,1:T(8,128)(2,1)S(1)} %copy.55), channel_id=1, source_target_pairs={{0,4},{2,6},{4,0},{6,2},{8,12},{10,14},{12,8},{14,10},{16,20},{18,... | collective-permute-start | bytes 1572872 | tf_op jit(solution)/shard_map/ppermute | solution.py:637
  128.9 25.9 %collective-permute-start.19 = (f32[8,1024]{1,0:T(8,128)S(1)}, f32[8,1024]{1,0:T(8,128)S(1)}, u32[]{:S(2)}, u32[]{:S(2)}) collective-permute-start(f32[8,1024]{1,0:T(8,128)S(1)} %add.159.refs_13_), channel_id=1, source_target_pairs={{0,8},{2,10},{4,12},{6,14},{8,0},{10,2},{12,4},{14,6},{16,24},{18,... | collective-permute-start | bytes 98312 | tf_op jit(solution)/shard_map/ppermute | solution.py:637
  155.6 14.1 %collective-permute-start.22 = (f32[8,1024]{1,0:T(8,128)S(1)}, f32[8,1024]{1,0:T(8,128)S(1)}, u32[]{:S(2)}, u32[]{:S(2)}) collective-permute-start(f32[8,1024]{1,0:T(8,128)S(1)} %add.160), channel_id=1, source_target_pairs={{0,16},{2,18},{4,20},{6,22},{8,24},{10,26},{12,28},{14,30},{16,0},... | collective-permute-start | bytes 98312 | tf_op jit(solution)/shard_map/ppermute | solution.py:637
  159.9 9.2 %collective-permute-start.26 = (bf16[2,1,1,128,512]{4,3,0,2,1:T(8,128)(2,1)S(1)}, bf16[2,1,1,128,512]{4,3,0,2,1:T(8,128)(2,1)S(1)}, u32[]{:S(2)}, u32[]{:S(2)}) collective-permute-start(bf16[2,1,1,128,512]{4,3,0,2,1:T(8,128)(2,1)S(1)} %get-tuple-element.222), channel_id=1, source_target_pairs={{0,1},{1,0},{2,3},{3,2},{4,5},{5,4},{6,7},{7,6},{8,9},{9,8},{10,11... | collective-permute-start | bytes 786440 | tf_op jit(solution)/shard_map/ppermute | solution.py:637
  160.5 9.2 %collective-permute-start.25 = (bf16[2,1,1,128,512]{4,3,0,2,1:T(8,128)(2,1)S(1)}, bf16[2,1,1,128,512]{4,3,0,2,1:T(8,128)(2,1)S(1)}, u32[]{:S(2)}, u32[]{:S(2)}) collective-permute-start(bf16[2,1,1,128,512]{4,3,0,2,1:T(8,128)(2,1)S(1)} %get-tuple-element.223), channel_id=1, source_target_pairs={{0,4},{2,6},{4,0},{6,2},{8,12},{10,14},{12,8},{14,10},{16,20},{18,... | collective-permute-start | bytes 786440 | tf_op jit(solution)/shard_map/ppermute | solution.py:637
  163.3 10.9 %collective-permute-start.28 = (bf16[1,2,1,128,512]{4,3,0,2,1:T(8,128)(2,1)S(1)}, bf16[1,2,1,128,512]{4,3,0,2,1:T(8,128)(2,1)S(1)}, u32[]{:S(2)}, u32[]{:S(2)}) collective-permute-start(bf16[1,2,1,128,512]{4,3,0,2,1:T(8,128)(2,1)S(1)} %dynamic-slice_convert_fusion.1), channel_id=1, source_target_pairs={{0,4},{2,6},{4,0},{6,2},{8,12},{10,14},{12,8},{14,10},{16,20},{18,... | collective-permute-start | bytes 786440 | tf_op jit(solution)/shard_map/ppermute | solution.py:637
  164.3 11.7 %collective-permute-start.24 = (bf16[1,1,2,128,512]{4,3,0,2,1:T(8,128)(2,1)S(1)}, bf16[1,1,2,128,512]{4,3,0,2,1:T(8,128)(2,1)S(1)}, u32[]{:S(2)}, u32[]{:S(2)}) collective-permute-start(bf16[1,1,2,128,512]{4,3,0,2,1:T(8,128)(2,1)S(1)} %dynamic-slice_convert_fusion.2), channel_id=1, source_target_pairs={{0,1},{1,0},{2,3},{3,2},{4,5},{5,4},{6,7},{7,6},{8,9},{9,8},{10,11... | collective-permute-start | bytes 786440 | tf_op jit(solution)/shard_map/ppermute | solution.py:637
  169.8 13.4 %collective-permute-start.31 = (bf16[4,64,512]{2,1,0:T(8,128)(2,1)S(1)}, bf16[4,64,512]{2,1,0:T(8,128)(2,1)S(1)}, u32[]{:S(2)}, u32[]{:S(2)}) collective-permute-start(bf16[4,64,512]{2,1,0:T(8,128)(2,1)S(1)} %fusion.6), channel_id=1, source_target_pairs={{0,8},{2,10},{4,12},{6,14},{8,0},{10,2},{12,4},{14,6},{16,24},{18,... | collective-permute-start | bytes 786440 | tf_op jit(solution)/shard_map/ppermute | solution.py:637
  183.3 16.4 %collective-permute-start.32 = (bf16[4,64,512]{2,1,0:T(8,128)(2,1)S(1)}, bf16[4,64,512]{2,1,0:T(8,128)(2,1)S(1)}, u32[]{:S(2)}, u32[]{:S(2)}) collective-permute-start(bf16[4,64,512]{2,1,0:T(8,128)(2,1)S(1)} %fusion.17), channel_id=1, source_target_pairs={{0,16},{2,18},{4,20},{6,22},{8,24},{10,26},{12,28},{14,30},{16,0},... | collective-permute-start | bytes 786440 | tf_op jit(solution)/shard_map/ppermute | solution.py:637
  187.4 21.2 %collective-permute-start.34 = (bf16[2,64,512]{2,1,0:T(8,128)(2,1)S(1)}, bf16[2,64,512]{2,1,0:T(8,128)(2,1)S(1)}, u32[]{:S(2)}, u32[]{:S(2)}) collective-permute-start(bf16[2,64,512]{2,1,0:T(8,128)(2,1)S(1)} %fusion.16), channel_id=1, source_target_pairs={{0,16},{2,18},{4,20},{6,22},{8,24},{10,26},{12,28},{14,30},{16,0},... | collective-permute-start | bytes 393224 | tf_op jit(solution)/shard_map/ppermute | solution.py:637
  201.0 7.5 %collective-permute-start.35 = (bf16[256,512]{1,0:T(8,128)(2,1)S(1)}, bf16[256,512]{1,0:T(8,128)(2,1)S(1)}, u32[]{:S(2)}, u32[]{:S(2)}) collective-permute-start(bf16[256,512]{1,0:T(8,128)(2,1)S(1)} %dynamic-slice_convert_fusion), channel_id=1, source_target_pairs={{0,1},{1,0},{2,3},{3,2},{4,5},{5,4},{6,7},{7,6},{8,9},{9,8},{10,11... | collective-permute-start | bytes 786440 | tf_op jit(solution)/shard_map/ppermute | solution.py:637
  203.0 10.3 %collective-permute-start.43 = (bf16[4,64,512]{2,1,0:T(8,128)(2,1)S(1)}, bf16[4,64,512]{2,1,0:T(8,128)(2,1)S(1)}, u32[]{:S(2)}, u32[]{:S(2)}) collective-permute-start(bf16[4,64,512]{2,1,0:T(8,128)(2,1)S(1)} %reduce-precision_convert_fusion.1), channel_id=1, source_target_pairs={{0,12},{2,14},{4,8},{6,10},{8,4},{10,6},{12,0},{14,2},{16,28},{18,... | collective-permute-start | bytes 786440 | tf_op jit(solution)/shard_map/ppermute | solution.py:637
  203.1 13.4 %collective-permute-start.42 = (bf16[4,64,512]{2,1,0:T(8,128)(2,1)S(1)}, bf16[4,64,512]{2,1,0:T(8,128)(2,1)S(1)}, u32[]{:S(2)}, u32[]{:S(2)}) collective-permute-start(bf16[4,64,512]{2,1,0:T(8,128)(2,1)S(1)} %reduce-precision_convert_fusion.1), channel_id=1, source_target_pairs={{0,4},{2,6},{4,0},{6,2},{8,12},{10,14},{12,8},{14,10},{16,20},{18,... | collective-permute-start | bytes 786440 | tf_op jit(solution)/shard_map/ppermute | solution.py:637
  205.7 11.2 %collective-permute-start.41 = (bf16[4,64,512]{2,1,0:T(8,128)(2,1)S(1)}, bf16[4,64,512]{2,1,0:T(8,128)(2,1)S(1)}, u32[]{:S(2)}, u32[]{:S(2)}) collective-permute-start(bf16[4,64,512]{2,1,0:T(8,128)(2,1)S(1)} %reduce-precision_convert_fusion.1), channel_id=1, source_target_pairs={{0,8},{2,10},{4,12},{6,14},{8,0},{10,2},{12,4},{14,6},{16,24},{18,... | collective-permute-start | bytes 786440 | tf_op jit(solution)/shard_map/ppermute | solution.py:637
  208.7 12.9 %collective-permute-start.39 = (bf16[2,64,512]{2,1,0:T(8,128)(2,1)S(1)}, bf16[2,64,512]{2,1,0:T(8,128)(2,1)S(1)}, u32[]{:S(2)}, u32[]{:S(2)}) collective-permute-start(bf16[2,64,512]{2,1,0:T(8,128)(2,1)S(1)} %reduce-precision_convert_fusion.2.refs_4_), channel_id=1, source_target_pairs={{0,12},{2,14},{4,8},{6,10},{8,4},{10,6},{12,0},{14,2},{16,28},{18,... | collective-permute-start | bytes 393224 | tf_op jit(solution)/shard_map/ppermute | solution.py:637
  209.2 12.5 %collective-permute-start.38 = (bf16[2,64,512]{2,1,0:T(8,128)(2,1)S(1)}, bf16[2,64,512]{2,1,0:T(8,128)(2,1)S(1)}, u32[]{:S(2)}, u32[]{:S(2)}) collective-permute-start(bf16[2,64,512]{2,1,0:T(8,128)(2,1)S(1)} %reduce-precision_convert_fusion.2.refs_4_), channel_id=1, source_target_pairs={{0,4},{2,6},{4,0},{6,2},{8,12},{10,14},{12,8},{14,10},{16,20},{18,... | collective-permute-start | bytes 393224 | tf_op jit(solution)/shard_map/ppermute | solution.py:637
  213.3 8.4 %collective-permute-start.37 = (bf16[2,64,512]{2,1,0:T(8,128)(2,1)S(1)}, bf16[2,64,512]{2,1,0:T(8,128)(2,1)S(1)}, u32[]{:S(2)}, u32[]{:S(2)}) collective-permute-start(bf16[2,64,512]{2,1,0:T(8,128)(2,1)S(1)} %reduce-precision_convert_fusion.2.refs_4_), channel_id=1, source_target_pairs={{0,8},{2,10},{4,12},{6,14},{8,0},{10,2},{12,4},{14,6},{16,24},{18,... | collective-permute-start | bytes 393224 | tf_op jit(solution)/shard_map/ppermute | solution.py:637
  (36 other events, 235.1 us)
